TPU v7x, 32 devices: a whole 2x2x4 slice. The times are simulated.
32 devices in a mesh: dp: 16 (over z, x, core), seq: 2 (over y).
Axes of the slice: x: 2, y: 2, z: 4, core: 2. Of those that a mesh axis runs over, the one named last changes fastest.
Arguments:
- decoder_in: bfloat16 [16, 1024, 768], P('dp', 'seq'), may hold values from -6 to 6
- encoder_out: bfloat16 [16, 2048, 768], P('dp', 'seq'), may hold values from -6 to 6
- dec_lengths: int32 [16, 2], P('dp'), may hold values from 1 to 1022, as said below
- pair_flags: int32 [16, 2], P('dp'), may hold values from 0 to 1
- enc_segments: int32 [16, 2048], P('dp'), may hold values from 0 to 2, as said below
- self_proj: float32 [3, 768, 768], P(None, ('dp', 'seq')), may hold values from -0.21875 to 0.21875
- self_out: float32 [768, 768], P(('dp', 'seq')), may hold values from -0.875 to 0.875
- cross_proj: float32 [3, 768, 768], P(None, ('dp', 'seq')), may hold values from -0.21875 to 0.21875
- cross_out: float32 [768, 768], P(('dp', 'seq')), may hold values from -1.25 to 1.25
- ffn_in: float32 [768, 3072], P(('dp', 'seq')), may hold values from -0.21875 to 0.21875
- ffn_out: float32 [3072, 768], P(('dp', 'seq')), may hold values from -0.109375 to 0.109375
- norm_gains: float32 [3, 768], P(None, ('dp', 'seq')), may hold values from 0.25 to 1.75
- rel_table: float32 [768], P(('dp', 'seq')), may hold values from -4 to 4
- out_grad: bfloat16 [16, 1024, 768], P('dp', 'seq'), may hold values from -6 to 6
Outputs:
- layer_out: bfloat16 [16, 1024, 768], P('dp', 'seq')
- grad_input: float32 [16, 1024, 768], P('dp', 'seq')
- grad_encoder: float32 [16, 2048, 768], P('dp', 'seq')
- grad_self_proj: float32 [3, 768, 768], P(None, ('dp', 'seq'))
- grad_self_out: float32 [768, 768], P(('dp', 'seq'))
- grad_cross_proj: float32 [3, 768, 768], P(None, ('dp', 'seq'))
- grad_cross_out: float32 [768, 768], P(('dp', 'seq'))
- grad_ffn_in: float32 [768, 3072], P(('dp', 'seq'))
- grad_ffn_out: float32 [3072, 768], P(('dp', 'seq'))
- grad_gains: float32 [3, 768], P(None, ('dp', 'seq'))
- grad_table: float32 [768], P(('dp', 'seq'))
Inputs may be any that keep to these rules, and one draw needn't show every extreme that they name: `dec_lengths`: each row holds the decoder lengths of the stream's two pairs; after them come 1 to 128 padding positions. Some stream has a pair of length 1 and one of length 1022. `enc_segments`: along a stream the pair numbers never fall: 0 for the first pair, 1 for the second, 2 for padding; each of the three appears, padding at most 1024 // 4 times.
All inputs are finite; a program needn't handle non-finite values.
Results may differ from a plain program's by a relative error of at most 0.03.
Values may be sent and summed in bfloat16 or wider, within the bound.
A program may use at most 1 GiB of HBM per device.

v0:
```python
from functools import partial

import jax
import jax.numpy as jnp
from jax import lax
from jax.sharding import PartitionSpec as P

D = 768
HEADS = 12
HDIM = 64
FF = 3072
BUCKETS = 32


epsilon = 1e-06
neg_large = -1e30
bucket_edges = (19, 21, 24, 27, 31, 35, 40, 46, 52, 59, 67, 77, 87, 99, 113)


def bucket_of(distance):
    above_count = sum(((distance >= border).astype(jnp.int32) for border in bucket_edges))
    return jnp.where(distance < 16, distance, 16 + above_count)


def rms_norm(values, gain_vec):
    return (
        values * lax.rsqrt(jnp.mean(values * values, axis=-1, keepdims=True) + epsilon) * gain_vec
    )


def pair_of(positions, lengths):
    first_len = lengths[:, 0:1]
    second_end = first_len + lengths[:, 1:2]
    return (positions[None, :] >= first_len).astype(jnp.int32) + (
        positions[None, :] >= second_end
    ).astype(jnp.int32)


def key_blocks(length):
    block_width = min(512, length)
    return [(block_start, block_width) for block_start in range(0, length, block_width)]


def split_heads(tensor):
    return tensor.reshape(tensor.shape[0], tensor.shape[1], HEADS, HDIM)


def merge_heads(tensor):
    return tensor.reshape(tensor.shape[0], tensor.shape[1], HEADS * HDIM)


def code_onehot(codes_block):
    code_range = jnp.arange(2 * BUCKETS, dtype=jnp.int32)
    return (codes_block[:, :, None, :] == code_range[None, None, :, None]).astype(jnp.bfloat16)


def build_bias(code_table, table_low):
    table_flat = table_low.reshape(2 * BUCKETS, HEADS)
    bias_parts = []
    for block_start, block_width in key_blocks(code_table.shape[2]):
        onehot = code_onehot(code_table[:, :, block_start : block_start + block_width])
        bias_parts.append(
            jnp.einsum("sqck,ch->shqk", onehot, table_flat, preferred_element_type=jnp.float32)
        )
    return jnp.concatenate(bias_parts, axis=3)


def attend_forward(queries, key_rows, value_rows, allowed, bias_term):
    scores = (
        jnp.einsum("sqhe,skhe->shqk", queries, key_rows, preferred_element_type=jnp.float32) * 0.125
        + bias_term
    )
    scores = jnp.where(allowed[:, None], scores, neg_large)
    row_peak = jnp.max(scores, axis=-1, keepdims=True)
    weighted = jnp.where(allowed[:, None], jnp.exp(scores - row_peak), 0.0)
    row_total = jnp.sum(weighted, axis=-1, keepdims=True)
    soft_probs = (weighted / row_total).astype(jnp.bfloat16)
    mixed_out = jnp.einsum(
        "shqk,skhe->sqhe", soft_probs, value_rows, preferred_element_type=jnp.float32
    ).astype(jnp.bfloat16)
    return (mixed_out, row_peak + jnp.log(row_total))


def head_delta(grad_mixed, mixed_out):
    products = jnp.sum(grad_mixed.astype(jnp.float32) * mixed_out.astype(jnp.float32), axis=-1)
    return jnp.transpose(products, (0, 2, 1))[..., None]


def query_backward(
    queries, key_rows, value_rows, allowed, log_total, row_delta, grad_mixed, code_table, table_low
):
    grad_queries = jnp.zeros(queries.shape, jnp.float32)
    table_grad = jnp.zeros((2 * BUCKETS, HEADS), jnp.float32)
    key_parts = []
    value_parts = []
    for block_start, block_width in key_blocks(key_rows.shape[1]):
        block_stop = block_start + block_width
        block_keys = key_rows[:, block_start:block_stop]
        block_values = value_rows[:, block_start:block_stop]
        scores = (
            jnp.einsum("sqhe,skhe->shqk", queries, block_keys, preferred_element_type=jnp.float32)
            * 0.125
        )
        if code_table is not None:
            onehot = code_onehot(code_table[:, :, block_start:block_stop])
            scores = scores + jnp.einsum(
                "sqck,ch->shqk",
                onehot,
                table_low.reshape(2 * BUCKETS, HEADS),
                preferred_element_type=jnp.float32,
            )
        soft_probs = jnp.where(
            allowed[:, None, :, block_start:block_stop], jnp.exp(scores - log_total), 0.0
        )
        grad_probs = jnp.einsum(
            "sqhe,skhe->shqk", grad_mixed, block_values, preferred_element_type=jnp.float32
        )
        grad_scores = (soft_probs * (grad_probs - row_delta)).astype(jnp.bfloat16)
        grad_queries = (
            grad_queries
            + jnp.einsum(
                "shqk,skhe->sqhe", grad_scores, block_keys, preferred_element_type=jnp.float32
            )
            * 0.125
        )
        key_parts.append(
            jnp.einsum("shqk,sqhe->skhe", grad_scores, queries, preferred_element_type=jnp.float32)
            * 0.125
        )
        value_parts.append(
            jnp.einsum(
                "shqk,sqhe->skhe",
                soft_probs.astype(jnp.bfloat16),
                grad_mixed,
                preferred_element_type=jnp.float32,
            )
        )
        if code_table is not None:
            table_grad = table_grad + jnp.einsum(
                "sqck,shqk->ch", onehot, grad_scores, preferred_element_type=jnp.float32
            )
    return (
        grad_queries,
        jnp.concatenate(key_parts, axis=1),
        jnp.concatenate(value_parts, axis=1),
        table_grad,
    )


def on_device(
    decoder_in,
    encoder_out,
    dec_lengths,
    pair_flags,
    enc_segments,
    self_proj,
    self_out,
    cross_proj,
    cross_out,
    ffn_in,
    ffn_out,
    norm_gains,
    rel_table,
    out_grad,
):
    flat_self = self_proj.astype(jnp.bfloat16).reshape(3, -1)
    flat_cross = cross_proj.astype(jnp.bfloat16).reshape(3, -1)
    gathered = (
        lax.all_gather(flat_self, ("dp", "seq"), axis=1, tiled=True),
        lax.all_gather(
            self_out.astype(jnp.bfloat16).reshape(-1), ("dp", "seq"), axis=0, tiled=True
        ),
        lax.all_gather(flat_cross, ("dp", "seq"), axis=1, tiled=True),
        lax.all_gather(
            cross_out.astype(jnp.bfloat16).reshape(-1), ("dp", "seq"), axis=0, tiled=True
        ),
        lax.all_gather(ffn_in.astype(jnp.bfloat16).reshape(-1), ("dp", "seq"), axis=0, tiled=True),
        lax.all_gather(ffn_out.astype(jnp.bfloat16).reshape(-1), ("dp", "seq"), axis=0, tiled=True),
        lax.all_gather(norm_gains.astype(jnp.bfloat16), ("dp", "seq"), axis=1, tiled=True),
        lax.all_gather(rel_table.astype(jnp.bfloat16), ("dp", "seq"), axis=0, tiled=True),
    )
    proj_self = gathered[0].reshape(3, D, D)
    out_self = gathered[1].reshape(D, D)
    proj_cross = gathered[2].reshape(3, D, D)
    out_cross = gathered[3].reshape(D, D)
    mat_in = gathered[4].reshape(D, FF)
    mat_out = gathered[5].reshape(FF, D)
    gain_low = gathered[6]
    table_low = gathered[7]
    gain_vals = gain_low.astype(jnp.float32)
    dec_shard = decoder_in.shape[1]
    seq_count = lax.axis_size("seq")
    seq_index = lax.axis_index("seq")
    dec_len = dec_shard * seq_count
    dec_all = jnp.arange(dec_len, dtype=jnp.int32)
    dec_here = seq_index * dec_shard + jnp.arange(dec_shard, dtype=jnp.int32)
    pair_here = pair_of(dec_here, dec_lengths)
    pair_all = pair_of(dec_all, dec_lengths)
    flag_here = jnp.where(
        pair_here == 0, pair_flags[:, 0:1], jnp.where(pair_here == 1, pair_flags[:, 1:2], 0)
    )
    self_allowed = (pair_here[:, :, None] == pair_all[:, None, :]) & (
        dec_all[None, None, :] <= dec_here[None, :, None]
    )
    distance = jnp.maximum(dec_here[:, None] - dec_all[None, :], 0)
    code_table = flag_here[:, :, None] * BUCKETS + bucket_of(distance)[None]
    cross_allowed = pair_here[:, :, None] == enc_segments[:, None, :]
    resid_in = decoder_in.astype(jnp.float32)
    normed_one = rms_norm(resid_in, gain_vals[0]).astype(jnp.bfloat16)
    qkv_here = jnp.einsum(
        "std,cde->stce", normed_one, proj_self, preferred_element_type=jnp.float32
    ).astype(jnp.bfloat16)
    kv_self = lax.all_gather(qkv_here[:, :, 1:], "seq", axis=1, tiled=True)
    queries_one = split_heads(qkv_here[:, :, 0])
    keys_one = split_heads(kv_self[:, :, 0])
    values_one = split_heads(kv_self[:, :, 1])
    bias_self = build_bias(code_table, table_low)
    mixed_one, lse_one = attend_forward(queries_one, keys_one, values_one, self_allowed, bias_self)
    attn_one = merge_heads(mixed_one)
    resid_one = resid_in + jnp.einsum(
        "ste,ed->std", attn_one, out_self, preferred_element_type=jnp.float32
    )
    normed_two = rms_norm(resid_one, gain_vals[1]).astype(jnp.bfloat16)
    query_two_flat = jnp.einsum(
        "std,de->ste", normed_two, proj_cross[0], preferred_element_type=jnp.float32
    ).astype(jnp.bfloat16)
    kv_enc_here = jnp.einsum(
        "std,cde->stce", encoder_out, proj_cross[1:], preferred_element_type=jnp.float32
    ).astype(jnp.bfloat16)
    kv_cross = lax.all_gather(kv_enc_here, "seq", axis=1, tiled=True)
    queries_two = split_heads(query_two_flat)
    keys_two = split_heads(kv_cross[:, :, 0])
    values_two = split_heads(kv_cross[:, :, 1])
    mixed_two, lse_two = attend_forward(queries_two, keys_two, values_two, cross_allowed, 0.0)
    attn_two = merge_heads(mixed_two)
    resid_two = resid_one + jnp.einsum(
        "ste,ed->std", attn_two, out_cross, preferred_element_type=jnp.float32
    )
    normed_three = rms_norm(resid_two, gain_vals[2]).astype(jnp.bfloat16)
    hidden_pre = jnp.einsum("std,df->stf", normed_three, mat_in, preferred_element_type=jnp.float32)
    hidden_act = jax.nn.gelu(hidden_pre, approximate=False).astype(jnp.bfloat16)
    layer_out = (
        resid_two
        + jnp.einsum("stf,fd->std", hidden_act, mat_out, preferred_element_type=jnp.float32)
    ).astype(jnp.bfloat16)
    grad_hidden = jnp.einsum("std,fd->stf", out_grad, mat_out, preferred_element_type=jnp.float32)
    grad_ffn_out = jnp.einsum(
        "stf,std->fd", hidden_act, out_grad, preferred_element_type=jnp.float32
    )
    gelu_pull = jax.vjp(partial(jax.nn.gelu, approximate=False), hidden_pre)[1]
    grad_pre = gelu_pull(grad_hidden)[0].astype(jnp.bfloat16)
    grad_ffn_in = jnp.einsum(
        "std,stf->df", normed_three, grad_pre, preferred_element_type=jnp.float32
    )
    grad_normed = jnp.einsum("stf,df->std", grad_pre, mat_in, preferred_element_type=jnp.float32)
    norm_pull = jax.vjp(rms_norm, resid_two, gain_vals[2])[1]
    grad_part, gain_three = norm_pull(grad_normed)
    grad_resid = out_grad.astype(jnp.float32) + grad_part
    grad_attn_two = grad_resid.astype(jnp.bfloat16)
    grad_cross_out = jnp.einsum(
        "ste,std->ed", attn_two, grad_attn_two, preferred_element_type=jnp.float32
    )
    grad_flat_two = jnp.einsum(
        "std,ed->ste", grad_attn_two, out_cross, preferred_element_type=jnp.float32
    ).astype(jnp.bfloat16)
    grad_mixed_two = split_heads(grad_flat_two)
    delta_two = head_delta(grad_mixed_two, mixed_two)
    grad_q_two, grad_k_two, grad_v_two, unused_table = query_backward(
        queries_two,
        keys_two,
        values_two,
        cross_allowed,
        lse_two,
        delta_two,
        grad_mixed_two,
        None,
        None,
    )
    cross_terms = jnp.stack((merge_heads(grad_k_two), merge_heads(grad_v_two)), axis=2)
    grad_kv_enc = lax.psum_scatter(
        cross_terms.astype(jnp.bfloat16), "seq", scatter_dimension=1, tiled=True
    )
    grad_query_two = merge_heads(grad_q_two).astype(jnp.bfloat16)
    grad_encoder = jnp.einsum(
        "stce,cde->std", grad_kv_enc, proj_cross[1:], preferred_element_type=jnp.float32
    )
    grad_cross_kv = jnp.einsum(
        "std,stce->cde", encoder_out, grad_kv_enc, preferred_element_type=jnp.float32
    )
    grad_cross_query = jnp.einsum(
        "std,ste->de", normed_two, grad_query_two, preferred_element_type=jnp.float32
    )
    grad_normed = jnp.einsum(
        "ste,de->std", grad_query_two, proj_cross[0], preferred_element_type=jnp.float32
    )
    norm_pull = jax.vjp(rms_norm, resid_one, gain_vals[1])[1]
    grad_part, gain_two = norm_pull(grad_normed)
    grad_resid = grad_resid + grad_part
    grad_attn_one = grad_resid.astype(jnp.bfloat16)
    grad_self_out = jnp.einsum(
        "ste,std->ed", attn_one, grad_attn_one, preferred_element_type=jnp.float32
    )
    grad_flat_one = jnp.einsum(
        "std,ed->ste", grad_attn_one, out_self, preferred_element_type=jnp.float32
    ).astype(jnp.bfloat16)
    grad_mixed_one = split_heads(grad_flat_one)
    delta_one = head_delta(grad_mixed_one, mixed_one)
    grad_q_one, grad_k_one, grad_v_one, table_grad = query_backward(
        queries_one,
        keys_one,
        values_one,
        self_allowed,
        lse_one,
        delta_one,
        grad_mixed_one,
        code_table,
        table_low,
    )
    self_terms = jnp.stack((merge_heads(grad_k_one), merge_heads(grad_v_one)), axis=2)
    grad_kv_self = lax.psum_scatter(
        self_terms.astype(jnp.bfloat16), "seq", scatter_dimension=1, tiled=True
    )
    grad_qkv = jnp.concatenate(
        (merge_heads(grad_q_one).astype(jnp.bfloat16)[:, :, None], grad_kv_self), axis=2
    )
    grad_self_proj = jnp.einsum(
        "std,stce->cde", normed_one, grad_qkv, preferred_element_type=jnp.float32
    )
    grad_normed = jnp.einsum(
        "stce,cde->std", grad_qkv, proj_self, preferred_element_type=jnp.float32
    )
    norm_pull = jax.vjp(rms_norm, resid_in, gain_vals[0])[1]
    grad_part, gain_one = norm_pull(grad_normed)
    grad_input = grad_resid + grad_part
    cross_all = jnp.concatenate((grad_cross_query[None], grad_cross_kv), axis=0)
    reduced = (
        lax.psum_scatter(
            grad_self_proj.reshape(3, -1), ("dp", "seq"), scatter_dimension=1, tiled=True
        ),
        lax.psum_scatter(grad_self_out.reshape(-1), ("dp", "seq"), scatter_dimension=0, tiled=True),
        lax.psum_scatter(cross_all.reshape(3, -1), ("dp", "seq"), scatter_dimension=1, tiled=True),
        lax.psum_scatter(
            grad_cross_out.reshape(-1), ("dp", "seq"), scatter_dimension=0, tiled=True
        ),
        lax.psum_scatter(grad_ffn_in.reshape(-1), ("dp", "seq"), scatter_dimension=0, tiled=True),
        lax.psum_scatter(grad_ffn_out.reshape(-1), ("dp", "seq"), scatter_dimension=0, tiled=True),
        lax.psum_scatter(
            jnp.stack((gain_one, gain_two, gain_three), axis=0),
            ("dp", "seq"),
            scatter_dimension=1,
            tiled=True,
        ),
        lax.psum_scatter(table_grad.reshape(-1), ("dp", "seq"), scatter_dimension=0, tiled=True),
    )
    return (
        layer_out,
        grad_input,
        grad_encoder,
        reduced[0].reshape(self_proj.shape),
        reduced[1].reshape(self_out.shape),
        reduced[2].reshape(cross_proj.shape),
        reduced[3].reshape(cross_out.shape),
        reduced[4].reshape(ffn_in.shape),
        reduced[5].reshape(ffn_out.shape),
        reduced[6],
        reduced[7],
    )


def solution(mesh):
    placed = (
        P("dp", "seq", None),
        P("dp", "seq", None),
        P("dp", None),
        P("dp", None),
        P("dp", None),
        P(None, ("dp", "seq"), None),
        P(("dp", "seq"), None),
        P(None, ("dp", "seq"), None),
        P(("dp", "seq"), None),
        P(("dp", "seq"), None),
        P(("dp", "seq"), None),
        P(None, ("dp", "seq")),
        P(("dp", "seq")),
        P("dp", "seq", None),
    )
    return jax.shard_map(
        on_device,
        mesh=mesh,
        in_specs=placed,
        out_specs=(
            P("dp", "seq", None),
            P("dp", "seq", None),
            P("dp", "seq", None),
            P(None, ("dp", "seq"), None),
            P(("dp", "seq"), None),
            P(None, ("dp", "seq"), None),
            P(("dp", "seq"), None),
            P(("dp", "seq"), None),
            P(("dp", "seq"), None),
            P(None, ("dp", "seq")),
            P(("dp", "seq")),
        ),
        check_vma=False,
    )
```

profile of v0, /device:TPU:0, one launch (start us, length us, event | category | flops | bytes accessed | tf_op | source)
XLA Modules:
  0.0 6349.8 jit_solution(15712139526273563708)
XLA Ops:
  21.9 42.4 all-reduce
  64.4 65.9 %all-gather.1 = bf16[32,24,3]{1,2,0:T(4,128)(2,1)S(1)} all-gather(bf16[1,24,3]{1,2,0:T(4,128)(2,1)S(1)} %convert_bitcast_fusion.4), channel_id=1, replica_groups=mesh['dp'=16,'seq'=2] {'dp','seq'}, dimensions={0}, use_global_device_ids=true | all-gather | bytes 4752 | tf_op jit(solution)/shard_map/all_gather | solution.py:179
  144.1 12.3 iota_compare_fusion
  156.4 90.3 %copy.258 = pred[512,64,512]{2,1,0:T(32,128)(4,1)} copy(pred[512,64,512]{0,1,2:T(32,128)(4,1)} %iota_compare_fusion) | data formatting | bytes 33554432 | tf_op jit(solution)/shard_map/eq | solution.py:54
  246.7 11.0 iota_compare_fusion.1
  257.7 90.3 %copy.255 = pred[512,64,512]{2,1,0:T(32,128)(4,1)} copy(pred[512,64,512]{0,1,2:T(32,128)(4,1)} %iota_compare_fusion.1) | data formatting | bytes 33554432 | tf_op jit(solution)/shard_map/eq | solution.py:54
  348.8 17.4 fusion.168
  366.3 16.9 fusion.170
  391.2 18.4 copy.260
  409.6 18.0 copy.259
  442.6 24.1 slice_reduce_fusion
  480.9 8.7 reshape.1394
  489.5 9.3 reshape.1396
  507.9 18.0 fusion.199
  525.9 12.0 fusion.4
  537.9 11.7 fusion.112
  554.9 9.9 exponential_select_fusion.2
  564.8 9.5 exponential_select_fusion.3
  616.6 22.7 fusion
  639.3 22.6 fusion.1
  662.0 21.8 fusion.113
  684.8 21.2 multiply_convert_fusion.6
  884.8 10.8 reshape.1425
  919.2 141.7 %copy.296 = f32[3,768,768]{0,2,1:T(8,128)} copy(f32[3,768,768]{1,2,0:T(8,128)} %convolution_bitcast_fusion.1) | data formatting | bytes 14155776
  1086.9 129.0 %copy.292 = f32[3,589824]{0,1:T(8,128)} copy(f32[3,589824]{1,0:T(4,128)} %pad_maximum_fusion) | data formatting | bytes 14155776
  1215.9 14.4 copy.282
  1230.4 14.8 copy.281
  1245.2 12.2 convolution_bitcast_fusion.4
  1257.5 10.6 fusion.138
  1281.6 38.3 all-reduce.7
  1338.7 2488.1 %reduce-scatter.14.cloned.1.call-done = f32[18432,3]{1,0:T(8,128)} async-done(((f32[589824,3]{1,0:T(8,128)}), f32[18432,3]{1,0:T(8,128)}) %reduce-scatter.14.cloned.1.call-update) | async-done | bytes 221200
  3834.0 2501.9 %reduce-scatter.16.cloned.1.call-done = f32[18432,3]{1,0:T(8,128)} async-done(((f32[589824,3]{1,0:T(8,128)}), f32[18432,3]{1,0:T(8,128)}) %reduce-scatter.16.cloned.1.call-update) | async-done | bytes 221200
  (408 shorter events, 396.6 us)
Async XLA Ops:
  7.2 469.6 %copy-start = (bf16[1,1024,768]{2,1,0:T(8,128)(2,1)S(1)}, bf16[1,1024,768]{2,1,0:T(8,128)(2,1)}, u32[]{:S(2)}) copy-start(bf16[1,1024,768]{2,1,0:T(8,128)(2,1)} %param.15) | copy-start | bytes 4718596
  7.2 376.0 %all-gather.11.cloned.1.call-start = ((), (), s32[]{:S(2)}) async-start(), calls=%async_computation.4 | async-start | bytes 4866048 | tf_op jit(solution)/shard_map/all_gather | solution.py:169
  9.0 424.7 %all-gather.15.cloned.1.call-start = ((), (), s32[]{:S(2)}) async-start(), calls=%async_computation.6 | async-start | bytes 1216512 | tf_op jit(solution)/shard_map/all_gather | solution.py:170
  10.7 426.4 %all-gather.19.cloned.1.call-start = ((), (), s32[]{:S(2)}) async-start(), calls=%async_computation.8 | async-start | bytes 1216512 | tf_op jit(solution)/shard_map/all_gather | solution.py:174
  12.3 430.2 %all-gather.17.cloned.1.call-start = ((), (), s32[]{:S(2)}) async-start(), calls=%async_computation.7 | async-start | bytes 4866048 | tf_op jit(solution)/shard_map/all_gather | solution.py:173
  14.1 466.8 %all-gather.21.cloned.1.call-start = ((), (), s32[]{:S(2)}) async-start(), calls=%async_computation.9 | async-start | bytes 4866048 | tf_op jit(solution)/shard_map/all_gather | solution.py:177
  15.8 473.7 %all-gather.23.cloned.1.call-start = ((), (), s32[]{:S(2)}) async-start(), calls=%async_computation.10 | async-start | bytes 4866048 | tf_op jit(solution)/shard_map/all_gather | solution.py:178
  17.7 481.2 %all-gather.13.cloned.1.call-start = ((), (), s32[]{:S(2)}) async-start(), calls=%async_computation.5 | async-start | bytes 4718592 | tf_op jit(solution)/shard_map/all_gather | solution.py:213
  141.2 105.5 %copy-start.32 = (s32[512,512]{0,1:T(8,128)}, s32[512,512]{0,1:T(8,128)S(1)}, u32[]{:S(2)}) copy-start(s32[512,512]{0,1:T(8,128)S(1)} %copy.253) | copy-start | bytes 3145732
  257.7 90.9 %copy-start.42 = (bf16[1,512,768]{2,1,0:T(8,128)(2,1)S(1)}, bf16[1,512,768]{2,1,0:T(8,128)(2,1)}, u32[]{:S(2)}) copy-start(bf16[1,512,768]{2,1,0:T(8,128)(2,1)} %param.14) | copy-start | bytes 2359300
  348.6 34.7 copy-start.73
  348.6 202.0 %copy-start.66 = (f32[768]{0:T(1024)}, f32[768]{0:T(1024)S(1)}, u32[]{:S(2)}) copy-start(f32[768]{0:T(1024)S(1)} %get-tuple-element.18) | copy-start | bytes 9220
  348.8 34.4 copy-start.76
  390.3 184.0 %all-gather.25.cloned.1.call-start = ((), (), s32[]{:S(2)}) async-start(), calls=%async_computation.13 | async-start | bytes 9437184 | tf_op jit(solution)/shard_map/all_gather | solution.py:230
  470.0 94.8 %copy-start.9 = (bf16[1,512,1,768]{1,3,2,0:T(8,128)(2,1)}, bf16[1,512,1,768]{1,3,2,0:T(8,128)(2,1)S(1)}, u32[]{:S(2)}) copy-start(bf16[1,512,1,768]{1,3,2,0:T(8,128)(2,1)S(1)} %copy.251) | copy-start | bytes 2359300
  480.8 431.5 %reduce-scatter.10.cloned.1.call-start = ((), (), s32[]{:S(2)}) async-start(), calls=%async_computation.11 | async-start | bytes 4718592 | tf_op jit(solution)/shard_map/reduce_scatter | solution.py:320
  554.9 61.7 copy-start.1
  661.9 21.9 copy-start.19
  662.0 21.9 copy-start.31
  683.8 22.2 copy-start.27
  683.8 29.4 slice-start.19
  684.7 31.9 copy-start.15
  684.8 21.2 copy-start.30
  684.8 21.2 copy-start.56
  684.8 28.5 slice-start.20
  717.1 54.5 copy-start.23
  818.4 242.6 %reduce-scatter.12.cloned.1.call-start = ((), (), s32[]{:S(2)}) async-start(), calls=%async_computation.12 | async-start | bytes 9437184 | tf_op jit(solution)/shard_map/reduce_scatter | solution.py:280
  853.4 470.9 %all-reduce.11.cloned.1.call-start = ((), (), s32[]{:S(2)}) async-start(), calls=%async_computation.16 | async-start | bytes 47185920
  895.7 2931.2 %reduce-scatter.14.cloned.1.call-start = ((), (), s32[]{:S(2)}) async-start(), calls=%async_computation.14 | async-start | bytes 311427072
  1061.0 5274.9 %reduce-scatter.16.cloned.1.call-start = ((), (), s32[]{:S(2)}) async-start(), calls=%async_computation.15 | async-start | bytes 311427072
  1275.3 45.7 copy-start.72
  1275.3 45.8 copy-start.22
  (87 other events, 565.3 us)
Sparse Core Ops, SparseCore 0:
  11.5 67.4 all-gather.10
  82.5 52.5 all-gather.14
  138.6 53.0 all-gather.18
  195.1 62.5 all-gather.16
  260.5 62.4 all-gather.20
  325.8 62.4 all-gather.22
  390.5 43.6 all-gather.12
  480.9 76.2 all-gather.24
  818.5 39.1 reduce-scatter.9
  860.0 77.0 reduce-scatter.11
  943.6 375.0 all-reduce.10
  1325.0 2501.8 reduce-scatter.13
  3834.4 2501.4 reduce-scatter.15
where the time goes:
time: 6360 us; the launch traced here: 6350 us
  waiting for transfers between devices  4990 us (78%)
  local copies, waits for them, and re-layouts  709 us (11%)
  matrix products  388 us (6%)
  blocking collectives  147 us (2%)
  other arithmetic  98.5 us (2%)
    unnamed x16, waiting for transfers between devices  4990 us
    unnamed x228, local copies, waits for them, and re-layouts  308 us
    eq x5, local copies, waits for them, and re-layouts, code_onehot(): codes_block[:, :, None, :] == code_range[None, None, :, None]  187 us
  transfers between devices with their start and end apart: 13, of which 2 were waited for; matrix products, arithmetic and copies ran while one was open for 15% of the time, Pallas kernels for 0%

commit v1 on v0

v1 whole, which is shorter than its diff:
```python
import functools
import math

import jax
import jax.numpy as jnp
from jax import lax
from jax.experimental import pallas as pl
from jax.experimental.pallas import tpu as pltpu
from jax.sharding import PartitionSpec as P

D = 768
HEADS = 12
HDIM = 64
FF = 3072
BUCKETS = 32
PAIRS = HEADS // 2
LOG2E = math.log2(math.e)
LN2 = math.log(2.0)
epsilon = 1e-06
neg_large = -1e30
bucket_edges = (19, 21, 24, 27, 31, 35, 40, 46, 52, 59, 67, 77, 87, 99, 113)
f32 = jnp.float32
bf16 = jnp.bfloat16
NT = (((1,), (1,)), ((), ()))
NN = (((1,), (0,)), ((), ()))
TN = (((0,), (0,)), ((), ()))
BOTH = ("dp", "seq")


def bucket_of(distance):
    above_count = sum(((distance >= border).astype(jnp.int32) for border in bucket_edges))
    return jnp.where(distance < 16, distance, 16 + above_count)


def mm(a, b, dims=NN):
    return lax.dot_general(a, b, dims, preferred_element_type=f32)


def head_lanes(which):
    low = lax.broadcasted_iota(jnp.int32, (1, 128), 1) < HDIM
    return low if which == 0 else jnp.logical_not(low)


def row_chunks(rows, keys, causal, step):
    return [
        (slice(i, i + step), (keys - rows + i + step) if causal else keys)
        for i in range(0, rows, step)
    ]


def near_bias(near_ref, which):
    row = lax.broadcasted_iota(jnp.int32, (128, 256), 0)
    column = lax.broadcasted_iota(jnp.int32, (128, 256), 1)
    tiles = []
    for flag in (0, 1):
        line = near_ref[0, 2 * which + flag : 2 * which + flag + 1, :]
        tile = pltpu.roll(jnp.broadcast_to(line, (128, 256)), 0, 1, stride=1, stride_axis=0)
        tiles.append(jnp.where(column - row > 128, neg_large, tile))
    return tiles


def diagonal_sums(tile):
    for step in (64, 32, 16, 8):
        tile = tile[:step] + pltpu.roll(tile[step:], 256 - step, 1)
    row = lax.broadcasted_iota(jnp.int32, (8, 256), 0)
    for step in (4, 2, 1):
        tile = jnp.where((row & step) != 0, pltpu.roll(tile, 256 - step, 1), tile)
    return jnp.sum(tile, axis=0, keepdims=True)


def attend_body(rows, keys, causal, step, *refs):
    if causal:
        q_ref, k_ref, v_ref, qx_ref, kx_ref, far_ref, near_ref, flag_ref = refs[:8]
    else:
        q_ref, k_ref, v_ref, qx_ref, kx_ref = refs[:5]
    o_ref, e_ref, inv_ref = refs[-3:]
    extra = kx_ref[...]
    if causal:
        extra = extra + far_ref[0]
    key_pair = k_ref[...]
    value_pair = v_ref[...]
    chunks = row_chunks(rows, keys, causal, step)
    found = []
    for which in (0, 1):
        mine = head_lanes(which)
        key_head = jnp.where(mine, key_pair, extra)
        value_head = jnp.where(mine, value_pair, jnp.ones_like(value_pair))
        if causal:
            tile_zero, tile_one = near_bias(near_ref, which)
        parts = []
        for here, width in chunks:
            query = jnp.where(mine, q_ref[here], qx_ref[here])
            scores = mm(query, key_head[:width], NT)
            if causal:
                cut = width - 256
                near = scores[:, cut:] + jnp.where(flag_ref[here, :1] > 0, tile_one, tile_zero)
                far = scores[:, :cut]
                peak = jnp.maximum(
                    jnp.max(far, axis=1, keepdims=True), jnp.max(near, axis=1, keepdims=True)
                )
                near = jnp.exp2(near - peak).astype(bf16)
                far = jnp.exp2(far - peak).astype(bf16)
                e_ref[which, here, :cut] = far
                e_ref[which, here, cut:width] = near
                mixed = mm(far, value_head[:cut]) + mm(near, value_head[cut:width])
            else:
                peak = jnp.max(scores, axis=1, keepdims=True)
                weights = jnp.exp2(scores - peak).astype(bf16)
                e_ref[which, here, :] = weights
                mixed = mm(weights, value_head)
            total = mixed[:, HDIM : HDIM + 1] if which == 0 else mixed[:, 0:1]
            inverse = 1.0 / total
            parts.append((mixed * inverse, jnp.broadcast_to(inverse, mixed.shape)))
        found.append(parts)
    low = head_lanes(0)
    for index, (here, _) in enumerate(chunks):
        o_ref[here] = jnp.where(low, found[0][index][0], found[1][index][0]).astype(bf16)
        inv_ref[here] = jnp.where(low, found[0][index][1], found[1][index][1])


def pair_columns(rows):
    return pl.BlockSpec((rows, 128), lambda p: (0, p))


def same_block(rows):
    return pl.BlockSpec((rows, 128), lambda p: (0, 0))


def per_pair(height, width):
    return pl.BlockSpec((1, height, width), lambda p: (p, 0, 0))


def attend(query, key, value, query_extra, key_extra, far=None, near=None, flags=None):
    rows, keys = query.shape[0], key.shape[0]
    causal = far is not None
    step = 128 if causal else min(256, rows)
    operands = [query, key, value, query_extra, key_extra]
    specs = [
        pair_columns(rows),
        pair_columns(keys),
        pair_columns(keys),
        same_block(rows),
        same_block(keys),
    ]
    if causal:
        operands += [far, near, flags]
        specs += [per_pair(1, 128), per_pair(4, 256), same_block(rows)]
    work = HEADS * rows * keys
    return pl.pallas_call(
        functools.partial(attend_body, rows, keys, causal, step),
        grid=(PAIRS,),
        in_specs=specs,
        out_specs=(
            pair_columns(rows),
            pl.BlockSpec((2, rows, keys), lambda p: (p, 0, 0)),
            pair_columns(rows),
        ),
        out_shape=(
            jax.ShapeDtypeStruct((rows, D), bf16),
            jax.ShapeDtypeStruct((HEADS, rows, keys), bf16),
            jax.ShapeDtypeStruct((rows, D), f32),
        ),
        compiler_params=pltpu.CompilerParams(vmem_limit_bytes=56 << 20),
        cost_estimate=pl.CostEstimate(
            flops=4 * work * 256, bytes_accessed=2 * work, transcendentals=work
        ),
        name="attend_causal" if causal else "attend_cross",
    )(*operands)


def attend_back_body(rows, keys, causal, step, *refs):
    q_ref, k_ref, v_ref, e_ref, o_ref, inv_ref, d_ref = refs[:7]
    if causal:
        flag_ref, dq_ref, dk_ref, dv_ref, near_ref, sum_ref, ds_ref = refs[7:]
    else:
        dq_ref, dk_ref, dv_ref, ds_ref = refs[7:]
    lane = lax.broadcasted_iota(jnp.int32, (1, 128), 1)
    key_pair = k_ref[...]
    value_pair = v_ref[...]
    scaled = (d_ref[...].astype(f32) * inv_ref[...]).astype(bf16)
    product = scaled.astype(f32) * o_ref[...].astype(f32)
    scaled_t = scaled.T
    query_t = q_ref[...].T
    chunks = row_chunks(rows, keys, causal, step)
    query_parts = []
    for which in (0, 1):
        mine = head_lanes(which)
        base = HDIM if which == 0 else 0
        value_head = jnp.where(mine, value_pair, jnp.ones_like(value_pair))
        key_head = jnp.where(mine, key_pair, jnp.ones_like(key_pair))
        delta = jnp.sum(jnp.where(mine, product, 0.0), axis=1, keepdims=True)
        high = delta.astype(bf16)
        rest = (delta - high.astype(f32)).astype(bf16)
        extra = jnp.where(
            lane == base, -high, jnp.where(lane == base + 1, -rest, jnp.zeros_like(rest))
        )
        grad_head = jnp.where(mine, scaled, extra)
        parts = []
        if causal:
            near_all = jnp.zeros((128, 256), f32)
            near_one = jnp.zeros((128, 256), f32)
        for here, width in chunks:
            centred = mm(grad_head[here], value_head[:width], NT)
            grad_scores = e_ref[which, here, :width].astype(f32) * centred
            if causal:
                near = grad_scores[:, width - 256 :]
                near_all = near_all + near
                near_one = near_one + jnp.where(flag_ref[here, :1] > 0, near, 0.0)
            grad_scores = grad_scores.astype(bf16)
            ds_ref[here, :width] = grad_scores
            parts.append(mm(grad_scores, key_head[:width]))
        query_parts.append(parts)
        half = slice(HDIM * which, HDIM * which + HDIM)
        if causal:
            spans = [(slice(0, keys - rows), 0)] if keys > rows else []
            spans += [
                (slice(keys - rows + i, keys - rows + i + step), i) for i in range(0, rows, step)
            ]
        else:
            spans = [(slice(0, keys), 0)]
        for span, first in spans:
            grad_key = mm(query_t[half, first:], ds_ref[first:, span])
            dk_ref[half, span] = (grad_key * LN2).astype(dk_ref.dtype)
            grad_value = mm(scaled_t[half, first:], e_ref[which, first:, span])
            dv_ref[half, span] = grad_value.astype(dv_ref.dtype)
        if causal:
            for flag, tile in ((0, near_all - near_one), (1, near_one)):
                near_ref[0, 2 * which + flag : 2 * which + flag + 1, :] = diagonal_sums(tile)
    low = head_lanes(0)
    for index, (here, _) in enumerate(chunks):
        both = jnp.where(low, query_parts[0][index], query_parts[1][index])
        dq_ref[here] = (both * 0.125).astype(dq_ref.dtype)
    if causal:
        flagged = flag_ref[:, :1] > 0
        for which in (0, 1):
            whole = jnp.concatenate(query_parts[which], axis=0)
            one = jnp.sum(jnp.where(flagged, whole, 0.0), axis=0, keepdims=True)
            every = jnp.sum(whole, axis=0, keepdims=True)
            sum_ref[0, 2 * which : 2 * which + 1, :] = every - one
            sum_ref[0, 2 * which + 1 : 2 * which + 2, :] = one


def attend_back(query, key, value, weights, mixed, inverse, grad_mixed, flags=None):
    rows, keys = query.shape[0], key.shape[0]
    causal = flags is not None
    step = 128 if causal else min(256, rows)
    operands = [query, key, value, weights, mixed, inverse, grad_mixed]
    specs = [
        pair_columns(rows),
        pair_columns(keys),
        pair_columns(keys),
        pl.BlockSpec((2, rows, keys), lambda p: (p, 0, 0)),
        pair_columns(rows),
        pair_columns(rows),
        pair_columns(rows),
    ]
    turned = jax.ShapeDtypeStruct((D, keys), bf16)
    turned_spec = pl.BlockSpec((128, keys), lambda p: (p, 0))
    shapes = [jax.ShapeDtypeStruct((rows, D), bf16), turned, turned]
    out_specs = [pair_columns(rows), turned_spec, turned_spec]
    if causal:
        operands.append(flags)
        specs.append(same_block(rows))
        shapes += [
            jax.ShapeDtypeStruct((PAIRS, 4, 256), f32),
            jax.ShapeDtypeStruct((PAIRS, 4, 128), f32),
        ]
        out_specs += [per_pair(4, 256), per_pair(4, 128)]
    work = HEADS * rows * keys
    return pl.pallas_call(
        functools.partial(attend_back_body, rows, keys, causal, step),
        grid=(PAIRS,),
        in_specs=specs,
        out_specs=tuple(out_specs),
        out_shape=tuple(shapes),
        scratch_shapes=[pltpu.VMEM((rows, keys), bf16)],
        compiler_params=pltpu.CompilerParams(vmem_limit_bytes=56 << 20),
        cost_estimate=pl.CostEstimate(
            flops=6 * work * 256, bytes_accessed=2 * work, transcendentals=0
        ),
        name="attend_causal_back" if causal else "attend_cross_back",
    )(*operands)


def pair_of(positions, lengths):
    return (positions >= lengths[0]).astype(jnp.int32) + (
        positions >= lengths[0] + lengths[1]
    ).astype(jnp.int32)


def on_both_halves(columns):
    half = jnp.pad(columns, ((0, 0), (0, HDIM - columns.shape[1])))
    return jnp.concatenate((half, half), axis=1).astype(bf16)


def pair_mask(key_pairs):
    wrong = key_pairs[:, None] != jnp.arange(3, dtype=jnp.int32)[None, :]
    return on_both_halves(jnp.where(wrong, neg_large, 0.0))


def bias_parts(table):
    scaled = table.astype(f32) * LOG2E
    far = jnp.stack((scaled[BUCKETS - 1], scaled[2 * BUCKETS - 1]), axis=0)
    high = far.astype(bf16)
    rest = (far - high.astype(f32)).astype(bf16)
    columns = jnp.stack((high[0], rest[0], high[1], rest[1]), axis=1)
    columns = jnp.pad(columns, ((0, 0), (3, HDIM - 7))).reshape(PAIRS, 2, HDIM)
    far_lanes = jnp.concatenate((columns[:, 1], columns[:, 0]), axis=1).reshape(PAIRS, 1, 128)
    place = jnp.arange(256, dtype=jnp.int32)
    buckets = bucket_of(jnp.where(place <= 128, 128 - place, 384 - place))
    chosen = (buckets[:, None] == jnp.arange(BUCKETS, dtype=jnp.int32)[None, :]).astype(f32)
    steps = scaled.reshape(2, BUCKETS, HEADS) - far[:, None, :]
    lines = jnp.einsum("jb,fbh->hfj", chosen, steps, precision=lax.Precision.HIGHEST)
    return far_lanes, lines.reshape(PAIRS, 4, 256), chosen


def table_gradient(near_lines, row_sums, chosen):
    lines = near_lines.reshape(HEADS, 2, 256)
    near = jnp.einsum("hfj,jb->fbh", lines, chosen, precision=lax.Precision.HIGHEST)
    sums = row_sums.reshape(PAIRS, 2, 2, 128)
    every = jnp.stack((sums[:, 0, :, HDIM], sums[:, 1, :, 0]), axis=1).reshape(HEADS, 2).T
    rest = every - jnp.sum(near[:, : BUCKETS - 1], axis=1)
    return jnp.concatenate((near[:, : BUCKETS - 1], rest[:, None]), axis=1).reshape(-1)


def inverse_rms(values):
    return lax.rsqrt(jnp.mean(values * values, axis=-1, keepdims=True) + epsilon)


def norm_back(values, inverse, gain, grad):
    unit = values * inverse
    grad_gain = jnp.sum(grad * unit, axis=0)
    grad = grad * gain
    return inverse * (grad - unit * jnp.mean(grad * unit, axis=-1, keepdims=True)), grad_gain


def gelu_and_slope(value):
    upper = 0.5 * (1.0 + lax.erf(value * math.sqrt(0.5)))
    density = jnp.exp(-0.5 * value * value) * (1.0 / math.sqrt(2.0 * math.pi))
    return value * upper, upper + value * density


def seq_shift(array, count):
    length = array.shape[0]
    return lax.dynamic_slice_in_dim(jnp.concatenate((array, array), axis=0), count, length, axis=0)


def others_rows(rows, own_last):
    parts = lax.axis_size("seq")
    if parts == 2:
        return lax.ppermute(rows, "seq", [(0, 1)] if own_last else [(0, 1), (1, 0)])
    whole = lax.all_gather(rows, "seq", axis=0, tiled=True)
    step = rows.shape[0]
    start = lax.rem(lax.axis_index("seq") + 1, parts) * step
    return seq_shift(whole, start)[: (parts - 1) * step]


def to_owners(grads, own_last):
    parts = lax.axis_size("seq")
    if parts == 2:
        return lax.ppermute(grads, "seq", [(1, 0)] if own_last else [(0, 1), (1, 0)])
    step = grads.shape[0] // (parts - 1)
    whole = jnp.concatenate((grads, jnp.zeros((step, grads.shape[1]), grads.dtype)), axis=0)
    start = lax.rem(parts - 1 - lax.axis_index("seq"), parts) * step
    return lax.psum_scatter(seq_shift(whole, start), "seq", scatter_dimension=0, tiled=True)


def on_device(
    decoder_in,
    encoder_out,
    dec_lengths,
    pair_flags,
    enc_segments,
    self_proj,
    self_out,
    cross_proj,
    cross_out,
    ffn_in,
    ffn_out,
    norm_gains,
    rel_table,
    out_grad,
):
    shard = self_out.shape[0]
    small = jnp.concatenate((norm_gains, rel_table[None]), axis=0).T
    block_self = jnp.concatenate(
        (self_proj[0], self_proj[1], self_proj[2], self_out, jnp.pad(small, ((0, 0), (0, 124)))),
        axis=1,
    ).astype(bf16)
    block_cross = jnp.concatenate(
        (cross_proj[0], cross_proj[1], cross_proj[2], cross_out), axis=1
    ).astype(bf16)
    all_self = lax.all_gather(block_self, BOTH, axis=0, tiled=True)
    all_cross = lax.all_gather(block_cross, BOTH, axis=0, tiled=True)
    mat_in = lax.all_gather(ffn_in.astype(bf16), BOTH, axis=0, tiled=True)
    mat_out = lax.all_gather(ffn_out.astype(bf16), BOTH, axis=0, tiled=True)
    self_q, self_k, self_v, out_self = (all_self[:, i * D : (i + 1) * D] for i in range(4))
    cross_q, cross_k, cross_v, out_cross = (all_cross[:, i * D : (i + 1) * D] for i in range(4))
    small_all = all_self[:, 4 * D : 4 * D + 4].T
    gains = small_all[:3].astype(f32)
    table = small_all[3].reshape(2 * BUCKETS, HEADS)

    tokens = decoder_in[0]
    memory = encoder_out[0]
    grad_out = out_grad[0]
    rows, enc_rows = tokens.shape[0], memory.shape[0]
    seq_count = lax.axis_size("seq")
    seq_index = lax.axis_index("seq")
    keys, enc_keys = rows * seq_count, enc_rows * seq_count

    lengths = dec_lengths[0]
    place_here = seq_index * rows + jnp.arange(rows, dtype=jnp.int32)
    place_keys = (seq_index + 1) * rows - keys + jnp.arange(keys, dtype=jnp.int32)
    pair_here = pair_of(place_here, lengths)
    pair_keys = jnp.where(place_keys < 0, 3, pair_of(place_keys, lengths))
    segments = seq_shift(enc_segments[0], seq_index * enc_rows)
    flag_here = jnp.where(
        pair_here == 0, pair_flags[0, 0], jnp.where(pair_here == 1, pair_flags[0, 1], 0)
    )
    one_pair = (pair_here[:, None] == jnp.arange(3, dtype=jnp.int32)[None, :]).astype(f32)
    one_flag = (flag_here[:, None] == jnp.array((0, 0, 1, 1), jnp.int32)[None, :]).astype(f32)
    query_extra = on_both_halves(jnp.concatenate((one_pair, one_flag), axis=1))
    key_extra = pair_mask(pair_keys)
    memory_extra = pair_mask(segments)
    flag_rows = jnp.broadcast_to(flag_here.astype(f32)[:, None], (rows, 128))
    far_lanes, near_lines, chosen = bias_parts(table)

    before = others_rows(tokens, True)
    others = others_rows(memory, False)
    memory_all = jnp.concatenate((memory, others), axis=0)

    tokens = tokens.astype(f32)
    inverse_one = inverse_rms(tokens)
    normed_one = (tokens * inverse_one * gains[0]).astype(bf16)
    before = before.astype(f32)
    normed_before = (before * inverse_rms(before) * gains[0]).astype(bf16)
    normed_all = jnp.concatenate((normed_before, normed_one), axis=0)
    scale = 0.125 * LOG2E
    query_one = (mm(normed_one, self_q) * scale).astype(bf16)
    key_one = mm(normed_all, self_k).astype(bf16)
    value_one = mm(normed_all, self_v).astype(bf16)
    mixed_one, weights_one, total_one = attend(
        query_one, key_one, value_one, query_extra, key_extra, far_lanes, near_lines, flag_rows
    )
    resid_one = tokens + mm(mixed_one, out_self)
    inverse_two = inverse_rms(resid_one)
    normed_two = (resid_one * inverse_two * gains[1]).astype(bf16)
    query_two = (mm(normed_two, cross_q) * scale).astype(bf16)
    key_two = mm(memory_all, cross_k).astype(bf16)
    value_two = mm(memory_all, cross_v).astype(bf16)
    mixed_two, weights_two, total_two = attend(
        query_two, key_two, value_two, query_extra, memory_extra
    )
    resid_two = resid_one + mm(mixed_two, out_cross)
    inverse_three = inverse_rms(resid_two)
    normed_three = (resid_two * inverse_three * gains[2]).astype(bf16)
    hidden_act, hidden_slope = gelu_and_slope(mm(normed_three, mat_in))
    hidden_act = hidden_act.astype(bf16)
    layer_out = (resid_two + mm(hidden_act, mat_out)).astype(bf16)

    grad_pre = (hidden_slope * mm(grad_out, mat_out, NT)).astype(bf16)
    grad_ffn_out = mm(hidden_act, grad_out, TN).astype(bf16)
    grad_ffn_in = mm(normed_three, grad_pre, TN).astype(bf16)
    part, gain_three = norm_back(resid_two, inverse_three, gains[2], mm(grad_pre, mat_in, NT))
    grad_resid = grad_out.astype(f32) + part
    grad_low = grad_resid.astype(bf16)
    grad_cross_out = mm(mixed_two, grad_low, TN)
    grad_mixed = mm(grad_low, out_cross, NT).astype(bf16)
    grad_query, grad_key, grad_value = attend_back(
        query_two, key_two, value_two, weights_two, mixed_two, total_two, grad_mixed
    )
    turned = (((0,), (1,)), ((), ()))
    grad_memory = mm(grad_key, cross_k, turned) + mm(grad_value, cross_v, turned)
    grad_others = to_owners(grad_memory[enc_rows:].astype(bf16), False)
    grad_encoder = grad_memory[:enc_rows] + grad_others.astype(f32)
    grad_cross = jnp.concatenate(
        (
            mm(normed_two, grad_query, TN),
            mm(memory_all, grad_key, turned),
            mm(memory_all, grad_value, turned),
            grad_cross_out,
        ),
        axis=1,
    ).astype(bf16)
    part, gain_two = norm_back(resid_one, inverse_two, gains[1], mm(grad_query, cross_q, NT))
    grad_resid = grad_resid + part
    grad_low = grad_resid.astype(bf16)
    grad_self_out = mm(mixed_one, grad_low, TN)
    grad_mixed = mm(grad_low, out_self, NT).astype(bf16)
    grad_query, grad_key, grad_value, near_sums, row_sums = attend_back(
        query_one, key_one, value_one, weights_one, mixed_one, total_one, grad_mixed, flag_rows
    )
    grad_normed = mm(grad_key, self_k, turned) + mm(grad_value, self_v, turned)
    grad_before = to_owners(grad_normed[: keys - rows].astype(bf16), True)
    grad_normed = grad_normed[keys - rows :] + mm(grad_query, self_q, NT)
    grad_normed = grad_normed + grad_before.astype(f32)
    part, gain_one = norm_back(tokens, inverse_one, gains[0], grad_normed)
    grad_input = grad_resid + part
    table_grad = table_gradient(near_sums, row_sums, chosen)
    small = jnp.stack((gain_one, gain_two, gain_three, table_grad), axis=1)
    grad_self = jnp.concatenate(
        (
            mm(normed_one, grad_query, TN),
            mm(normed_all, grad_key, turned),
            mm(normed_all, grad_value, turned),
            grad_self_out,
            jnp.pad(small, ((0, 0), (0, 124))),
        ),
        axis=1,
    ).astype(bf16)

    def owned(array):
        return lax.psum_scatter(array, BOTH, scatter_dimension=0, tiled=True).astype(f32)

    own_ffn_out = owned(grad_ffn_out)
    own_ffn_in = owned(grad_ffn_in)
    own_cross = owned(grad_cross)
    own_self = owned(grad_self)
    own_small = own_self[:, 4 * D : 4 * D + 4].T

    def projections(block):
        return jnp.stack([block[:, i * D : (i + 1) * D] for i in range(3)], axis=0)

    return (
        layer_out[None],
        grad_input[None],
        grad_encoder[None],
        projections(own_self),
        own_self[:, 3 * D : 4 * D],
        projections(own_cross),
        own_cross[:, 3 * D : 4 * D],
        own_ffn_in,
        own_ffn_out,
        own_small[:3],
        own_small[3],
    )


def solution(mesh):
    hidden = P("dp", "seq", None)
    rows_split = P(BOTH, None)
    stacked = P(None, BOTH, None)
    stream = P("dp", None)
    return jax.shard_map(
        on_device,
        mesh=mesh,
        in_specs=(
            hidden,
            hidden,
            stream,
            stream,
            stream,
            stacked,
            rows_split,
            stacked,
            rows_split,
            rows_split,
            rows_split,
            P(None, BOTH),
            P(BOTH),
            hidden,
        ),
        out_specs=(
            hidden,
            hidden,
            hidden,
            stacked,
            rows_split,
            stacked,
            rows_split,
            rows_split,
            rows_split,
            P(None, BOTH),
            P(BOTH),
        ),
        check_vma=False,
    )
```

time: 6360 us -> 897 us (0.14)
  waiting for transfers between devices: 4990 us -> 595 us
  local copies, waits for them, and re-layouts: 709 us -> 30.4 us
  matrix products: 388 us -> 116 us
  blocking collectives: 147 us -> 0 us
  Pallas kernels: 0 us -> 90.7 us
  other arithmetic: 98.5 us -> 32.2 us
    unnamed x16 -> x10, waiting for transfers between devices: 4990 us -> 160 us
    unnamed x228 -> x93, local copies, waits for them, and re-layouts: 308 us -> 18.9 us
    dot_general x59 -> x32, matrix products: 388 us -> 116 us  [the longest x30 115 us: mm(): return lax.dot_general(a, b, dims, preferred_element_type=f32)]
    reduce_scatter x2, waiting for transfers between devices: 0.04 us -> 219 us  [owned(): lax.psum_scatter(array, BOTH, scatter_dimension=0, tiled=True).astype(f32)]
    eq x5 -> x0, local copies, waits for them, and re-layouts: 187 us -> none  [code_onehot(): codes_block[:, :, None, :] == code_range[None, None, :, None]]
    all_gather x8 -> x4, waiting for transfers between devices: 0.03 us -> 119 us  [the longest x1 59.7 us: on_device(): all_self = lax.all_gather(block_self, BOTH, axis=0, tiled=True)]
    ppermute x0 -> x4, waiting for transfers between devices: none -> 96.6 us  [the longest x2 51.8 us: others_rows(): return lax.ppermute(rows, 'seq', [(0, 1)] if own_last else [(0, 1), (1, 0)])]
    pallas_call x0 -> x4, Pallas kernels: none -> 90.7 us  [the longest x2 47.2 us: attend_back(): pl.pallas_call(functools.partial(attend_back_body, rows, keys, causal, st...]
  transfers between devices with their start and end apart: 13 -> 12, of which waited for: 2 -> 11; matrix products, arithmetic and copies ran while one was open for 15% -> 14% of each run, Pallas kernels for 0% -> 5%
where the time goes in v1:
time: 897 us; the launch traced here: 887 us
  waiting for transfers between devices  595 us (66%)
  matrix products  116 us (13%)
  Pallas kernels  90.7 us (10%)
  other arithmetic  32.2 us (4%)
  local copies, waits for them, and re-layouts  30.4 us (3%)
  between operations  16.7 us (2%)
    reduce_scatter x2, waiting for transfers between devices, owned(): lax.psum_scatter(array, BOTH, scatter_dimension=0, tiled=True).astype(f32)  219 us
    unnamed x10, waiting for transfers between devices  160 us
    dot_general x30, matrix products, mm(): return lax.dot_general(a, b, dims, preferred_element_type=f32)  115 us
    all_gather x1, waiting for transfers between devices, on_device(): all_self = lax.all_gather(block_self, BOTH, axis=0, tiled=True)  59.7 us
    all_gather x1, waiting for transfers between devices, on_device(): mat_out = lax.all_gather(ffn_out.astype(bf16), BOTH, axis=0, tiled=True)  57.3 us
    ppermute x2, waiting for transfers between devices, others_rows(): return lax.ppermute(rows, 'seq', [(0, 1)] if own_last else [(0, 1), (1, 0)])  51.8 us
    pallas_call x2, Pallas kernels, attend_back(): pl.pallas_call(functools.partial(attend_back_body, rows, keys, causal, st...  47.2 us
    ppermute x2, waiting for transfers between devices, to_owners(): lax.ppermute(grads, 'seq', [(1, 0)] if own_last else [(0, 1), (1, 0)])  44.8 us
  transfers between devices with their start and end apart: 12, of which 11 were waited for; matrix products, arithmetic and copies ran while one was open for 14% of the time, Pallas kernels for 5%

profile of v1, /device:TPU:0, one launch (start us, length us, event | category | flops | bytes accessed | tf_op | source)
XLA Modules:
  0.0 887.3 jit_solution(11231561694633115305)
XLA Ops:
  14.0 4.9 collective-permute-start
  29.0 8.9 %collective-permute-done = bf16[512,768]{1,0:T(8,128)(2,1)S(1)} collective-permute-done((bf16[512,768]{1,0:T(8,128)(2,1)S(1)}, bf16[512,768]{1,0:T(8,128)(2,1)S(1)}, u32[]{:S(2)}, u32[]{:S(2)}) %collective-permute-start) | collective-permute-done | bytes 786464 | tf_op jit(solution)/shard_map/ppermute | solution.py:351
  38.1 43.0 %collective-permute-done.1 = bf16[1024,768]{1,0:T(8,128)(2,1)} collective-permute-done((bf16[1024,768]{1,0:T(8,128)(2,1)}, bf16[1024,768]{1,0:T(8,128)(2,1)}, u32[]{:S(2)}, u32[]{:S(2)}) %collective-permute-start.1) | collective-permute-done | bytes 1572896 | tf_op jit(solution)/shard_map/ppermute | solution.py:351
  81.0 6.5 convolution_convert_fusion.2.refs_2_
  87.6 6.5 convolution_convert_fusion.3.refs_1_
  94.1 59.7 %all-gather.5.cloned.1.call-done = bf16[768,3200]{1,0:T(8,128)(2,1)} async-done(((bf16[24,3200]{1,0:T(8,128)(2,1)}), bf16[768,3200]{1,0:T(8,128)(2,1)}) %all-gather.5.cloned.1.call-update) | async-done | bytes 4915216 | tf_op jit(solution)/shard_map/all_gather | solution.py:393
  167.7 20.6 %attend_causal.1 = (bf16[512,768]{1,0:T(8,128)(2,1)}, bf16[12,512,1024]{2,1,0:T(8,128)(2,1)}, f32[512,768]{1,0:T(8,128)}) custom-call(bf16[512,768]{1,0:T(8,128)(2,1)} %multiply_convert_fusion.4.refs_0_, bf16[1024,768]{1,0:T(8,128)(2,1)} %convolution_convert_fusion.5.refs_1_, bf16[1024,768]{1,0:T(8,128)(2,1)} %convolution_convert_fusion.4.refs_2_, ...), custom_call_target="tpu_custom_call" | custom-call | flops 6442450944 | bytes 12582912 | tf_op jit(solution)/shard_map/attend_causal/pallas_call | solution.py:149
  192.6 22.9 %attend_cross.1 = (bf16[512,768]{1,0:T(8,128)(2,1)}, bf16[12,512,2048]{2,1,0:T(8,128)(2,1)}, f32[512,768]{1,0:T(8,128)}) custom-call(bf16[512,768]{1,0:T(8,128)(2,1)} %multiply_convert_fusion.2.refs_0_, bf16[2048,768]{1,0:T(8,128)(2,1)} %convolution_convert_fusion.3.refs_1_, bf16[2048,768]{1,0:T(8,128)(2,1)} %convolution_convert_fusion.2.refs_2_, ...), custom_call_target="tpu_custom_call" | custom-call | flops 12884901888 | bytes 25165824 | tf_op jit(solution)/shard_map/attend_cross/pallas_call | solution.py:149
  219.3 8.0 multiply_convert_fusion
  227.3 57.3 %all-gather.11.cloned.1.call-done = bf16[3072,768]{1,0:T(8,128)(2,1)} async-done(((bf16[96,768]{1,0:T(8,128)(2,1)}), bf16[3072,768]{1,0:T(8,128)(2,1)}) %all-gather.11.cloned.1.call-update) | async-done | bytes 4718608 | tf_op jit(solution)/shard_map/all_gather | solution.py:396
  284.6 7.4 fusion.5
  299.7 27.1 %attend_cross_back.1 = (bf16[512,768]{1,0:T(8,128)(2,1)}, bf16[768,2048]{1,0:T(8,128)(2,1)}, bf16[768,2048]{1,0:T(8,128)(2,1)}) custom-call(bf16[512,768]{1,0:T(8,128)(2,1)} %multiply_convert_fusion.2.refs_0_, bf16[2048,768]{1,0:T(8,128)(2,1)} %convolution_convert_fusion.3.refs_1_, bf16[2048,768]{1,0:T(8,128)(2,1)} %convolution_convert_fusion.2.refs_2_, ...), custom_call_target="tpu_custom_call" | custom-call | flops 19327352832 | bytes 25165824 | tf_op jit(solution)/shard_map/attend_cross_back/pallas_call | solution.py:270
  331.1 3.0 convolution_convert_fusion.14.refs_6_
  334.1 20.1 %attend_causal_back.1 = (bf16[512,768]{1,0:T(8,128)(2,1)}, bf16[768,1024]{1,0:T(8,128)(2,1)}, bf16[768,1024]{1,0:T(8,128)(2,1)}, f32[6,4,256]{2,1,0:T(4,128)}, f32[6,4,128]{2,1,0:T(4,128)}) custom-call(bf16[512,768]{1,0:T(8,128)(2,1)} %multiply_convert_fusion.4.refs_0_, bf16[1024,768]{1,0:T(8,128)(2,1)} %convolution_convert_fusion.5.refs_1_, ...), custom_call_target="tpu_custom_call" | custom-call | flops 9663676416 | bytes 12582912 | tf_op jit(solution)/shard_map/attend_causal_back/pallas_call | solution.py:270
  356.4 3.4 fusion.26
  372.4 4.4 fusion.23
  378.7 13.8 %collective-permute-done.2 = bf16[512,768]{1,0:T(8,128)(2,1)} collective-permute-done((bf16[512,768]{1,0:T(8,128)(2,1)}, bf16[512,768]{1,0:T(8,128)(2,1)}, u32[]{:S(2)}, u32[]{:S(2)}) %collective-permute-start.2) | collective-permute-done | bytes 786464 | tf_op jit(solution)/shard_map/ppermute | solution.py:361
  392.5 3.8 fusion.20
  401.0 4.3 convolution_convert_fusion.6
  405.3 4.1 convolution_convert_fusion.7
  411.9 6.7 copy.158
  420.0 6.4 convolution_convert_fusion.1
  426.7 7.1 convolution_convert_fusion
  433.9 5.1 fusion.33
  439.0 4.1 convolution_add_fusion
  447.1 6.9 fusion.27
  455.6 31.0 %collective-permute-done.3 = bf16[1024,768]{1,0:T(8,128)(2,1)} collective-permute-done((bf16[1024,768]{1,0:T(8,128)(2,1)}, bf16[1024,768]{1,0:T(8,128)(2,1)}, u32[]{:S(2)}, u32[]{:S(2)}) %collective-permute-start.3) | collective-permute-done | bytes 1572896 | tf_op jit(solution)/shard_map/ppermute | solution.py:361
  486.6 3.4 fusion.6
  490.0 52.8 %all-reduce.9.cloned.1.call-done = bf16[768,3200]{0,1:T(8,128)(2,1)} async-done(((bf16[768,3200]{0,1:T(8,128)(2,1)}), bf16[768,3200]{0,1:T(8,128)(2,1)}) %all-reduce.9.cloned.1.call-update) | async-done | bytes 4915216
  547.1 107.3 %reduce-scatter.11.cloned.1.call-done = bf16[24,3072]{1,0:T(8,128)(2,1)} async-done(((bf16[768,3072]{1,0:T(8,128)(2,1)}), bf16[24,3072]{1,0:T(8,128)(2,1)}) %reduce-scatter.11.cloned.1.call-update) | async-done | bytes 147472
  657.1 109.7 %reduce-scatter.7.cloned.1.call-done = bf16[24,3072]{1,0:T(8,128)(2,1)} async-done(((bf16[768,3072]{1,0:T(8,128)(2,1)}), bf16[24,3072]{1,0:T(8,128)(2,1)}) %reduce-scatter.7.cloned.1.call-update) | async-done | bytes 147472 | tf_op jit(solution)/shard_map/reduce_scatter | solution.py:513
  769.2 109.2 %reduce-scatter.9.cloned.1.call-done = bf16[96,768]{1,0:T(8,128)(2,1)} async-done(((bf16[3072,768]{1,0:T(8,128)(2,1)}), bf16[96,768]{1,0:T(8,128)(2,1)}) %reduce-scatter.9.cloned.1.call-update) | async-done | bytes 147472 | tf_op jit(solution)/shard_map/reduce_scatter | solution.py:513
  (230 shorter events, 91.2 us)
Async XLA Ops:
  7.2 6.8 copy-start.2
  7.2 11.8 %copy-start.18 = (f32[96,768]{1,0:T(8,128)S(1)}, f32[96,768]{1,0:T(8,128)}, u32[]{:S(2)}) copy-start(f32[96,768]{1,0:T(8,128)} %param.25) | copy-start | bytes 884740
  7.2 73.8 %all-gather.7.cloned.1.call-start = ((), (), s32[]{:S(2)}) async-start(), calls=%async_computation.4 | async-start | bytes 4866048 | tf_op jit(solution)/shard_map/all_gather | solution.py:394
  9.2 10.8 %copy-start.26 = (s32[1,2]{1,0:T(1,128)S(1)}, s32[1,2]{1,0:T(1,128)}, u32[]{:S(2)}) copy-start(s32[1,2]{1,0:T(1,128)} %param.17) | copy-start | bytes 28
  9.2 11.4 %copy-start.27 = (s32[1,2]{1,0:T(1,128)S(1)}, s32[1,2]{1,0:T(1,128)}, u32[]{:S(2)}) copy-start(s32[1,2]{1,0:T(1,128)} %param.18) | copy-start | bytes 28
  9.9 14.5 %copy-start.28 = (s32[4]{0:T(128)S(1)}, s32[4]{0:T(128)}, u32[]{:S(2)}) copy-start(s32[4]{0:T(128)} %constant.94.clone) | copy-start | bytes 52
  9.9 143.8 %all-gather.5.cloned.1.call-start = ((), (), s32[]{:S(2)}) async-start(), calls=%async_computation.3 | async-start | bytes 5068800 | tf_op jit(solution)/shard_map/all_gather | solution.py:393
  13.2 206.1 %all-gather.9.cloned.1.call-start = ((), (), s32[]{:S(2)}) async-start(), calls=%async_computation.5 | async-start | bytes 4866048 | tf_op jit(solution)/shard_map/all_gather | solution.py:395
  13.9 270.7 %all-gather.11.cloned.1.call-start = ((), (), s32[]{:S(2)}) async-start(), calls=%async_computation.6 | async-start | bytes 4866048 | tf_op jit(solution)/shard_map/all_gather | solution.py:396
  14.0 23.9 %collective-permute-start = (bf16[512,768]{1,0:T(8,128)(2,1)S(1)}, bf16[512,768]{1,0:T(8,128)(2,1)S(1)}, u32[]{:S(2)}, u32[]{:S(2)}) collective-permute-start(bf16[512,768]{1,0:T(8,128)(2,1)S(1)} %bitcast.132), channel_id=1, source_target_pairs={{0,1},{2,3},{4,5},{6,7},{8,9},{10,11},{12,13},{14,15},{16,17},{18,... | collective-permute-start | bytes 2359304 | tf_op jit(solution)/shard_map/ppermute | solution.py:351
  18.9 8.5 copy-start.23
  18.9 62.1 %collective-permute-start.1 = (bf16[1024,768]{1,0:T(8,128)(2,1)}, bf16[1024,768]{1,0:T(8,128)(2,1)}, u32[]{:S(2)}, u32[]{:S(2)}) collective-permute-start(bf16[1024,768]{1,0:T(8,128)(2,1)} %bitcast.142), channel_id=1, source_target_pairs={{0,1},{1,0},{2,3},{3,2},{4,5},{5,4},{6,7},{7,6},{8,9},{9,8},{10,11... | collective-permute-start | bytes 4718600 | tf_op jit(solution)/shard_map/ppermute | solution.py:351
  19.7 523.1 %all-reduce.9.cloned.1.call-start = ((), (), s32[]{:S(2)}) async-start(), calls=%async_computation.10 | async-start | bytes 9830400
  158.2 6.2 copy-start.11
  158.2 6.2 copy-start.13
  164.3 26.4 %slice-start = ((s8[4718592]{0:T(1024)(128)(4,1)}), s8[4194304]{0:T(1024)(128)(4,1)S(1)}, s32[]{:S(2)}) async-start(s8[4718592]{0:T(1024)(128)(4,1)} %bitcast.133), calls=%async_computation.11 | async-start | bytes 8388608
  167.7 23.1 %slice-start.1 = ((s8[4718592]{0:T(1024)(128)(4,1)}), s8[524288]{0:T(1024)(128)(4,1)S(1)}, s32[]{:S(2)}) async-start(s8[4718592]{0:T(1024)(128)(4,1)} %bitcast.133), calls=%async_computation.12 | async-start | bytes 1048576
  190.8 136.0 %copy-start = (f32[512,768]{1,0:T(8,128)}, f32[512,768]{1,0:T(8,128)S(1)}, u32[]{:S(2)}) copy-start(f32[512,768]{1,0:T(8,128)S(1)} %get-tuple-element.158) | copy-start | bytes 4718596
  217.5 74.5 %copy-start.5 = (f32[512,768]{1,0:T(8,128)}, f32[512,768]{1,0:T(8,128)S(1)}, u32[]{:S(2)}) copy-start(f32[512,768]{1,0:T(8,128)S(1)} %get-tuple-element.160) | copy-start | bytes 4718596
  284.6 7.4 copy-start.29
  370.6 21.9 %collective-permute-start.2 = (bf16[512,768]{1,0:T(8,128)(2,1)}, bf16[512,768]{1,0:T(8,128)(2,1)}, u32[]{:S(2)}, u32[]{:S(2)}) collective-permute-start(bf16[512,768]{1,0:T(8,128)(2,1)} %slice.336), channel_id=1, source_target_pairs={{1,0},{3,2},{5,4},{7,6},{9,8},{11,10},{13,12},{15,14},{17,16},{19,... | collective-permute-start | bytes 2359304 | tf_op jit(solution)/shard_map/ppermute | solution.py:361
  372.4 20.1 %copy-start.21 = (f32[1024,768]{1,0:T(8,128)S(1)}, f32[1024,768]{1,0:T(8,128)}, u32[]{:S(2)}) copy-start(f32[1024,768]{1,0:T(8,128)} %copy-done.20) | copy-start | bytes 9437188
  376.8 15.7 %copy-start.3 = (bf16[1,512,768]{2,1,0:T(8,128)(2,1)S(1)}, bf16[1,512,768]{2,1,0:T(8,128)(2,1)}, u32[]{:S(2)}) copy-start(bf16[1,512,768]{2,1,0:T(8,128)(2,1)} %param.15) | copy-start | bytes 2359300
  376.8 15.7 %copy-start.34 = (bf16[512,768]{1,0:T(8,128)(2,1)S(1)}, bf16[512,768]{1,0:T(8,128)(2,1)}, u32[]{:S(2)}) copy-start(bf16[512,768]{1,0:T(8,128)(2,1)} %get-tuple-element.34) | copy-start | bytes 2359300
  397.0 257.4 %reduce-scatter.11.cloned.1.call-start = ((), (), s32[]{:S(2)}) async-start(), calls=%async_computation.9 | async-start | bytes 4866048
  418.6 348.2 %reduce-scatter.7.cloned.1.call-start = ((), (), s32[]{:S(2)}) async-start(), calls=%async_computation.7 | async-start | bytes 4866048 | tf_op jit(solution)/shard_map/reduce_scatter | solution.py:513
  426.4 452.0 %reduce-scatter.9.cloned.1.call-start = ((), (), s32[]{:S(2)}) async-start(), calls=%async_computation.8 | async-start | bytes 4866048 | tf_op jit(solution)/shard_map/reduce_scatter | solution.py:513
  447.1 39.5 %collective-permute-start.3 = (bf16[1024,768]{1,0:T(8,128)(2,1)}, bf16[1024,768]{1,0:T(8,128)(2,1)}, u32[]{:S(2)}, u32[]{:S(2)}) collective-permute-start(bf16[1024,768]{1,0:T(8,128)(2,1)} %slice.335), channel_id=1, source_target_pairs={{0,1},{1,0},{2,3},{3,2},{4,5},{5,4},{6,7},{7,6},{8,9},{9,8},{10,11... | collective-permute-start | bytes 4718600 | tf_op jit(solution)/shard_map/ppermute | solution.py:361
  447.1 6.9 copy-start.4
  447.1 6.9 copy-start.9
  447.1 39.5 %copy-start.8 = (f32[2048,768]{1,0:T(8,128)S(1)}, f32[2048,768]{1,0:T(8,128)}, u32[]{:S(2)}) copy-start(f32[2048,768]{1,0:T(8,128)} %copy-done.7) | copy-start | bytes 18874372
  546.6 109.2 %copy-start.25 = (f32[4,24]{1,0:T(4,128)}, f32[4,24]{1,0:T(4,128)S(1)}, u32[]{:S(2)}) copy-start(f32[4,24]{1,0:T(4,128)S(1)} %slice_bitcast_fusion.13) | copy-start | bytes 1156
  (20 other events, 62.3 us)
Sparse Core Ops, SparseCore 0:
  11.5 66.8 all-gather.6
  81.9 71.8 all-gather.4
  156.7 62.5 all-gather.8
  222.1 62.4 all-gather.10
  397.1 145.6 all-reduce.8
  548.2 106.1 reduce-scatter.10
  660.7 106.0 reduce-scatter.6
  772.3 106.0 reduce-scatter.8

commit v2 on v1

--- a/solution.py
+++ b/solution.py
@@ -25,6 +25,7 @@
 NN = (((1,), (0,)), ((), ()))
 TN = (((0,), (0,)), ((), ()))
 BOTH = ("dp", "seq")
+MESH = pl.DeviceIdType.MESH
 
 
 def bucket_of(distance):
@@ -282,6 +283,355 @@
     )(*operands)
 
 
+def place_here():
+    index = lax.axis_index("dp")
+    return index // 4, (index // 2) % 2, index % 2, lax.axis_index("seq")
+
+
+def block_of(z, x, core, y):
+    return ((z * 2 + x) * 2 + core) * 2 + y
+
+
+def device_of(z, x, core, y):
+    return ((z * 2 + x) * 2 + core, y)
+
+
+def greet_neighbours(z, x, core, y):
+    barrier = pltpu.get_barrier_semaphore()
+
+    def greet(device):
+        pl.semaphore_signal(barrier, inc=1, device_id=device, device_id_type=MESH)
+
+    greet(device_of(z, x, 1 - core, y))
+    greet(device_of(z, 1 - x, core, y))
+    greet(device_of(z, x, core, 1 - y))
+
+    @pl.when(z > 0)
+    def _():
+        greet(device_of(z - 1, x, core, y))
+
+    @pl.when(z < 3)
+    def _():
+        greet(device_of(z + 1, x, core, y))
+
+    pl.semaphore_wait(barrier, 4 + ((z + 1) // 2) % 2)
+
+
+def gather_body(count, *refs):
+    sources, wholes = refs[:count], refs[count : 2 * count]
+    own_sems, up_sems, down_sems, side_sems, turn_sems, mate_sems, recv_sems = refs[2 * count :]
+    z, x, core, y = place_here()
+    mate = device_of(z, x, 1 - core, y)
+    me = block_of(z, x, core, y)
+    greet_neighbours(z, x, core, y)
+
+    def near(which, side, turn):
+        return ((x + side) % 2, (y + turn) % 2) if which == 0 else ((x + turn) % 2, (y + side) % 2)
+
+    def send(which, source, block, send_sem, device):
+        return pltpu.make_async_remote_copy(
+            src_ref=source,
+            dst_ref=wholes[which].at[block],
+            send_sem=send_sem,
+            recv_sem=recv_sems.at[which, block],
+            device_id=device,
+            device_id_type=MESH,
+        )
+
+    def copies(which, far, up, side, turn, source=None):
+        at_z = z + far if up else z - far
+        bx, by = near(which, side, turn)
+        block = block_of(at_z, bx, core, by)
+        source = wholes[which].at[block] if source is None else source
+        slot = (2 * far + (1 if up else 0)) if far else 0
+        slot = max(slot - 1, 0)
+        out = [(None, send(which, source, block, mate_sems.at[which, (side * 2 + turn) * 7 + slot], mate))]
+        if turn == 0:
+            tx, ty = near(which, 0, 1)
+            out.append(
+                (None, send(which, source, block, turn_sems.at[which, side * 7 + slot], device_of(z, tx, core, ty)))
+            )
+            if side == 0:
+                sx, sy = near(which, 1, 0)
+                out.append((None, send(which, source, block, side_sems.at[which, slot], device_of(z, sx, core, sy))))
+                if far == 0 or not up:
+                    out.append(
+                        (z < 3, send(which, source, block, up_sems.at[which, far], device_of(z + 1, x, core, y)))
+                    )
+                if far == 0 or up:
+                    out.append(
+                        (z > 0, send(which, source, block, down_sems.at[which, far], device_of(z - 1, x, core, y)))
+                    )
+        return block, out
+
+    def when(condition, action):
+        if condition is None:
+            action()
+        else:
+            pl.when(condition)(action)
+
+    def exists(far, up):
+        if far == 0:
+            return None
+        return z + far < 4 if up else z - far >= 0
+
+    def onwards(which, far, up, side, turn, source=None):
+        def run():
+            block, out = copies(which, far, up, side, turn, source)
+            if source is None:
+                pltpu.make_async_copy(wholes[which].at[block], wholes[which].at[block], recv_sems.at[which, block]).wait()
+            for condition, copy in reversed(out):
+                when(condition, copy.start)
+
+        when(exists(far, up), run)
+
+    own = [
+        pltpu.make_async_copy(sources[i], wholes[i].at[me], own_sems.at[i]) for i in range(count)
+    ]
+    for which in range(count):
+        onwards(which, 0, True, 0, 0, sources[which])
+    for copy in own:
+        copy.start()
+    waves = [[] for _ in range(6)]
+    for side in (0, 1):
+        for turn in (0, 1):
+            for far in range(4):
+                for up in (False, True):
+                    if far == 0 and (up or (side == 0 and turn == 0)):
+                        continue
+                    waves[far + side + turn].append((far, up, side, turn))
+    for wave in waves:
+        for far, up, side, turn in wave:
+            for which in range(count):
+                onwards(which, far, up, side, turn)
+    for side in (0, 1):
+        for turn in (0, 1):
+            for far in range(4):
+                for up in (False, True):
+                    if far == 0 and up:
+                        continue
+                    for which in range(count):
+
+                        def finish(which=which, far=far, up=up, side=side, turn=turn):
+                            at_z = z + far if up else z - far
+                            bx, by = near(which, side, turn)
+                            block = block_of(at_z, bx, 1 - core, by)
+                            whole = wholes[which].at[block]
+                            pltpu.make_async_copy(whole, whole, recv_sems.at[which, block]).wait()
+                            source = sources[which] if (far, side, turn) == (0, 0, 0) else None
+                            _, out = copies(which, far, up, side, turn, source)
+                            for condition, copy in out:
+                                when(condition, copy.wait_send)
+
+                        when(exists(far, up), finish)
+    for copy in own:
+        copy.wait()
+
+
+def gather_blocks(*blocks):
+    count = len(blocks)
+    any_space = pl.BlockSpec(memory_space=pl.ANY)
+    dma = pltpu.SemaphoreType.DMA
+    return pl.pallas_call(
+        functools.partial(gather_body, count),
+        in_specs=[any_space] * count,
+        out_specs=[any_space] * count,
+        out_shape=[jax.ShapeDtypeStruct((32, *block.shape), block.dtype) for block in blocks],
+        scratch_shapes=[
+            dma((count,)),
+            dma((count, 4)),
+            dma((count, 4)),
+            dma((count, 7)),
+            dma((count, 14)),
+            dma((count, 28)),
+            dma((count, 32)),
+        ],
+        compiler_params=pltpu.CompilerParams(collective_id=0, has_side_effects=True),
+        name="gather_blocks",
+    )(*blocks)
+
+
+def scatter_body(count, *refs):
+    parts, outs = refs[:count], refs[count : 2 * count]
+    refs = refs[2 * count :]
+    sums, mate_in, first_in, second_in, line_in = (
+        refs[i * count : (i + 1) * count] for i in range(5)
+    )
+    local_sems, mate_sems, first_sems, second_sems, line_sems = refs[5 * count : 5 * count + 5]
+    mate_recv, first_recv, second_recv, line_recv = refs[5 * count + 5 :]
+    z, x, core, y = place_here()
+    greet_neighbours(z, x, core, y)
+    half = z // 2
+    order = (3 - 3 * half, 2 - half, 1 - z + 4 * half, z)
+
+    def near(which, first, second):
+        return ((x + second) % 2, (y + first) % 2) if which == 0 else ((x + first) % 2, (y + second) % 2)
+
+    def cell(which, i, first, second):
+        bx, by = near(which, first, second)
+        return (order[i] * 2 + bx) * 2 + by
+
+    def local(which, i, first, second):
+        bx, by = near(which, first, second)
+        here = cell(which, i, first, second)
+        return pltpu.make_async_copy(
+            parts[which].at[block_of(order[i], bx, core, by)],
+            sums[which].at[here],
+            local_sems.at[which, here],
+        )
+
+    def to_mate(which, i, first, second):
+        bx, by = near(which, first, second)
+        here = cell(which, i, first, second)
+        return pltpu.make_async_remote_copy(
+            src_ref=parts[which].at[block_of(order[i], bx, 1 - core, by)],
+            dst_ref=mate_in[which].at[here],
+            send_sem=mate_sems.at[which, here],
+            recv_sem=mate_recv.at[which, here],
+            device_id=device_of(z, x, 1 - core, y),
+            device_id_type=MESH,
+        )
+
+    def to_first(which, i, second):
+        bx, by = near(which, 1, 0)
+        return pltpu.make_async_remote_copy(
+            src_ref=sums[which].at[cell(which, i, 1, second)],
+            dst_ref=first_in[which].at[2 * i + second],
+            send_sem=first_sems.at[which, 2 * i + second],
+            recv_sem=first_recv.at[which, 2 * i + second],
+            device_id=device_of(z, bx, core, by),
+            device_id_type=MESH,
+        )
+
+    def to_second(which, i):
+        bx, by = near(which, 0, 1)
+        return pltpu.make_async_remote_copy(
+            src_ref=sums[which].at[cell(which, i, 0, 1)],
+            dst_ref=second_in[which].at[i],
+            send_sem=second_sems.at[which, i],
+            recv_sem=second_recv.at[which, i],
+            device_id=device_of(z, bx, core, by),
+            device_id_type=MESH,
+        )
+
+    def along_line(which, i):
+        step = 1 - 2 * half if i < 2 else 1 - 2 * (z % 2)
+        came = (1 - step) // 2
+        return came, pltpu.make_async_remote_copy(
+            src_ref=sums[which].at[cell(which, i, 0, 0)],
+            dst_ref=line_in[which].at[came * 4 + order[i]],
+            send_sem=line_sems.at[which, i],
+            recv_sem=line_recv.at[which, came * 4 + order[i]],
+            device_id=device_of(z + step, x, core, y),
+            device_id_type=MESH,
+        )
+
+    def arrived(buffer, sem):
+        pltpu.make_async_copy(buffer, buffer, sem).wait()
+
+    def wide(ref, index):
+        return ref[index].astype(f32)
+
+    every = [(1, 1), (1, 0), (0, 1), (0, 0)]
+    for first, second in every:
+        for i in range(4):
+            for which in range(count):
+                to_mate(which, i, first, second).start()
+                local(which, i, first, second).start()
+
+    def chip_sum(which, i, first, second):
+        here = cell(which, i, first, second)
+        local(which, i, first, second).wait()
+        arrived(mate_in[which].at[here], mate_recv.at[which, here])
+        return here, wide(sums[which], here) + wide(mate_in[which], here)
+
+    for second in (1, 0):
+        for i in range(4):
+            for which in range(count):
+                here, total = chip_sum(which, i, 1, second)
+                sums[which][here] = total.astype(bf16)
+                to_first(which, i, second).start()
+    for i in range(4):
+        for which in range(count):
+            here, total = chip_sum(which, i, 0, 1)
+            arrived(first_in[which].at[2 * i + 1], first_recv.at[which, 2 * i + 1])
+            sums[which][here] = (total + wide(first_in[which], 2 * i + 1)).astype(bf16)
+            to_second(which, i).start()
+    middle = (z + 1) // 2 == 1
+    for i in range(4):
+        for which in range(count):
+            here, total = chip_sum(which, i, 0, 0)
+            arrived(first_in[which].at[2 * i], first_recv.at[which, 2 * i])
+            arrived(second_in[which].at[i], second_recv.at[which, i])
+            total = total + wide(first_in[which], 2 * i) + wide(second_in[which], i)
+            if i < 3:
+                sums[which][here] = total.astype(bf16)
+                came, copy = along_line(which, i)
+                slot = came * 4 + order[i]
+
+                @pl.when(middle)
+                def _():
+                    arrived(line_in[which].at[slot], line_recv.at[which, slot])
+                    sums[which][here] = (wide(sums[which], here) + wide(line_in[which], slot)).astype(bf16)
+
+                copy.start()
+            else:
+                outs[which][...] = total
+    for which in range(count):
+        for came, there in ((0, z > 0), (1, z < 3)):
+            slot = came * 4 + z
+
+            @pl.when(there)
+            def _():
+                arrived(line_in[which].at[slot], line_recv.at[which, slot])
+                outs[which][...] += wide(line_in[which], slot)
+
+    for which in range(count):
+        for i in range(4):
+            for first, second in every:
+                to_mate(which, i, first, second).wait_send()
+            for second in (0, 1):
+                to_first(which, i, second).wait_send()
+            to_second(which, i).wait_send()
+            if i < 3:
+                along_line(which, i)[1].wait_send()
+
+
+def scatter_blocks(*parts):
+    count = len(parts)
+    dma = pltpu.SemaphoreType.DMA
+
+    def buffers(slots):
+        return [pltpu.VMEM((slots, *part.shape[1:]), part.dtype) for part in parts]
+
+    return pl.pallas_call(
+        functools.partial(scatter_body, count),
+        in_specs=[pl.BlockSpec(memory_space=pl.ANY)] * count,
+        out_specs=[pl.BlockSpec(memory_space=pltpu.VMEM)] * count,
+        out_shape=[jax.ShapeDtypeStruct(part.shape[1:], f32) for part in parts],
+        scratch_shapes=buffers(16)
+        + buffers(16)
+        + buffers(8)
+        + buffers(4)
+        + buffers(8)
+        + [
+            dma((count, 16)),
+            dma((count, 16)),
+            dma((count, 8)),
+            dma((count, 4)),
+            dma((count, 3)),
+            dma((count, 16)),
+            dma((count, 8)),
+            dma((count, 4)),
+            dma((count, 8)),
+        ],
+        compiler_params=pltpu.CompilerParams(
+            collective_id=1, has_side_effects=True, vmem_limit_bytes=48 << 20
+        ),
+        name="scatter_blocks",
+    )(*parts)
+
+
 def pair_of(positions, lengths):
     return (positions >= lengths[0]).astype(jnp.int32) + (
         positions >= lengths[0] + lengths[1]
@@ -390,8 +740,14 @@
     block_cross = jnp.concatenate(
         (cross_proj[0], cross_proj[1], cross_proj[2], cross_out), axis=1
     ).astype(bf16)
-    all_self = lax.all_gather(block_self, BOTH, axis=0, tiled=True)
-    all_cross = lax.all_gather(block_cross, BOTH, axis=0, tiled=True)
+    own_kernels = (lax.axis_size("dp"), lax.axis_size("seq")) == (16, 2)
+    if own_kernels:
+        all_self, all_cross = gather_blocks(block_self, block_cross)
+        all_self = all_self.reshape(-1, all_self.shape[2])
+        all_cross = all_cross.reshape(-1, all_cross.shape[2])
+    else:
+        all_self = lax.all_gather(block_self, BOTH, axis=0, tiled=True)
+        all_cross = lax.all_gather(block_cross, BOTH, axis=0, tiled=True)
     mat_in = lax.all_gather(ffn_in.astype(bf16), BOTH, axis=0, tiled=True)
     mat_out = lax.all_gather(ffn_out.astype(bf16), BOTH, axis=0, tiled=True)
     self_q, self_k, self_v, out_self = (all_self[:, i * D : (i + 1) * D] for i in range(4))
@@ -514,8 +870,14 @@
 
     own_ffn_out = owned(grad_ffn_out)
     own_ffn_in = owned(grad_ffn_in)
-    own_cross = owned(grad_cross)
-    own_self = owned(grad_self)
+    if own_kernels:
+        own_self, own_cross = scatter_blocks(
+            grad_self.reshape(-1, shard, grad_self.shape[1]),
+            grad_cross.reshape(-1, shard, grad_cross.shape[1]),
+        )
+    else:
+        own_cross = owned(grad_cross)
+        own_self = owned(grad_self)
     own_small = own_self[:, 4 * D : 4 * D + 4].T
 
     def projections(block):

time: 897 us -> 482 us (0.54)
  waiting for transfers between devices: 595 us -> 20.2 us
  Pallas kernels: 90.7 us -> 264 us
  matrix products: 116 us -> 103 us
    reduce_scatter x2, waiting for transfers between devices: 219 us -> 20.1 us  [owned(): lax.psum_scatter(array, BOTH, scatter_dimension=0, tiled=True).astype(f32)]
    pallas_call x0 -> x2, Pallas kernels: none -> 173 us  [the longest x1 102 us: gather_blocks(): pl.pallas_call(functools.partial(gather_body, count), in_specs=[any_space...]
    unnamed x10 -> x4, waiting for transfers between devices: 160 us -> 0.07 us
    all_gather x2 -> x0, waiting for transfers between devices: 59.7 us -> none  [the longest x1 59.7 us: on_device(): all_self = lax.all_gather(block_self, BOTH, axis=0, tiled=True)]
    all_gather x1, waiting for transfers between devices: 57.3 us -> 0.01 us  [on_device(): mat_out = lax.all_gather(ffn_out.astype(bf16), BOTH, axis=0, tiled=True)]
    ppermute x2, waiting for transfers between devices: 51.8 us -> 0.01 us  [others_rows(): return lax.ppermute(rows, 'seq', [(0, 1)] if own_last else [(0, 1), (1, 0)])]
    ppermute x2, waiting for transfers between devices: 44.8 us -> 0.01 us  [to_owners(): lax.ppermute(grads, 'seq', [(1, 0)] if own_last else [(0, 1), (1, 0)])]
    dot_general x30, matrix products: 115 us -> 103 us  [mm(): return lax.dot_general(a, b, dims, preferred_element_type=f32)]
  transfers between devices with their start and end apart: 12 -> 8, of which waited for: 11 -> 1; matrix products, arithmetic and copies ran while one was open for 14% -> 28% of each run, Pallas kernels for 5% -> 56%
where the time goes in v2:
time: 482 us; the launch traced here: 475 us
  Pallas kernels  264 us (55%)
  matrix products  103 us (21%)
  local copies, waits for them, and re-layouts  31.4 us (7%)
  other arithmetic  28.3 us (6%)
  waiting for transfers between devices  20.2 us (4%)
  between operations  16.4 us (3%)
  starting transfers between devices  11.4 us (2%)
    dot_general x30, matrix products, mm(): return lax.dot_general(a, b, dims, preferred_element_type=f32)  103 us
    pallas_call x1, Pallas kernels, gather_blocks(): pl.pallas_call(functools.partial(gather_body, count), in_specs=[any_space...  102 us
    pallas_call x1, Pallas kernels, scatter_blocks(): pl.pallas_call(functools.partial(scatter_body, count), in_specs=[pl.Block...  70.5 us
    pallas_call x2, Pallas kernels, attend_back(): pl.pallas_call(functools.partial(attend_back_body, rows, keys, causal, st...  47.6 us
    pallas_call x2, Pallas kernels, attend(): pl.pallas_call(functools.partial(attend_body, rows, keys, causal, step),...  43.7 us
    reduce_scatter x2, waiting for transfers between devices, owned(): lax.psum_scatter(array, BOTH, scatter_dimension=0, tiled=True).astype(f32)  20.1 us
    unnamed x132, local copies, waits for them, and re-layouts  18 us
  transfers between devices with their start and end apart: 8, of which 1 were waited for; matrix products, arithmetic and copies ran while one was open for 28% of the time, Pallas kernels for 56%

profile of v2, /device:TPU:0, one launch (start us, length us, event | category | flops | bytes accessed | tf_op | source)
XLA Modules:
  0.0 475.0 jit_solution(15093966530638507214)
XLA Ops:
  9.1 4.9 %collective-permute-start = (bf16[512,768]{1,0:T(8,128)(2,1)}, bf16[512,768]{1,0:T(8,128)(2,1)S(1)}, u32[]{:S(2)}, u32[]{:S(2)}) collective-permute-start(bf16[512,768]{1,0:T(8,128)(2,1)} %bitcast.139), channel_id=1, source_target_pairs={{0,1},{2,3},{4,5},{6,7},{8,9},{10,11},{12,13},{14,15},{16,17},{18,... | collective-permute-start | bytes 2359304 | tf_op jit(solution)/shard_map/ppermute | solution.py:701
  17.8 102.3 %gather_blocks.1 = (bf16[32,24,3200]{2,1,0:T(8,128)(2,1)}, bf16[32,24,3072]{2,1,0:T(8,128)(2,1)}) custom-call(bf16[24,3200]{1,0:T(8,128)(2,1)} %copy-done.20, bf16[24,3072]{1,0:T(8,128)(2,1)} %pad_maximum_fusion.7.refs_1_), custom_call_target="tpu_custom_call" | custom-call | tf_op jit(solution)/shard_map/gather_blocks/pallas_call | solution.py:435
  134.2 2.6 convolution_convert_fusion.4.refs_2_
  136.8 2.6 convolution_convert_fusion.5.refs_1_
  143.1 20.6 %attend_causal.1 = (bf16[512,768]{1,0:T(8,128)(2,1)}, bf16[12,512,1024]{2,1,0:T(8,128)(2,1)}, f32[512,768]{1,0:T(8,128)}) custom-call(bf16[512,768]{1,0:T(8,128)(2,1)} %multiply_convert_fusion.4.refs_0_, bf16[1024,768]{1,0:T(8,128)(2,1)} %convolution_convert_fusion.5.refs_1_, bf16[1024,768]{1,0:T(8,128)(2,1)} %convolution_convert_fusion.4.refs_2_, ...), custom_call_target="tpu_custom_call" | custom-call | flops 6442450944 | bytes 12582912 | tf_op jit(solution)/shard_map/attend_causal/pallas_call | solution.py:150
  166.2 3.6 multiply_convert_fusion.2.refs_0_
  169.8 6.2 %convolution_convert_fusion.2.refs_2_ = bf16[2048,768]{1,0:T(8,128)(2,1)} fusion(bf16[768,3072]{1,0:T(8,128)(2,1)} %bitcast.151, bf16[1024,768]{1,0:T(8,128)(2,1)} %collective-permute-done.1, bf16[1024,768]{1,0:T(8,128)(2,1)S(1)} %bitcast.184), kind=kOutput, calls=%fused_computation.13 | convolution fusion | flops 2423783424 | bytes 7471104 | tf_op jit(solution)/shard_map/dot_general | solution.py:37
  176.0 5.7 %convolution_convert_fusion.3.refs_1_ = bf16[2048,768]{1,0:T(8,128)(2,1)} fusion(bf16[768,3072]{1,0:T(8,128)(2,1)S(1)} %bitcast.156, bf16[1024,768]{1,0:T(8,128)(2,1)} %collective-permute-done.1, bf16[1024,768]{1,0:T(8,128)(2,1)S(1)} %bitcast.185), kind=kOutput, calls=%fused_computation.14 | convolution fusion | flops 2423783424 | bytes 7471104 | tf_op jit(solution)/shard_map/dot_general | solution.py:37
  181.7 23.1 %attend_cross.1 = (bf16[512,768]{1,0:T(8,128)(2,1)}, bf16[12,512,2048]{2,1,0:T(8,128)(2,1)}, f32[512,768]{1,0:T(8,128)}) custom-call(bf16[512,768]{1,0:T(8,128)(2,1)} %multiply_convert_fusion.2.refs_0_, bf16[2048,768]{1,0:T(8,128)(2,1)} %convolution_convert_fusion.3.refs_1_, bf16[2048,768]{1,0:T(8,128)(2,1)} %convolution_convert_fusion.2.refs_2_, ...), custom_call_target="tpu_custom_call" | custom-call | flops 12884901888 | bytes 25165824 | tf_op jit(solution)/shard_map/attend_cross/pallas_call | solution.py:150
  204.8 3.1 multiply_reduce_fusion.4
  208.0 8.2 %multiply_convert_fusion = (bf16[512,3072]{1,0:T(8,128)(2,1)}, f32[512,3072]{1,0:T(8,128)}) fusion(bf16[768,3072]{1,0:T(8,128)(2,1)} %all-gather.3.cloned.1.call-done, f32[512,768]{1,0:T(8,128)} %get-tuple-element.147, f32[768]{0:T(1024)S(1)} %get-tuple-element.108, f32[512]{0:T(512)S(1)} %add_rsqrt_fusion), kind=kOutput, calls=%fused_computation.7 | convolution fusion | flops 2424963072 | bytes 15733760 | tf_op jit(solution)/shard_map/dot_general | solution.py:37
  216.2 6.9 %fusion.5 = bf16[512,3072]{1,0:T(8,128)(2,1)S(1)} fusion(f32[512,3072]{1,0:T(8,128)} %get-tuple-element.149, bf16[3072,768]{1,0:T(8,128)(2,1)} %all-gather.5.cloned.1.call-done, bf16[1,512,768]{2,1,0:T(8,128)(2,1)} %param.28), kind=kOutput, calls=%fused_computation.6 | convolution fusion | flops 2431647744 | bytes 14942208 | tf_op jit(solution)/shard_map/dot_general | solution.py:37
  224.8 4.5 convolution_convert_fusion.1
  229.5 6.7 %multiply_reduce_fusion = (bf16[768]{0:T(1024)(128)(2,1)S(1)}, f32[512]{0:T(512)S(1)}, f32[512,768]{1,0:T(8,128)S(1)}) fusion(f32[512,768]{1,0:T(8,128)} %get-tuple-element.147, f32[512]{0:T(512)S(1)} %add_rsqrt_fusion, f32[768]{0:T(1024)S(1)} %get-tuple-element.108, bf16[512,3072]{1,0:T(8,128)(2,1)} %copy-done.50, ...), kind=kOutput, calls=%fused_computation.46 | convolution fusion | flops 2418277120 | bytes 11018752 | tf_op jit(solution)/shard_map/dot_general | solution.py:37
  236.6 3.5 convolution_convert_fusion.15.refs_6_
  240.2 27.6 %attend_cross_back.1 = (bf16[512,768]{1,0:T(8,128)(2,1)}, bf16[768,2048]{1,0:T(8,128)(2,1)}, bf16[768,2048]{1,0:T(8,128)(2,1)}) custom-call(bf16[512,768]{1,0:T(8,128)(2,1)} %multiply_convert_fusion.2.refs_0_, bf16[2048,768]{1,0:T(8,128)(2,1)} %convolution_convert_fusion.3.refs_1_, bf16[2048,768]{1,0:T(8,128)(2,1)} %convolution_convert_fusion.2.refs_2_, ...), custom_call_target="tpu_custom_call" | custom-call | flops 19327352832 | bytes 25165824 | tf_op jit(solution)/shard_map/attend_cross_back/pallas_call | solution.py:271
  272.2 3.0 convolution_convert_fusion.14.refs_6_
  275.2 20.0 %attend_causal_back.1 = (bf16[512,768]{1,0:T(8,128)(2,1)}, bf16[768,1024]{1,0:T(8,128)(2,1)}, bf16[768,1024]{1,0:T(8,128)(2,1)}, f32[6,4,256]{2,1,0:T(4,128)}, f32[6,4,128]{2,1,0:T(4,128)}) custom-call(bf16[512,768]{1,0:T(8,128)(2,1)} %multiply_convert_fusion.4.refs_0_, bf16[1024,768]{1,0:T(8,128)(2,1)} %convolution_convert_fusion.5.refs_1_, ...), custom_call_target="tpu_custom_call" | custom-call | flops 9663676416 | bytes 12582912 | tf_op jit(solution)/shard_map/attend_causal_back/pallas_call | solution.py:271
  297.8 3.4 fusion.40
  301.3 3.0 convolution_add_fusion.1
  308.4 2.8 fusion.30
  311.3 2.8 convolution_add_fusion
  315.4 4.8 %collective-permute-start.3 = (bf16[1024,768]{1,0:T(8,128)(2,1)}, bf16[1024,768]{1,0:T(8,128)(2,1)}, u32[]{:S(2)}, u32[]{:S(2)}) collective-permute-start(bf16[1024,768]{1,0:T(8,128)(2,1)} %slice.329), channel_id=1, source_target_pairs={{0,1},{1,0},{2,3},{3,2},{4,5},{5,4},{6,7},{7,6},{8,9},{9,8},{10,11... | collective-permute-start | bytes 4718600 | tf_op jit(solution)/shard_map/ppermute | solution.py:711
  327.7 4.5 convolution_convert_fusion
  340.9 4.2 convolution_convert_fusion.8
  345.1 4.1 convolution_convert_fusion.7
  349.3 3.0 pad_maximum_fusion.refs_1_
  353.4 3.5 fusion.24
  357.0 3.8 fusion.20
  364.2 70.5 %scatter_blocks.1 = (f32[24,3200]{1,0:T(8,128)S(1)}, f32[24,3072]{1,0:T(8,128)S(1)}) custom-call(bf16[32,24,3200]{2,1,0:T(8,128)(2,1)} %constant_dynamic-update-slice_fusion.1.refs_0_, bf16[32,24,3072]{2,1,0:T(8,128)(2,1)S(1)} %copy-done), custom_call_target="tpu_custom_call" | custom-call | tf_op jit(solution)/shard_map/scatter_blocks/pallas_call | solution.py:607
  440.4 4.3 fusion.6
  446.4 20.1 %reduce-scatter.5.cloned.1.call-done = bf16[96,768]{1,0:T(8,128)(2,1)} async-done(((bf16[3072,768]{1,0:T(8,128)(2,1)}), bf16[96,768]{1,0:T(8,128)(2,1)}) %reduce-scatter.5.cloned.1.call-update) | async-done | bytes 147472 | tf_op jit(solution)/shard_map/reduce_scatter | solution.py:869
  (254 shorter events, 68.5 us)
Async XLA Ops:
  7.2 9.7 %copy-start.34 = (f32[3,24]{1,0:T(4,128)S(1)}, f32[3,24]{1,0:T(4,128)}, u32[]{:S(2)}) copy-start(f32[3,24]{1,0:T(4,128)} %param.26) | copy-start | bytes 868
  7.2 9.7 %copy-start.40 = (f32[24]{0:T(128)S(1)}, f32[24]{0:T(128)}, u32[]{:S(2)}) copy-start(f32[24]{0:T(128)} %param.27) | copy-start | bytes 292
  7.2 9.8 %copy-start.21 = (f32[3,24,768]{2,1,0:T(8,128)S(1)}, f32[3,24,768]{2,1,0:T(8,128)}, u32[]{:S(2)}) copy-start(f32[3,24,768]{2,1,0:T(8,128)} %param.22) | copy-start | bytes 663556
  7.2 9.8 %copy-start.24 = (f32[24,768]{1,0:T(8,128)S(1)}, f32[24,768]{1,0:T(8,128)}, u32[]{:S(2)}) copy-start(f32[24,768]{1,0:T(8,128)} %param.23) | copy-start | bytes 221188
  7.2 9.8 %copy-start.25 = (f32[24,768]{1,0:T(8,128)S(1)}, f32[24,768]{1,0:T(8,128)}, u32[]{:S(2)}) copy-start(f32[24,768]{1,0:T(8,128)} %param.21) | copy-start | bytes 221188
  7.2 200.8 %all-gather.3.cloned.1.call-start = ((), (), s32[]{:S(2)}) async-start(), calls=%async_computation.2 | async-start | bytes 4866048 | tf_op jit(solution)/shard_map/all_gather | solution.py:751
  9.1 207.2 %all-gather.5.cloned.1.call-start = ((), (), s32[]{:S(2)}) async-start(), calls=%async_computation.3 | async-start | bytes 4866048 | tf_op jit(solution)/shard_map/all_gather | solution.py:752
  9.1 123.5 %collective-permute-start = (bf16[512,768]{1,0:T(8,128)(2,1)}, bf16[512,768]{1,0:T(8,128)(2,1)S(1)}, u32[]{:S(2)}, u32[]{:S(2)}) collective-permute-start(bf16[512,768]{1,0:T(8,128)(2,1)} %bitcast.139), channel_id=1, source_target_pairs={{0,1},{2,3},{4,5},{6,7},{8,9},{10,11},{12,13},{14,15},{16,17},{18,... | collective-permute-start | bytes 2359304 | tf_op jit(solution)/shard_map/ppermute | solution.py:701
  14.0 155.8 %collective-permute-start.1 = (bf16[1024,768]{1,0:T(8,128)(2,1)}, bf16[1024,768]{1,0:T(8,128)(2,1)}, u32[]{:S(2)}, u32[]{:S(2)}) collective-permute-start(bf16[1024,768]{1,0:T(8,128)(2,1)} %bitcast.183), channel_id=1, source_target_pairs={{0,1},{1,0},{2,3},{3,2},{4,5},{5,4},{6,7},{7,6},{8,9},{9,8},{10,11... | collective-permute-start | bytes 4718600 | tf_op jit(solution)/shard_map/ppermute | solution.py:701
  15.7 107.6 %copy-start.35 = (s32[1,2]{1,0:T(1,128)S(1)}, s32[1,2]{1,0:T(1,128)}, u32[]{:S(2)}) copy-start(s32[1,2]{1,0:T(1,128)} %param.17) | copy-start | bytes 28
  15.7 108.2 %copy-start.36 = (s32[1,2]{1,0:T(1,128)S(1)}, s32[1,2]{1,0:T(1,128)}, u32[]{:S(2)}) copy-start(s32[1,2]{1,0:T(1,128)} %param.18) | copy-start | bytes 28
  15.7 112.0 %copy-start.37 = (s32[4]{0:T(128)S(1)}, s32[4]{0:T(128)}, u32[]{:S(2)}) copy-start(s32[4]{0:T(128)} %constant.94.clone) | copy-start | bytes 52
  15.8 113.0 %copy-start.32 = (s32[1,2048]{1,0:T(1,128)S(1)}, s32[1,2048]{1,0:T(1,128)}, u32[]{:S(2)}) copy-start(s32[1,2048]{1,0:T(1,128)} %param.19) | copy-start | bytes 24580
  15.8 429.0 %reduce-scatter.3.cloned.1.call-start = ((), (), s32[]{:S(2)}) async-start(), calls=%async_computation.4 | async-start | bytes 4866048 | tf_op jit(solution)/shard_map/reduce_scatter | solution.py:869
  17.8 112.9 %copy-start.3 = (bf16[1,512,768]{2,1,0:T(8,128)(2,1)S(1)}, bf16[1,512,768]{2,1,0:T(8,128)(2,1)}, u32[]{:S(2)}) copy-start(bf16[1,512,768]{2,1,0:T(8,128)(2,1)} %param.15) | copy-start | bytes 2359300
  166.2 101.6 %copy-start.4 = (f32[512,768]{1,0:T(8,128)}, f32[512,768]{1,0:T(8,128)S(1)}, u32[]{:S(2)}) copy-start(f32[512,768]{1,0:T(8,128)S(1)} %get-tuple-element.145) | copy-start | bytes 4718596
  166.2 104.2 %copy-start.30 = (f32[512]{0:T(512)}, f32[512]{0:T(512)S(1)}, u32[]{:S(2)}) copy-start(f32[512]{0:T(512)S(1)} %add_rsqrt_fusion.1) | copy-start | bytes 6148
  166.2 9.8 %slice-start = ((s8[4718592]{0:T(1024)(128)(4,1)}), s8[4194304]{0:T(1024)(128)(4,1)S(1)}, s32[]{:S(2)}) async-start(s8[4718592]{0:T(1024)(128)(4,1)} %bitcast.154), calls=%async_computation.6 | async-start | bytes 8388608
  169.8 6.2 %slice-start.1 = ((s8[4718592]{0:T(1024)(128)(4,1)}), s8[524288]{0:T(1024)(128)(4,1)S(1)}, s32[]{:S(2)}) async-start(s8[4718592]{0:T(1024)(128)(4,1)} %bitcast.154), calls=%async_computation.7 | async-start | bytes 1048576
  216.2 8.6 %copy-start.6 = (f32[512,768]{1,0:T(8,128)S(1)}, f32[512,768]{1,0:T(8,128)}, u32[]{:S(2)}) copy-start(f32[512,768]{1,0:T(8,128)} %get-tuple-element.147) | copy-start | bytes 4718596
  229.4 237.1 %reduce-scatter.5.cloned.1.call-start = ((), (), s32[]{:S(2)}) async-start(), calls=%async_computation.5 | async-start | bytes 4866048 | tf_op jit(solution)/shard_map/reduce_scatter | solution.py:869
  229.4 6.7 %copy-start.7 = (f32[512,768]{1,0:T(8,128)S(1)}, f32[512,768]{1,0:T(8,128)}, u32[]{:S(2)}) copy-start(f32[512,768]{1,0:T(8,128)} %get-tuple-element.147) | copy-start | bytes 4718596
  229.5 6.7 %copy-start.18 = (bf16[1,512,768]{2,1,0:T(8,128)(2,1)S(1)}, bf16[1,512,768]{2,1,0:T(8,128)(2,1)}, u32[]{:S(2)}) copy-start(bf16[1,512,768]{2,1,0:T(8,128)(2,1)} %param.28) | copy-start | bytes 2359300
  236.6 33.7 %copy-start.1 = (f32[512,768]{1,0:T(8,128)}, f32[512,768]{1,0:T(8,128)S(1)}, u32[]{:S(2)}) copy-start(f32[512,768]{1,0:T(8,128)S(1)} %multiply_add_fusion.1) | copy-start | bytes 4718596
  297.8 10.6 %slice-start.2 = ((s8[4718592]{0:T(1024)(128)(4,1)}), s8[4194304]{0:T(1024)(128)(4,1)S(1)}, s32[]{:S(2)}) async-start(s8[4718592]{0:T(1024)(128)(4,1)} %bitcast.158), calls=%async_computation.8 | async-start | bytes 8388608
  301.3 7.1 %slice-start.3 = ((s8[4718592]{0:T(1024)(128)(4,1)}), s8[524288]{0:T(1024)(128)(4,1)S(1)}, s32[]{:S(2)}) async-start(s8[4718592]{0:T(1024)(128)(4,1)} %bitcast.158), calls=%async_computation.9 | async-start | bytes 1048576
  301.3 7.1 %copy-start.51 = (bf16[768,2048]{1,0:T(8,128)(2,1)S(1)}, bf16[768,2048]{1,0:T(8,128)(2,1)}, u32[]{:S(2)}) copy-start(bf16[768,2048]{1,0:T(8,128)(2,1)} %get-tuple-element.41) | copy-start | bytes 9437188
  306.9 50.0 %collective-permute-start.2 = (bf16[512,768]{1,0:T(8,128)(2,1)}, bf16[512,768]{1,0:T(8,128)(2,1)}, u32[]{:S(2)}, u32[]{:S(2)}) collective-permute-start(bf16[512,768]{1,0:T(8,128)(2,1)} %slice.330), channel_id=1, source_target_pairs={{1,0},{3,2},{5,4},{7,6},{9,8},{11,10},{13,12},{15,14},{17,16},{19,... | collective-permute-start | bytes 2359304 | tf_op jit(solution)/shard_map/ppermute | solution.py:711
  314.0 9.2 %copy-start.10 = (f32[2048,768]{1,0:T(8,128)}, f32[2048,768]{1,0:T(8,128)S(1)}, u32[]{:S(2)}) copy-start(f32[2048,768]{1,0:T(8,128)S(1)} %convolution_add_fusion) | copy-start | bytes 18874372
  315.4 125.1 %collective-permute-start.3 = (bf16[1024,768]{1,0:T(8,128)(2,1)}, bf16[1024,768]{1,0:T(8,128)(2,1)}, u32[]{:S(2)}, u32[]{:S(2)}) collective-permute-start(bf16[1024,768]{1,0:T(8,128)(2,1)} %slice.329), channel_id=1, source_target_pairs={{0,1},{1,0},{2,3},{3,2},{4,5},{5,4},{6,7},{7,6},{8,9},{9,8},{10,11... | collective-permute-start | bytes 4718600 | tf_op jit(solution)/shard_map/ppermute | solution.py:711
  340.9 11.4 %slice-start.4 = ((s8[4718592]{0:T(1024)(128)(4,1)}), s8[4194304]{0:T(1024)(128)(4,1)S(1)}, s32[]{:S(2)}) async-start(s8[4718592]{0:T(1024)(128)(4,1)} %bitcast.181), calls=%async_computation.10 | async-start | bytes 8388608
  345.1 7.2 %slice-start.5 = ((s8[4718592]{0:T(1024)(128)(4,1)}), s8[524288]{0:T(1024)(128)(4,1)S(1)}, s32[]{:S(2)}) async-start(s8[4718592]{0:T(1024)(128)(4,1)} %bitcast.181), calls=%async_computation.11 | async-start | bytes 1048576
  (35 other events, 99.7 us)
Sparse Core Ops, SparseCore 0:
  11.0 77.2 all-gather.2
  91.2 62.2 all-gather.4
  229.5 110.8 reduce-scatter.2
  346.7 119.8 reduce-scatter.4

commit v3 on v2

v3 whole, which is shorter than its diff:
```python
import functools
import math

import jax
import jax.numpy as jnp
import numpy as np
from jax import lax
from jax.experimental import pallas as pl
from jax.experimental.pallas import tpu as pltpu
from jax.sharding import PartitionSpec as P

D = 768
HEADS = 12
HDIM = 64
FF = 3072
BUCKETS = 32
PAIRS = HEADS // 2
LOG2E = math.log2(math.e)
LN2 = math.log(2.0)
epsilon = 1e-06
neg_large = -1e30
bucket_edges = (19, 21, 24, 27, 31, 35, 40, 46, 52, 59, 67, 77, 87, 99, 113)
f32 = jnp.float32
bf16 = jnp.bfloat16
NT = (((1,), (1,)), ((), ()))
NN = (((1,), (0,)), ((), ()))
TN = (((0,), (0,)), ((), ()))
BOTH = ("dp", "seq")
MESH = pl.DeviceIdType.MESH


def mm(a, b, dims=NN):
    return lax.dot_general(a, b, dims, preferred_element_type=f32)


def head_lanes(which):
    low = lax.broadcasted_iota(jnp.int32, (1, 128), 1) < HDIM
    return low if which == 0 else jnp.logical_not(low)


def row_chunks(rows, keys, causal, step):
    return [
        (slice(i, i + step), (keys - rows + i + step) if causal else keys)
        for i in range(0, rows, step)
    ]


def near_bias(near_ref, which):
    row = lax.broadcasted_iota(jnp.int32, (128, 256), 0)
    column = lax.broadcasted_iota(jnp.int32, (128, 256), 1)
    tiles = []
    for flag in (0, 1):
        line = near_ref[0, 2 * which + flag : 2 * which + flag + 1, :]
        tile = pltpu.roll(jnp.broadcast_to(line, (128, 256)), 0, 1, stride=1, stride_axis=0)
        tiles.append(jnp.where(column - row > 128, neg_large, tile))
    return tiles


def diagonal_sums(tile):
    for step in (64, 32, 16, 8):
        tile = tile[:step] + pltpu.roll(tile[step:], 256 - step, 1)
    row = lax.broadcasted_iota(jnp.int32, (8, 256), 0)
    for step in (4, 2, 1):
        tile = jnp.where((row & step) != 0, pltpu.roll(tile, 256 - step, 1), tile)
    return jnp.sum(tile, axis=0, keepdims=True)


ROW, MEMORY_ROW, END_ONE, END_TWO, MEMORY_ONE, MEMORY_TWO, FLAG_ONE, FLAG_TWO = range(8)


def pairs_between(place, end_one, end_two):
    return (place >= end_one).astype(jnp.int32) + (place >= end_two).astype(jnp.int32)


def flagged(info, first, count, width):
    place = lax.broadcasted_iota(jnp.int32, (count, width), 0) + (info[ROW] + first)
    pair = pairs_between(place, info[END_ONE], info[END_TWO])
    return jnp.where(pair == 0, info[FLAG_ONE], jnp.where(pair == 1, info[FLAG_TWO], 0)) > 0


def extra_columns(info, rows, keys, causal, query_extra, key_extra):
    lane = lax.broadcasted_iota(jnp.int32, (rows, 128), 1) & (HDIM - 1)
    place = lax.broadcasted_iota(jnp.int32, (rows, 128), 0) + info[ROW]
    pair = pairs_between(place, info[END_ONE], info[END_TWO])
    flag = flagged(info, 0, rows, 128).astype(jnp.int32)
    wanted = jnp.where(lane < 3, pair, (flag << 1) + 3)
    chosen = jnp.where(lane < 3, lane, ((lane - 3) & ~1) + 3)
    here = jnp.logical_and(wanted == chosen, lane < 7)
    query_extra[...] = jnp.where(here, 1.0, 0.0).astype(bf16)
    lane = lax.broadcasted_iota(jnp.int32, (keys, 128), 1) & (HDIM - 1)
    place = lax.broadcasted_iota(jnp.int32, (keys, 128), 0)
    if causal:
        place = place + (info[ROW] + rows - keys)
        pair = pairs_between(place, info[END_ONE], info[END_TWO])
        pair = jnp.where(place < 0, 3, pair)
    else:
        place = place + info[MEMORY_ROW]
        place = jnp.where(place >= keys, place - keys, place)
        pair = pairs_between(place, info[MEMORY_ONE], info[MEMORY_TWO])
    wrong = jnp.logical_and(pair != lane, lane < 3)
    key_extra[...] = jnp.where(wrong, neg_large, 0.0).astype(bf16)


def attend_body(rows, keys, causal, step, parts, *refs):
    info, q_ref = refs[:2]
    key_refs, value_refs = refs[2 : 2 + parts], refs[2 + parts : 2 + 2 * parts]
    o_ref, e_ref, inv_ref, query_extra, key_extra = refs[-5:]

    @pl.when(pl.program_id(0) == 0)
    def _():
        extra_columns(info, rows, keys, causal, query_extra, key_extra)

    extra = key_extra[...]
    if causal:
        far_ref, near_ref = refs[2 + 2 * parts : 4 + 2 * parts]
        extra = extra + far_ref[0]
    key_pair = jnp.concatenate([ref[...] for ref in key_refs], axis=0)
    value_pair = jnp.concatenate([ref[...] for ref in value_refs], axis=0)
    chunks = row_chunks(rows, keys, causal, step)
    found = []
    for which in (0, 1):
        mine = head_lanes(which)
        key_head = jnp.where(mine, key_pair, extra)
        value_head = jnp.where(mine, value_pair, jnp.ones_like(value_pair))
        if causal:
            tile_zero, tile_one = near_bias(near_ref, which)
        done = []
        for here, width in chunks:
            query = jnp.where(mine, q_ref[here], query_extra[here])
            scores = mm(query, key_head[:width], NT)
            if causal:
                cut = width - 256
                flag = flagged(info, here.start, step, 1)
                near = scores[:, cut:] + jnp.where(flag, tile_one, tile_zero)
                far = scores[:, :cut]
                peak = jnp.maximum(
                    jnp.max(far, axis=1, keepdims=True), jnp.max(near, axis=1, keepdims=True)
                )
                near = jnp.exp2(near - peak).astype(bf16)
                far = jnp.exp2(far - peak).astype(bf16)
                e_ref[which, here, :cut] = far
                e_ref[which, here, cut:width] = near
                mixed = mm(far, value_head[:cut]) + mm(near, value_head[cut:width])
            else:
                peak = jnp.max(scores, axis=1, keepdims=True)
                weights = jnp.exp2(scores - peak).astype(bf16)
                e_ref[which, here, :] = weights
                mixed = mm(weights, value_head)
            total = mixed[:, HDIM : HDIM + 1] if which == 0 else mixed[:, 0:1]
            inverse = 1.0 / total
            done.append((mixed * inverse, jnp.broadcast_to(inverse, mixed.shape)))
        found.append(done)
    low = head_lanes(0)
    for index, (here, _) in enumerate(chunks):
        o_ref[here] = jnp.where(low, found[0][index][0], found[1][index][0]).astype(bf16)
        inv_ref[here] = jnp.where(low, found[0][index][1], found[1][index][1])


def pair_columns(rows, first=0):
    return pl.BlockSpec((rows, 128), lambda p: (0, first + p))


def operands_of(info, query, parts):
    arrays = [info, query] + [part[0] for part in parts] * 2
    specs = [pl.BlockSpec(memory_space=pltpu.SMEM), pair_columns(query.shape[0])]
    for place in (1, 2):
        specs += [pair_columns(part[0].shape[0], part[place]) for part in parts]
    return arrays, specs


def per_pair(height, width):
    return pl.BlockSpec((1, height, width), lambda p: (p, 0, 0))


def attend(info, rows, query, parts, far=None, near=None):
    keys = sum(part[0].shape[0] for part in parts)
    causal = far is not None
    step = 128 if causal else min(256, rows)
    operands, specs = operands_of(info, query, parts)
    if causal:
        operands += [far, near]
        specs += [per_pair(1, 128), per_pair(4, 256)]
    return pl.pallas_call(
        functools.partial(attend_body, rows, keys, causal, step, len(parts)),
        grid=(PAIRS,),
        in_specs=specs,
        out_specs=(
            pair_columns(rows),
            pl.BlockSpec((2, rows, keys), lambda p: (p, 0, 0)),
            pair_columns(rows),
        ),
        out_shape=(
            jax.ShapeDtypeStruct((rows, D), bf16),
            jax.ShapeDtypeStruct((HEADS, rows, keys), bf16),
            jax.ShapeDtypeStruct((rows, D), f32),
        ),
        scratch_shapes=[pltpu.VMEM((rows, 128), bf16), pltpu.VMEM((keys, 128), bf16)],
        compiler_params=pltpu.CompilerParams(vmem_limit_bytes=56 << 20),
        name="attend_causal" if causal else "attend_cross",
    )(*operands)


def attend_back_body(rows, keys, causal, step, parts, *refs):
    info, q_ref = refs[:2]
    key_refs, value_refs = refs[2 : 2 + parts], refs[2 + parts : 2 + 2 * parts]
    e_ref, o_ref, inv_ref, d_ref = refs[2 + 2 * parts : 6 + 2 * parts]
    if causal:
        dq_ref, dk_ref, dv_ref, near_ref, sum_ref, ds_ref = refs[6 + 2 * parts :]
    else:
        dq_ref, dk_ref, dv_ref, ds_ref = refs[6 + 2 * parts :]
    lane = lax.broadcasted_iota(jnp.int32, (1, 128), 1)
    key_pair = jnp.concatenate([ref[...] for ref in key_refs], axis=0)
    value_pair = jnp.concatenate([ref[...] for ref in value_refs], axis=0)
    scaled = (d_ref[...].astype(f32) * inv_ref[...]).astype(bf16)
    product = scaled.astype(f32) * o_ref[...].astype(f32)
    scaled_t = scaled.T
    query_t = q_ref[...].T
    chunks = row_chunks(rows, keys, causal, step)
    query_parts = []
    for which in (0, 1):
        mine = head_lanes(which)
        base = HDIM if which == 0 else 0
        value_head = jnp.where(mine, value_pair, jnp.ones_like(value_pair))
        key_head = jnp.where(mine, key_pair, jnp.ones_like(key_pair))
        delta = jnp.sum(jnp.where(mine, product, 0.0), axis=1, keepdims=True)
        high = delta.astype(bf16)
        rest = (delta - high.astype(f32)).astype(bf16)
        extra = jnp.where(
            lane == base, -high, jnp.where(lane == base + 1, -rest, jnp.zeros_like(rest))
        )
        grad_head = jnp.where(mine, scaled, extra)
        done = []
        if causal:
            near_all = jnp.zeros((128, 256), f32)
            near_one = jnp.zeros((128, 256), f32)
        for here, width in chunks:
            centred = mm(grad_head[here], value_head[:width], NT)
            grad_scores = e_ref[which, here, :width].astype(f32) * centred
            if causal:
                near = grad_scores[:, width - 256 :]
                near_all = near_all + near
                flag = flagged(info, here.start, step, 1)
                near_one = near_one + jnp.where(flag, near, 0.0)
            grad_scores = grad_scores.astype(bf16)
            ds_ref[here, :width] = grad_scores
            done.append(mm(grad_scores, key_head[:width]))
        query_parts.append(done)
        half = slice(HDIM * which, HDIM * which + HDIM)
        if causal:
            spans = [(slice(0, keys - rows), 0)] if keys > rows else []
            spans += [
                (slice(keys - rows + i, keys - rows + i + step), i) for i in range(0, rows, step)
            ]
        else:
            spans = [(slice(0, keys), 0)]
        for span, first in spans:
            grad_key = mm(query_t[half, first:], ds_ref[first:, span])
            dk_ref[half, span] = (grad_key * LN2).astype(dk_ref.dtype)
            grad_value = mm(scaled_t[half, first:], e_ref[which, first:, span])
            dv_ref[half, span] = grad_value.astype(dv_ref.dtype)
        if causal:
            for flag, tile in ((0, near_all - near_one), (1, near_one)):
                near_ref[0, 2 * which + flag : 2 * which + flag + 1, :] = diagonal_sums(tile)
    low = head_lanes(0)
    for index, (here, _) in enumerate(chunks):
        both = jnp.where(low, query_parts[0][index], query_parts[1][index])
        dq_ref[here] = (both * 0.125).astype(dq_ref.dtype)
    if causal:
        flags = flagged(info, 0, rows, 1)
        for which in (0, 1):
            whole = jnp.concatenate(query_parts[which], axis=0)
            one = jnp.sum(jnp.where(flags, whole, 0.0), axis=0, keepdims=True)
            every = jnp.sum(whole, axis=0, keepdims=True)
            sum_ref[0, 2 * which : 2 * which + 1, :] = every - one
            sum_ref[0, 2 * which + 1 : 2 * which + 2, :] = one


def attend_back(info, query, parts, weights, mixed, inverse, grad_mixed, causal):
    rows, keys = weights.shape[1:]
    step = 128 if causal else min(256, rows)
    operands, specs = operands_of(info, query, parts)
    operands += [weights, mixed, inverse, grad_mixed]
    specs += [pl.BlockSpec((2, rows, keys), lambda p: (p, 0, 0))] + [pair_columns(rows)] * 3
    turned = jax.ShapeDtypeStruct((D, keys), bf16)
    turned_spec = pl.BlockSpec((128, keys), lambda p: (p, 0))
    shapes = [jax.ShapeDtypeStruct((rows, D), bf16), turned, turned]
    out_specs = [pair_columns(rows), turned_spec, turned_spec]
    if causal:
        shapes += [
            jax.ShapeDtypeStruct((PAIRS, 4, 256), f32),
            jax.ShapeDtypeStruct((PAIRS, 4, 128), f32),
        ]
        out_specs += [per_pair(4, 256), per_pair(4, 128)]
    return pl.pallas_call(
        functools.partial(attend_back_body, rows, keys, causal, step, len(parts)),
        grid=(PAIRS,),
        in_specs=specs,
        out_specs=tuple(out_specs),
        out_shape=tuple(shapes),
        scratch_shapes=[pltpu.VMEM((rows, keys), bf16)],
        compiler_params=pltpu.CompilerParams(vmem_limit_bytes=56 << 20),
        name="attend_causal_back" if causal else "attend_cross_back",
    )(*operands)


def place_here():
    index = lax.axis_index("dp")
    return index // 4, (index // 2) % 2, index % 2, lax.axis_index("seq")


def block_of(z, x, core, y):
    return ((z * 2 + x) * 2 + core) * 2 + y


def device_of(z, x, core, y):
    return ((z * 2 + x) * 2 + core, y)


def greet_neighbours(z, x, core, y):
    barrier = pltpu.get_barrier_semaphore()

    def greet(device):
        pl.semaphore_signal(barrier, inc=1, device_id=device, device_id_type=MESH)

    greet(device_of(z, x, 1 - core, y))
    greet(device_of(z, 1 - x, core, y))
    greet(device_of(z, x, core, 1 - y))

    @pl.when(z > 0)
    def _():
        greet(device_of(z - 1, x, core, y))

    @pl.when(z < 3)
    def _():
        greet(device_of(z + 1, x, core, y))

    pl.semaphore_wait(barrier, 4 + ((z + 1) // 2) % 2)


def gather_body(count, *refs):
    sources, wholes = refs[:count], refs[count : 2 * count]
    own_sems, up_sems, down_sems, side_sems, turn_sems, mate_sems, recv_sems = refs[2 * count :]
    z, x, core, y = place_here()
    mate = device_of(z, x, 1 - core, y)
    me = block_of(z, x, core, y)
    greet_neighbours(z, x, core, y)

    def near(which, side, turn):
        return ((x + side) % 2, (y + turn) % 2) if which == 0 else ((x + turn) % 2, (y + side) % 2)

    def send(which, source, block, send_sem, device):
        return pltpu.make_async_remote_copy(
            src_ref=source,
            dst_ref=wholes[which].at[block],
            send_sem=send_sem,
            recv_sem=recv_sems.at[which, block],
            device_id=device,
            device_id_type=MESH,
        )

    def copies(which, far, up, side, turn, source=None):
        at_z = z + far if up else z - far
        bx, by = near(which, side, turn)
        block = block_of(at_z, bx, core, by)
        source = wholes[which].at[block] if source is None else source
        slot = (2 * far + (1 if up else 0)) if far else 0
        slot = max(slot - 1, 0)
        out = [(None, send(which, source, block, mate_sems.at[which, (side * 2 + turn) * 7 + slot], mate))]
        if turn == 0:
            tx, ty = near(which, 0, 1)
            out.append(
                (None, send(which, source, block, turn_sems.at[which, side * 7 + slot], device_of(z, tx, core, ty)))
            )
            if side == 0:
                sx, sy = near(which, 1, 0)
                out.append((None, send(which, source, block, side_sems.at[which, slot], device_of(z, sx, core, sy))))
                if far == 0 or not up:
                    out.append(
                        (z < 3, send(which, source, block, up_sems.at[which, far], device_of(z + 1, x, core, y)))
                    )
                if far == 0 or up:
                    out.append(
                        (z > 0, send(which, source, block, down_sems.at[which, far], device_of(z - 1, x, core, y)))
                    )
        return block, out

    def when(condition, action):
        if condition is None:
            action()
        else:
            pl.when(condition)(action)

    def exists(far, up):
        if far == 0:
            return None
        return z + far < 4 if up else z - far >= 0

    def onwards(which, far, up, side, turn, source=None):
        def run():
            block, out = copies(which, far, up, side, turn, source)
            if source is None:
                pltpu.make_async_copy(wholes[which].at[block], wholes[which].at[block], recv_sems.at[which, block]).wait()
            for condition, copy in reversed(out):
                when(condition, copy.start)

        when(exists(far, up), run)

    own = [
        pltpu.make_async_copy(sources[i], wholes[i].at[me], own_sems.at[i]) for i in range(count)
    ]
    for which in range(count):
        onwards(which, 0, True, 0, 0, sources[which])
    for copy in own:
        copy.start()
    waves = [[] for _ in range(6)]
    for side in (0, 1):
        for turn in (0, 1):
            for far in range(4):
                for up in (False, True):
                    if far == 0 and (up or (side == 0 and turn == 0)):
                        continue
                    waves[far + side + turn].append((far, up, side, turn))
    for wave in waves:
        for far, up, side, turn in wave:
            for which in range(count):
                onwards(which, far, up, side, turn)
    for side in (0, 1):
        for turn in (0, 1):
            for far in range(4):
                for up in (False, True):
                    if far == 0 and up:
                        continue
                    for which in range(count):

                        def finish(which=which, far=far, up=up, side=side, turn=turn):
                            at_z = z + far if up else z - far
                            bx, by = near(which, side, turn)
                            block = block_of(at_z, bx, 1 - core, by)
                            whole = wholes[which].at[block]
                            pltpu.make_async_copy(whole, whole, recv_sems.at[which, block]).wait()
                            source = sources[which] if (far, side, turn) == (0, 0, 0) else None
                            _, out = copies(which, far, up, side, turn, source)
                            for condition, copy in out:
                                when(condition, copy.wait_send)

                        when(exists(far, up), finish)
    for copy in own:
        copy.wait()


def gather_blocks(*blocks):
    count = len(blocks)
    any_space = pl.BlockSpec(memory_space=pl.ANY)
    dma = pltpu.SemaphoreType.DMA
    return pl.pallas_call(
        functools.partial(gather_body, count),
        in_specs=[any_space] * count,
        out_specs=[any_space] * count,
        out_shape=[jax.ShapeDtypeStruct((32, *block.shape), block.dtype) for block in blocks],
        scratch_shapes=[
            dma((count,)),
            dma((count, 4)),
            dma((count, 4)),
            dma((count, 7)),
            dma((count, 14)),
            dma((count, 28)),
            dma((count, 32)),
        ],
        compiler_params=pltpu.CompilerParams(collective_id=0, has_side_effects=True),
        name="gather_blocks",
    )(*blocks)


SELF_PRODUCTS = (((1,), 2, False), ((0, 1), 3, True), ((0, 1), 4, True), ((5,), 6, False))
CROSS_PRODUCTS = (((0,), 1, False), ((2, 3), 4, True), ((2, 3), 5, True), ((6,), 7, False))


def scatter_body(counts, *refs):
    total_in = sum(counts)
    arrays, small, outs = refs[:total_in], refs[total_in], refs[total_in + 1 : total_in + 6]
    refs = refs[total_in + 6 :]
    held, small_held = refs[:total_in], refs[total_in]
    refs = refs[total_in + 1 :]
    parts, mate_in, first_in, second_in, line_in = (refs[2 * i : 2 * i + 2] for i in range(5))
    load_sems, mate_sems, first_sems, second_sems, line_sems = refs[10:15]
    mate_recv, first_recv, second_recv, line_recv = refs[15:]
    z, x, core, y = place_here()
    loads = [
        pltpu.make_async_copy(source, target, load_sems.at[i])
        for i, (source, target) in enumerate(zip((*arrays, small), (*held, small_held)))
    ]
    for load in loads:
        load.start()
    greet_neighbours(z, x, core, y)
    half = z // 2
    order = (3 - 3 * half, 2 - half, 1 - z + 4 * half, z)

    def near(first, second):
        return (x + first) % 2, (y + second) % 2

    def block(i, first, second, other_core=0):
        bx, by = near(first, second)
        return block_of(order[i], bx, (core + other_core) % 2, by)

    def slot_of(i, first, second):
        bx, by = near(first, second)
        return (order[i] * 2 + bx) * 2 + by

    def remote(source, target, send_sem, recv_sem, device):
        return pltpu.make_async_remote_copy(
            src_ref=source,
            dst_ref=target,
            send_sem=send_sem,
            recv_sem=recv_sem,
            device_id=device,
            device_id_type=MESH,
        )

    def to_mate(which, i, first, second):
        slot = slot_of(i, first, second)
        return remote(
            parts[which].at[block(i, first, second, 1)],
            mate_in[which].at[slot],
            mate_sems.at[which, slot],
            mate_recv.at[which, slot],
            device_of(z, x, 1 - core, y),
        )

    def to_first(which, i, second):
        bx, by = near(1, 0)
        return remote(
            parts[which].at[block(i, 1, second)],
            first_in[which].at[2 * i + second],
            first_sems.at[which, 2 * i + second],
            first_recv.at[which, 2 * i + second],
            device_of(z, bx, core, by),
        )

    def to_second(which, i):
        bx, by = near(0, 1)
        return remote(
            parts[which].at[block(i, 0, 1)],
            second_in[which].at[i],
            second_sems.at[which, i],
            second_recv.at[which, i],
            device_of(z, bx, core, by),
        )

    def along_line(which, i, second=0):
        step = 1 - 2 * half if i < 2 else 1 - 2 * (z % 2)
        came = (1 - step) // 2
        slot = (came * 4 + order[i]) * 2 + second
        return slot, remote(
            parts[which].at[block(i, 0, second)],
            line_in[which].at[slot],
            line_sems.at[which, 2 * i + second],
            line_recv.at[which, slot],
            device_of(z + step, x, core, y),
        )

    def arrived(buffer, sem):
        pltpu.make_async_copy(buffer, buffer, sem).wait()

    def wide(ref, index):
        return ref[index].astype(f32)

    every = [(1, 1), (1, 0), (0, 1), (0, 0)]

    def products(which, i):
        first = 0 if which == 0 else counts[0]
        height = 8 * parts[which].shape[1]
        odd = order[i] % 2
        window = pl.ds(pl.multiple_of(order[i] * height - odd * 64, 128), height + 64)
        blocks = pl.ds(order[i] * 8, 8)
        taken = {}
        for column, (lefts, right, turned) in enumerate(SELF_PRODUCTS if which == 0 else CROSS_PRODUCTS):
            if i == 0:
                for needed in (*lefts, right):
                    if needed in waiting[which]:
                        waiting[which].remove(needed)
                        loads[first + needed].wait()
            for left in lefts:
                if left not in taken:
                    rows = held[first + left][:, window].T
                    taken[left] = jnp.where(odd > 0, rows[64:], rows[:height])
            other = held[first + right][...]
            value = mm(jnp.concatenate([taken[left] for left in lefts], axis=1), other, NT if turned else NN)
            value = value.reshape(8, height // 8, value.shape[1]).astype(bf16)
            parts[which][blocks, :, column * D : (column + 1) * D] = value
        if which == 0:
            if i == 0:
                loads[-1].wait()
            parts[0][blocks, :, 4 * D :] = small_held[blocks]

    waiting = [set(range(counts[0])), set(range(counts[1]))]

    def make(i):
        for which in (1, 0):
            products(which, i)
            for first, second in every:
                to_mate(which, i, first, second).start()

    def chip_sum(which, i, first, second):
        here = block(i, first, second)
        slot = slot_of(i, first, second)
        arrived(mate_in[which].at[slot], mate_recv.at[which, slot])
        return here, wide(parts[which], here) + wide(mate_in[which], slot)

    def send_first(i):
        for second in (1, 0):
            for which in (1, 0):
                here, total = chip_sum(which, i, 1, second)
                parts[which][here] = total.astype(bf16)
                to_first(which, i, second).start()

    middle = (z + 1) // 2 == 1

    def after_first(which, i, second):
        here, total = chip_sum(which, i, 0, second)
        arrived(first_in[which].at[2 * i + second], first_recv.at[which, 2 * i + second])
        return here, total + wide(first_in[which], 2 * i + second)

    def send_second(i):
        here, total = after_first(1, i, 1)
        parts[1][here] = total.astype(bf16)
        to_second(1, i).start()

    def send_line(which, i, second, here, total):
        parts[which][here] = total.astype(bf16)
        slot, copy = along_line(which, i, second)

        @pl.when(middle)
        def _():
            arrived(line_in[which].at[slot], line_recv.at[which, slot])
            total = wide(parts[which], here) + wide(line_in[which], slot)
            parts[which][here] = total.astype(bf16)

        copy.start()

    def line_self(i):
        for second in (1, 0):
            send_line(0, i, second, *after_first(0, i, second))

    def line_cross(i):
        here, total = after_first(1, i, 0)
        arrived(second_in[1].at[i], second_recv.at[1, i])
        total = total + wide(second_in[1], i)
        if i < 3:
            send_line(1, i, 0, here, total)
        else:
            put(1, total, False)

    def from_line(which, second, add):
        for came, there in ((0, z > 0), (1, z < 3)):
            slot = (came * 4 + z) * 2 + second

            @pl.when(there)
            def _():
                arrived(line_in[which].at[slot], line_recv.at[which, slot])
                add(wide(line_in[which], slot))

    def last_self():
        here, total = after_first(0, 3, 1)
        parts[0][here] = total.astype(bf16)

        def add(value):
            parts[0][here] = (wide(parts[0], here) + value).astype(bf16)

        from_line(0, 1, add)
        to_second(0, 3).start()
        put(0, after_first(0, 3, 0)[1], False)
        from_line(0, 0, lambda value: put(0, value, True))

    def put(which, value, add):
        stacked, single = outs[2 * which : 2 * which + 2]
        targets = [(stacked.at[j], j) for j in range(3)] + [(single, 3)]
        for target, j in targets:
            piece = value[:, j * D : (j + 1) * D]
            target[...] = target[...] + piece if add else piece
        if which == 0:
            piece = value[:, 4 * D :]
            outs[4][...] = outs[4][...] + piece if add else piece


    make(0)
    make(1)
    send_first(0)
    make(2)
    send_first(1)
    send_second(0)
    line_self(0)
    make(3)
    send_first(2)
    send_second(1)
    line_self(1)
    line_cross(0)
    send_first(3)
    send_second(2)
    line_self(2)
    line_cross(1)
    send_second(3)
    line_cross(2)
    last_self()
    line_cross(3)
    from_line(1, 0, lambda value: put(1, value, True))
    arrived(second_in[0].at[3], second_recv.at[0, 3])
    put(0, wide(second_in[0], 3), True)

    for which in (0, 1):
        for i in range(4):
            for first, second in every:
                to_mate(which, i, first, second).wait_send()
            for second in (0, 1):
                to_first(which, i, second).wait_send()
            if which == 1 or i == 3:
                to_second(which, i).wait_send()
            if i < 3:
                for second in (0, 1)[: 2 - which]:
                    along_line(which, i, second)[1].wait_send()


def scatter_products(self_arrays, cross_arrays, small):
    counts = (len(self_arrays), len(cross_arrays))
    arrays = (*self_arrays, *cross_arrays)
    shard = small.shape[1]
    shapes = [(shard, 4 * D + small.shape[2]), (shard, 4 * D)]
    dma = pltpu.SemaphoreType.DMA

    def buffers(slots):
        return [pltpu.VMEM((slots, *shape), bf16) for shape in shapes]

    return pl.pallas_call(
        functools.partial(scatter_body, counts),
        in_specs=[pl.BlockSpec(memory_space=pl.ANY)] * (len(arrays) + 1),
        out_specs=[pl.BlockSpec(memory_space=pltpu.VMEM)] * 5,
        out_shape=[
            jax.ShapeDtypeStruct(shape, f32)
            for shape in ((3, shard, D), (shard, D), (3, shard, D), (shard, D), (shard, small.shape[2]))
        ],
        scratch_shapes=[pltpu.VMEM(array.shape, array.dtype) for array in (*arrays, small)]
        + buffers(32)
        + buffers(16)
        + buffers(8)
        + buffers(4)
        + buffers(16)
        + [
            dma((len(arrays) + 1,)),
            dma((2, 16)),
            dma((2, 8)),
            dma((2, 4)),
            dma((2, 6)),
            dma((2, 16)),
            dma((2, 8)),
            dma((2, 4)),
            dma((2, 16)),
        ],
        compiler_params=pltpu.CompilerParams(
            collective_id=1, has_side_effects=True, vmem_limit_bytes=60 << 20
        ),
        name="scatter_products",
    )(*arrays, small)


def inverse_rms(values):
    return lax.rsqrt(jnp.mean(values * values, axis=-1, keepdims=True) + epsilon)


def norm_back(values, inverse, gain, grad):
    unit = values * inverse
    grad = grad * gain
    return inverse * (grad - unit * jnp.mean(grad * unit, axis=-1, keepdims=True))


def gelu_and_slope(value):
    upper = 0.5 * (1.0 + lax.erf(value * math.sqrt(0.5)))
    density = jnp.exp(-0.5 * value * value) * (1.0 / math.sqrt(2.0 * math.pi))
    return value * upper, upper + value * density


def feed_forward_body(rows, *refs):
    x1_ref, mixed_ref, out_ref, gain_ref, grad_ref, in_ref, back_ref = refs[:7]
    layer_ref, dx_ref, low_ref, mixed_back_ref, weight_ref = refs[7:12]
    x2, h3, h3_t, total, back, act = refs[12:]
    step, part = pl.program_id(0), pl.program_id(1)
    first = jnp.logical_and(step == 0, part == 0)
    last = jnp.logical_and(step == pl.num_programs(0) - 1, part == 1)

    @pl.when(first)
    def _():
        value = x1_ref[...] + mm(mixed_ref[...], out_ref[...])
        x2[...] = value
        normed = (value * inverse_rms(value) * gain_ref[...]).astype(bf16)
        h3[...] = normed
        h3_t[...] = normed.T
        total[...] = value
        back[...] = jnp.zeros_like(back)

    @pl.when(part == 0)
    def _():
        hidden, slope = gelu_and_slope(mm(h3[...], in_ref[...]))
        hidden = hidden.astype(bf16)
        act[...] = hidden
        total[...] += mm(hidden, back_ref[...])
        grad_pre = (slope * mm(grad_ref[...], back_ref[...], NT)).astype(bf16)
        back[...] += mm(grad_pre, in_ref[...], NT)
        weight_ref[...] = mm(h3_t[...], grad_pre).astype(bf16)

    @pl.when(part == 1)
    def _():
        weight_ref[...] = mm(act[...].T, grad_ref[...]).astype(bf16)

    @pl.when(last)
    def _():
        layer_ref[...] = total[...].astype(bf16)
        value = x2[...]
        grad = grad_ref[...].astype(f32)
        grad = grad + norm_back(value, inverse_rms(value), gain_ref[...], back[...])
        dx_ref[...] = grad
        low = grad.astype(bf16)
        low_ref[...] = low
        mixed_back_ref[...] = mm(low, out_ref[...], NT).astype(bf16)


def feed_forward(resid, mixed, all_cross, gain, grad_out, all_ffn):
    rows = resid.shape[0]
    units = FF // D

    def whole(height):
        return pl.BlockSpec((height, D), lambda j, s: (0, 0))

    rows_f32 = jax.ShapeDtypeStruct((rows, D), f32)
    rows_bf16 = jax.ShapeDtypeStruct((rows, D), bf16)
    return pl.pallas_call(
        functools.partial(feed_forward_body, rows),
        grid=(units, 2),
        in_specs=[
            whole(rows),
            whole(rows),
            pl.BlockSpec((D, D), lambda j, s: (0, 3)),
            whole(1),
            whole(rows),
            pl.BlockSpec((D, D), lambda j, s: (0, j)),
            pl.BlockSpec((D, D), lambda j, s: (0, units + j)),
        ],
        out_specs=[
            whole(rows),
            whole(rows),
            whole(rows),
            whole(rows),
            pl.BlockSpec((D, D), lambda j, s: (0, s * units + j)),
        ],
        out_shape=[
            rows_bf16,
            rows_f32,
            rows_bf16,
            rows_bf16,
            jax.ShapeDtypeStruct((D, 2 * FF), bf16),
        ],
        scratch_shapes=[
            pltpu.VMEM((rows, D), f32),
            pltpu.VMEM((rows, D), bf16),
            pltpu.VMEM((D, rows), bf16),
            pltpu.VMEM((rows, D), f32),
            pltpu.VMEM((rows, D), f32),
            pltpu.VMEM((rows, D), bf16),
        ],
        compiler_params=pltpu.CompilerParams(vmem_limit_bytes=48 << 20),
        name="feed_forward",
    )(resid, mixed, all_cross, gain[None], grad_out, all_ffn, all_ffn)


def bias_matrices():
    place = np.arange(256)
    distance = np.where(place <= 128, 128 - place, 384 - place)
    edges = np.array(bucket_edges)
    buckets = np.where(distance < 16, distance, 16 + (distance[:, None] >= edges).sum(axis=1))
    spread = np.zeros((2, 2, BUCKETS, 2, 2, 256), np.float32)
    columns = np.zeros((2, 2, BUCKETS, 128), np.float32)
    sums = np.zeros((2, 2, 128, 2, 2, BUCKETS), np.float32)
    for which in (0, 1):
        for flag in (0, 1):
            spread[which, flag, buckets, which, flag, place] += 1.0
            spread[which, flag, BUCKETS - 1, which, flag, :] -= 1.0
            base = (HDIM if which == 0 else 0) + 3 + 2 * flag
            columns[which, flag, BUCKETS - 1, base : base + 2] = 1.0
            sums[which, flag, HDIM if which == 0 else 0, which, flag, BUCKETS - 1] = 1.0
    spread = spread.reshape(128, 1024)
    forward = np.concatenate((spread, columns.reshape(128, 128)), axis=1)
    backward = np.concatenate((spread.T, sums.reshape(512, 128)), axis=0)
    return forward, backward


def bias_parts(table_low):
    by_pair = table_low.T.reshape(PAIRS, 4 * BUCKETS)
    both = mm(by_pair, jnp.asarray(bias_matrices()[0], bf16)) * LOG2E
    far = both[:, 1024:]
    high = far.astype(bf16)
    rest = (far - high.astype(f32)).astype(bf16)
    odd = lax.broadcasted_iota(jnp.int32, (1, 128), 1) % 2 == 1
    return jnp.where(odd, high, rest).reshape(PAIRS, 1, 128), both[:, :1024].reshape(PAIRS, 4, 256)


def table_gradient(near_sums, row_sums):
    both = jnp.concatenate((near_sums.reshape(PAIRS, -1), row_sums.reshape(PAIRS, -1)), axis=1)
    matrix = jnp.asarray(bias_matrices()[1], f32)
    by_pair = jnp.dot(both, matrix, precision=lax.Precision.HIGHEST, preferred_element_type=f32)
    return by_pair.reshape(HEADS, 2 * BUCKETS).T.reshape(-1)


def seq_shift(array, count):
    length = array.shape[0]
    return lax.dynamic_slice_in_dim(jnp.concatenate((array, array), axis=0), count, length, axis=0)


def others_rows(rows, own_last):
    parts = lax.axis_size("seq")
    if parts == 2:
        return lax.ppermute(rows, "seq", [(0, 1)] if own_last else [(0, 1), (1, 0)])
    whole = lax.all_gather(rows, "seq", axis=0, tiled=True)
    step = rows.shape[0]
    start = lax.rem(lax.axis_index("seq") + 1, parts) * step
    return seq_shift(whole, start)[: (parts - 1) * step]


def to_owners(grads, own_last):
    parts = lax.axis_size("seq")
    if parts == 2:
        return lax.ppermute(grads, "seq", [(1, 0)] if own_last else [(0, 1), (1, 0)])
    step = grads.shape[0] // (parts - 1)
    whole = jnp.concatenate((grads, jnp.zeros((step, grads.shape[1]), grads.dtype)), axis=0)
    start = lax.rem(parts - 1 - lax.axis_index("seq"), parts) * step
    return lax.psum_scatter(seq_shift(whole, start), "seq", scatter_dimension=0, tiled=True)


def on_device(
    decoder_in,
    encoder_out,
    dec_lengths,
    pair_flags,
    enc_segments,
    self_proj,
    self_out,
    cross_proj,
    cross_out,
    ffn_in,
    ffn_out,
    norm_gains,
    rel_table,
    out_grad,
):
    shard = self_out.shape[0]
    small = jnp.concatenate((norm_gains, rel_table[None]), axis=0).T
    block_self = jnp.concatenate(
        (self_proj[0], self_proj[1], self_proj[2], self_out, jnp.pad(small, ((0, 0), (0, 124)))),
        axis=1,
    ).astype(bf16)
    block_cross = jnp.concatenate(
        (cross_proj[0], cross_proj[1], cross_proj[2], cross_out), axis=1
    ).astype(bf16)
    own_kernels = (lax.axis_size("dp"), lax.axis_size("seq")) == (16, 2)
    if own_kernels:
        all_self, all_cross = gather_blocks(block_self, block_cross)
        all_self = all_self.reshape(-1, all_self.shape[2])
        all_cross = all_cross.reshape(-1, all_cross.shape[2])
    else:
        all_self = lax.all_gather(block_self, BOTH, axis=0, tiled=True)
        all_cross = lax.all_gather(block_cross, BOTH, axis=0, tiled=True)
    units = FF // D
    ffn_in_here = jnp.swapaxes(ffn_in.reshape(shard, D, units), 1, 2).reshape(shard, FF)
    block_ffn = jnp.concatenate((ffn_in_here, ffn_out.reshape(shard, FF)), axis=1).astype(bf16)
    block_ffn, encoder_out = lax.optimization_barrier((block_ffn, encoder_out, all_cross))[:2]
    all_ffn = lax.all_gather(block_ffn, BOTH, axis=0, tiled=True)
    self_q, self_k, self_v, out_self = (all_self[:, i * D : (i + 1) * D] for i in range(4))
    cross_q, cross_k, cross_v = (all_cross[:, i * D : (i + 1) * D] for i in range(3))
    small_all = all_self[:, 4 * D : 4 * D + 4].T
    gains = small_all[:3].astype(f32)
    far_lanes, near_lines = bias_parts(small_all[3].reshape(2 * BUCKETS, HEADS))

    tokens = decoder_in[0]
    memory = encoder_out[0]
    grad_out = out_grad[0]
    rows, enc_rows = tokens.shape[0], memory.shape[0]
    seq_count = lax.axis_size("seq")
    seq_index = lax.axis_index("seq")
    keys, enc_keys = rows * seq_count, enc_rows * seq_count

    lengths = dec_lengths[0]
    memory_one = jnp.sum((enc_segments[0] < 1).astype(jnp.int32))
    memory_two = jnp.sum((enc_segments[0] < 2).astype(jnp.int32))
    info = jnp.stack(
        (
            seq_index * rows,
            seq_index * enc_rows,
            lengths[0],
            lengths[0] + lengths[1],
            memory_one,
            memory_two,
            pair_flags[0, 0],
            pair_flags[0, 1],
        )
    ).astype(jnp.int32)
    before = others_rows(tokens, True)
    others = others_rows(memory, False)

    scale = 0.125 * LOG2E
    tokens = tokens.astype(f32)
    inverse_one = inverse_rms(tokens)
    normed_one = (tokens * inverse_one * gains[0]).astype(bf16)
    before = before.astype(f32)
    normed_before = (before * inverse_rms(before) * gains[0]).astype(bf16)
    query_one = (mm(normed_one, self_q) * scale).astype(bf16)
    kv_one = mm(normed_one, all_self[:, D : 3 * D]).astype(bf16)
    kv_before = mm(normed_before, all_self[:, D : 3 * D]).astype(bf16)
    parts_one = ((kv_before, 0, PAIRS), (kv_one, 0, PAIRS))
    mixed_one, weights_one, total_one = attend(info, rows, query_one, parts_one, far_lanes, near_lines)
    resid_one = tokens + mm(mixed_one, out_self)
    inverse_two = inverse_rms(resid_one)
    normed_two = (resid_one * inverse_two * gains[1]).astype(bf16)
    query_two = (mm(normed_two, cross_q) * scale).astype(bf16)
    kv_memory = mm(memory, all_cross[:, D : 3 * D]).astype(bf16)
    kv_others = mm(others, all_cross[:, D : 3 * D]).astype(bf16)
    parts_two = ((kv_memory, 0, PAIRS), (kv_others, 0, PAIRS))
    mixed_two, weights_two, total_two = attend(info, rows, query_two, parts_two)
    layer_out, grad_resid, grad_low_two, grad_mixed, grad_ffn = feed_forward(
        resid_one, mixed_two, all_cross, gains[2], grad_out, all_ffn
    )

    grad_query, grad_key, grad_value = attend_back(
        info, query_two, parts_two, weights_two, mixed_two, total_two, grad_mixed, False
    )
    turned = (((0,), (1,)), ((), ()))
    kv_other = mm(grad_key[:, enc_rows:], cross_k, turned)
    kv_other = (kv_other + mm(grad_value[:, enc_rows:], cross_v, turned)).astype(bf16)
    grad_memory = mm(grad_key[:, :enc_rows], cross_k, turned)
    grad_memory = grad_memory + mm(grad_value[:, :enc_rows], cross_v, turned)
    grad_two = (grad_query, grad_key, grad_value)
    grad_normed = mm(grad_query, cross_q, NT)
    grad_resid = grad_resid + norm_back(resid_one, inverse_two, gains[1], grad_normed)
    grad_low = grad_resid.astype(bf16)
    grad_mixed = mm(grad_low, out_self, NT).astype(bf16)
    grad_mixed, kv_other = lax.optimization_barrier((grad_mixed, kv_other))
    grad_query, grad_key, grad_value, near_sums, row_sums = attend_back(
        info, query_one, parts_one, weights_one, mixed_one, total_one, grad_mixed, True
    )
    grad_others = to_owners(kv_other, False)
    split = keys - rows
    grad_before = mm(grad_key[:, :split], self_k, turned) + mm(grad_value[:, :split], self_v, turned)
    grad_before = to_owners(grad_before.astype(bf16), True)
    table_grad = table_gradient(near_sums, row_sums)
    small = jnp.broadcast_to(table_grad[:, None], (D, 128)).astype(bf16)

    def owned(array):
        return lax.psum_scatter(array, BOTH, scatter_dimension=0, tiled=True).astype(f32)

    def projections(block):
        return jnp.stack([block[:, i * D : (i + 1) * D] for i in range(3)], axis=0)

    if own_kernels:
        own_self, own_self_out, own_cross, own_cross_out, own_small = scatter_products(
            (normed_before, normed_one, grad_query, grad_key, grad_value, mixed_one, grad_low),
            (normed_two, grad_two[0], memory, others, grad_two[1], grad_two[2], mixed_two, grad_low_two),
            small.reshape(-1, shard, small.shape[1]),
        )
    else:
        normed_all = jnp.concatenate((normed_before, normed_one), axis=0)
        memory_all = jnp.concatenate((memory, others), axis=0)
        self_grads = (
            mm(normed_one, grad_query, TN),
            mm(normed_all, grad_key, turned),
            mm(normed_all, grad_value, turned),
            mm(mixed_one, grad_low, TN),
        )
        cross_grads = (
            mm(normed_two, grad_two[0], TN),
            mm(memory_all, grad_two[1], turned),
            mm(memory_all, grad_two[2], turned),
            mm(mixed_two, grad_low_two, TN),
        )
        self_grads = jnp.concatenate(self_grads, axis=1).astype(bf16)
        block = owned(jnp.concatenate((self_grads, small), axis=1))
        own_self, own_self_out = projections(block), block[:, 3 * D : 4 * D]
        own_small = block[:, 4 * D :]
        block = owned(jnp.concatenate(cross_grads, axis=1).astype(bf16))
        own_cross, own_cross_out = projections(block), block[:, 3 * D :]

    arrived = lax.optimization_barrier((grad_before, grad_others, own_small))
    grad_before, grad_others, own_small = arrived
    grad_encoder = grad_memory + grad_others.astype(f32)
    grad_normed = mm(grad_key[:, split:], self_k, turned) + mm(grad_value[:, split:], self_v, turned)
    grad_normed = grad_normed + mm(grad_query, self_q, NT) + grad_before.astype(f32)
    grad_input = grad_resid + norm_back(tokens, inverse_one, gains[0], grad_normed)
    own_ffn = owned(grad_ffn)
    own_ffn_in = jnp.swapaxes(own_ffn[:, :FF].reshape(shard, units, D), 1, 2).reshape(shard, FF)
    own_ffn_out = own_ffn[:, FF:].reshape(ffn_out.shape)

    def products(weight, grad):
        return jnp.sum(weight.astype(bf16).astype(f32) * grad, axis=-1)

    gain_grads = jnp.stack(
        (
            jnp.sum(products(self_proj, own_self), axis=0),
            products(cross_proj[0], own_cross[0]),
            products(ffn_in, own_ffn_in),
        ),
        axis=0,
    )
    gain_grads = gain_grads / norm_gains.astype(bf16).astype(f32)

    return (
        layer_out[None],
        grad_input[None],
        grad_encoder[None],
        own_self,
        own_self_out,
        own_cross,
        own_cross_out,
        own_ffn_in,
        own_ffn_out,
        gain_grads,
        own_small[:, 0],
    )


def solution(mesh):
    hidden = P("dp", "seq", None)
    rows_split = P(BOTH, None)
    stacked = P(None, BOTH, None)
    stream = P("dp", None)
    return jax.shard_map(
        on_device,
        mesh=mesh,
        in_specs=(
            hidden,
            hidden,
            stream,
            stream,
            stream,
            stacked,
            rows_split,
            stacked,
            rows_split,
            rows_split,
            rows_split,
            P(None, BOTH),
            P(BOTH),
            hidden,
        ),
        out_specs=(
            hidden,
            hidden,
            hidden,
            stacked,
            rows_split,
            stacked,
            rows_split,
            rows_split,
            rows_split,
            P(None, BOTH),
            P(BOTH),
        ),
        check_vma=False,
    )
```

time: 482 us -> 401 us (0.83)
  matrix products: 103 us -> 50 us
  other arithmetic: 28.3 us -> 18.8 us
  local copies, waits for them, and re-layouts: 31.4 us -> 22.7 us
    pallas_call x1, Pallas kernels: 102 us -> 47.5 us  [gather_blocks(): pl.pallas_call(functools.partial(gather_body, count), in_specs=[any_space...]
    pallas_call x3 -> x4, Pallas kernels: 114 us -> 169 us  [the longest x1 95.3 us: scatter_products(): pl.pallas_call(functools.partial(scatter_body, counts), in_specs=[pl.Bloc...]
    dot_general x30 -> x19, matrix products: 103 us -> 48.7 us  [mm(): return lax.dot_general(a, b, dims, preferred_element_type=f32)]
    reduce_scatter x2 -> x1, waiting for transfers between devices: 20.1 us -> 0.01 us  [owned(): lax.psum_scatter(array, BOTH, scatter_dimension=0, tiled=True).astype(f32)]
    ppermute x2, waiting for transfers between devices: 0.01 us -> 15.5 us  [others_rows(): return lax.ppermute(rows, 'seq', [(0, 1)] if own_last else [(0, 1), (1, 0)])]
    unnamed x132 -> x100, local copies, waits for them, and re-layouts: 18 us -> 9.07 us
    convert_element_type x7 -> x2, other arithmetic: 9.42 us -> 1.77 us  [the longest x1 1.57 us: on_device(): grad_low = grad_resid.astype(bf16)]
    reduce_sum x1 -> x5, other arithmetic: 0.09 us -> 5.1 us  [the longest x1 1.84 us: norm_back(): jnp.mean(grad * unit, axis=-1, keepdims=True)]
  transfers between devices with their start and end apart: 8 -> 6, of which waited for: 1 -> 2; matrix products, arithmetic and copies ran while one was open for 28% -> 18% of each run, Pallas kernels for 56% -> 47%
where the time goes in v3:
time: 401 us; the launch traced here: 394 us
  Pallas kernels  263 us (66%)
  matrix products  50 us (12%)
  local copies, waits for them, and re-layouts  22.7 us (6%)
  other arithmetic  18.8 us (5%)
  between operations  16.5 us (4%)
  waiting for transfers between devices  15.5 us (4%)
  starting transfers between devices  7.67 us (2%)
    pallas_call x1, Pallas kernels, scatter_products(): pl.pallas_call(functools.partial(scatter_body, counts), in_specs=[pl.Bloc...  95.3 us
    dot_general x19, matrix products, mm(): return lax.dot_general(a, b, dims, preferred_element_type=f32)  48.7 us
    pallas_call x1, Pallas kernels, gather_blocks(): pl.pallas_call(functools.partial(gather_body, count), in_specs=[any_space...  47.5 us
    pallas_call x2, Pallas kernels, attend_back(): pl.pallas_call(functools.partial(attend_back_body, rows, keys, causal, st...  46.5 us
    pallas_call x2, Pallas kernels, attend(): pl.pallas_call(functools.partial(attend_body, rows, keys, causal, step, l...  44.2 us
    pallas_call x1, Pallas kernels, feed_forward(): pl.pallas_call(functools.partial(feed_forward_body, rows), grid=(units, 2...  29.1 us
    ppermute x2, waiting for transfers between devices, others_rows(): return lax.ppermute(rows, 'seq', [(0, 1)] if own_last else [(0, 1), (1, 0)])  15.5 us
    unnamed x100, local copies, waits for them, and re-layouts  9.07 us
  transfers between devices with their start and end apart: 6, of which 2 were waited for; matrix products, arithmetic and copies ran while one was open for 18% of the time, Pallas kernels for 47%

profile of v3, /device:TPU:0, one launch (start us, length us, event | category | flops | bytes accessed | tf_op | source)
XLA Modules:
  0.0 393.9 jit_solution(2115346692241564668)
XLA Ops:
  16.1 47.5 %gather_blocks.1 = (bf16[32,24,3200]{2,1,0:T(8,128)(2,1)}, bf16[32,24,3072]{2,1,0:T(8,128)(2,1)}) custom-call(bf16[24,3200]{1,0:T(8,128)(2,1)} %copy-done.27, bf16[24,3072]{1,0:T(8,128)(2,1)} %pad_maximum_fusion.1.refs_1_), custom_call_target="tpu_custom_call" | custom-call | tf_op jit(solution)/shard_map/gather_blocks/pallas_call | solution.py:455
  63.7 2.7 collective-permute-start
  72.4 3.8 stack.35.refs_0_
  76.5 6.6 %convolution_convert_fusion.1.refs_2_.refs_4_ = bf16[1024,1536]{1,0:T(8,128)(2,1)} fusion(bf16[768,3072]{1,0:T(8,128)(2,1)} %bitcast.90, bf16[1,1024,768]{2,1,0:T(8,128)(2,1)} %param.17), kind=kOutput, calls=%fused_computation.1 | convolution fusion | flops 2417491968 | bytes 7077888 | tf_op jit(solution)/shard_map/dot_general | solution.py:33
  83.1 3.2 collective-permute-done
  87.0 2.6 convolution_convert_fusion.2.refs_3_.refs_5_
  89.6 1.7 multiply_convert_fusion.2.refs_1_
  91.3 2.6 convolution_convert_fusion.3.refs_2_.refs_4_
  93.8 21.0 %attend_causal.1 = (bf16[512,768]{1,0:T(8,128)(2,1)}, bf16[12,512,1024]{2,1,0:T(8,128)(2,1)}, f32[512,768]{1,0:T(8,128)}) custom-call(s32[8]{0:T(128)} %stack.35.refs_0_, bf16[512,768]{1,0:T(8,128)(2,1)} %multiply_convert_fusion.2.refs_1_, bf16[512,1536]{1,0:T(8,128)(2,1)} %convolution_convert_fusion.3.refs_2_.refs_4_, ...), custom_call_target="tpu_custom_call" | custom-call | tf_op jit(solution)/shard_map/attend_causal/pallas_call | solution.py:183
  114.9 2.4 multiply_reduce_fusion.2
  117.5 1.7 multiply_convert_fusion.refs_1_
  119.2 12.3 %collective-permute-done.1.refs_10_ = bf16[1024,768]{1,0:T(8,128)(2,1)} collective-permute-done((bf16[1024,768]{1,0:T(8,128)(2,1)}, bf16[1024,768]{1,0:T(8,128)(2,1)}, u32[]{:S(2)}, u32[]{:S(2)}) %collective-permute-start.1) | collective-permute-done | bytes 1572896 | tf_op jit(solution)/shard_map/ppermute | solution.py:918
  131.5 5.5 %convolution_convert_fusion.refs_3_.refs_5_ = bf16[1024,1536]{1,0:T(8,128)(2,1)} fusion(bf16[1024,768]{1,0:T(8,128)(2,1)} %collective-permute-done.1.refs_10_, bf16[768,3072]{1,0:T(8,128)(2,1)S(1)} %bitcast.96), kind=kOutput, calls=%fused_computation | convolution fusion | flops 2417491968 | bytes 7077888 | tf_op jit(solution)/shard_map/dot_general | solution.py:33
  137.1 23.2 %attend_cross.1 = (bf16[512,768]{1,0:T(8,128)(2,1)}, bf16[12,512,2048]{2,1,0:T(8,128)(2,1)}, f32[512,768]{1,0:T(8,128)}) custom-call(s32[8]{0:T(128)} %stack.35.refs_0_, bf16[512,768]{1,0:T(8,128)(2,1)} %multiply_convert_fusion.refs_1_, bf16[1024,1536]{1,0:T(8,128)(2,1)} %convolution_convert_fusion.1.refs_2_.refs_4_, ...), custom_call_target="tpu_custom_call" | custom-call | tf_op jit(solution)/shard_map/attend_cross/pallas_call | solution.py:183
  161.4 29.1 %feed_forward.1 = (bf16[512,768]{1,0:T(8,128)(2,1)}, f32[512,768]{1,0:T(8,128)S(1)}, bf16[512,768]{1,0:T(8,128)(2,1)S(1)}, bf16[512,768]{1,0:T(8,128)(2,1)S(1)}, bf16[768,6144]{1,0:T(8,128)(2,1)}) custom-call(f32[512,768]{1,0:T(8,128)} %copy-done.4, bf16[512,768]{1,0:T(8,128)(2,1)S(1)} %copy-done, bf16[768,3072]{1,0:T(8,128)(2,1)} %bitcast.91, ...), custom_call_target="tpu_custom_call" | custom-call | tf_op jit(solution)/shard_map/feed_forward/pallas_call | solution.py:833
  192.3 27.1 %attend_cross_back.1 = (bf16[512,768]{1,0:T(8,128)(2,1)}, bf16[768,2048]{1,0:T(8,128)(2,1)}, bf16[768,2048]{1,0:T(8,128)(2,1)}) custom-call(s32[8]{0:T(128)} %stack.35.refs_0_, bf16[512,768]{1,0:T(8,128)(2,1)} %multiply_convert_fusion.refs_1_, bf16[1024,1536]{1,0:T(8,128)(2,1)} %convolution_convert_fusion.1.refs_2_.refs_4_, ...), custom_call_target="tpu_custom_call" | custom-call | tf_op jit(solution)/shard_map/attend_cross_back/pallas_call | solution.py:294
  219.5 2.7 multiply_reduce_fusion.1
  222.2 1.6 fusion.58
  223.8 3.4 convolution_convert_fusion.4.refs_9_
  229.2 2.6 add_convert_fusion
  231.8 19.4 %attend_causal_back.1 = (bf16[512,768]{1,0:T(8,128)(2,1)}, bf16[768,1024]{1,0:T(8,128)(2,1)}, bf16[768,1024]{1,0:T(8,128)(2,1)}, f32[6,4,256]{2,1,0:T(4,128)}, f32[6,4,128]{2,1,0:T(4,128)}) custom-call(s32[8]{0:T(128)} %stack.35.refs_0_, bf16[512,768]{1,0:T(8,128)(2,1)} %multiply_convert_fusion.2.refs_1_, ...), custom_call_target="tpu_custom_call" | custom-call | tf_op jit(solution)/shard_map/attend_causal_back/pallas_call | solution.py:294
  253.6 2.5 fusion.28
  256.1 3.0 add_convert_fusion.1
  260.4 3.5 collective-permute-start.3
  264.8 95.3 %scatter_products.1 = (f32[3,24,768]{2,1,0:T(8,128)}, f32[24,768]{1,0:T(8,128)}, f32[3,24,768]{2,1,0:T(8,128)}, f32[24,768]{1,0:T(8,128)}, f32[24,128]{1,0:T(8,128)}) custom-call(bf16[512,768]{1,0:T(8,128)(2,1)} %copy-done.11, bf16[512,768]{1,0:T(8,128)(2,1)} %copy-done.12, bf16[512,768]{1,0:T(8,128)(2,1)} %get-tuple-element.63.refs_2_, ...), custom_call_target="tpu_custom_call" | custom-call | tf_op jit(solution)/shard_map/scatter_products/pallas_call | solution.py:732
  360.1 2.5 fusion.40
  363.7 2.2 fusion.26
  366.0 2.3 fusion.30
  369.3 1.5 fusion.19
  373.3 1.8 fusion.11
  375.1 1.5 fusion.15
  376.7 2.3 add_bitcast_fusion
  (171 shorter events, 36.4 us)
Async XLA Ops:
  7.2 6.4 %copy-start.25 = (f32[24,3072]{1,0:T(8,128)S(1)}, f32[24,3072]{1,0:T(8,128)}, u32[]{:S(2)}) copy-start(f32[24,3072]{1,0:T(8,128)} %param.25) | copy-start | bytes 884740
  7.2 153.1 %all-gather.2.cloned.1.call-start = ((), (), s32[]{:S(2)}) async-start(), calls=%async_computation.1 | async-start | bytes 9732096 | tf_op jit(solution)/shard_map/all_gather | solution.py:972
  14.0 53.4 %copy-start.7 = (bf16[24,3072]{0,1:T(8,128)(2,1)}, bf16[24,3072]{0,1:T(8,128)(2,1)S(1)}, u32[]{:S(2)}) copy-start(bf16[24,3072]{0,1:T(8,128)(2,1)S(1)} %copy.55) | copy-start | bytes 442372
  14.0 49.7 %copy-start.6 = (bf16[1,512,768]{2,1,0:T(8,128)(2,1)S(1)}, bf16[1,512,768]{2,1,0:T(8,128)(2,1)}, u32[]{:S(2)}) copy-start(bf16[1,512,768]{2,1,0:T(8,128)(2,1)} %param.16) | copy-start | bytes 2359300
  14.0 53.9 %copy-start.24 = (bf16[128,1152]{1,0:T(8,128)(2,1)S(1)}, bf16[128,1152]{1,0:T(8,128)(2,1)}, u32[]{:S(2)}) copy-start(bf16[128,1152]{1,0:T(8,128)(2,1)} %constant.50.clone) | copy-start | bytes 884740
  14.6 54.7 %copy-start.34 = (s32[1,2]{1,0:T(1,128)S(1)}, s32[1,2]{1,0:T(1,128)}, u32[]{:S(2)}) copy-start(s32[1,2]{1,0:T(1,128)} %param.18) | copy-start | bytes 28
  14.6 56.6 %copy-start.35 = (s32[1,2]{1,0:T(1,128)S(1)}, s32[1,2]{1,0:T(1,128)}, u32[]{:S(2)}) copy-start(s32[1,2]{1,0:T(1,128)} %param.19) | copy-start | bytes 28
  14.6 57.2 %copy-start.32 = (s32[1,2048]{1,0:T(1,128)S(1)}, s32[1,2048]{1,0:T(1,128)}, u32[]{:S(2)}) copy-start(s32[1,2048]{1,0:T(1,128)} %param.20) | copy-start | bytes 24580
  63.6 315.3 %reduce-scatter.2.cloned.1.call-start = ((), (), s32[]{:S(2)}) async-start(), calls=%async_computation.2 | async-start | bytes 9732096 | tf_op jit(solution)/shard_map/reduce_scatter | solution.py:1053
  63.7 22.6 %collective-permute-start = (bf16[512,768]{1,0:T(8,128)(2,1)S(1)}, bf16[512,768]{1,0:T(8,128)(2,1)S(1)}, u32[]{:S(2)}, u32[]{:S(2)}) collective-permute-start(bf16[512,768]{1,0:T(8,128)(2,1)S(1)} %bitcast.89), channel_id=1, source_target_pairs={{0,1},{2,3},{4,5},{6,7},{8,9},{10,11},{12,13},{14,15},{16,17},{18,... | collective-permute-start | bytes 2359304 | tf_op jit(solution)/shard_map/ppermute | solution.py:918
  66.4 65.2 %collective-permute-start.1 = (bf16[1024,768]{1,0:T(8,128)(2,1)}, bf16[1024,768]{1,0:T(8,128)(2,1)}, u32[]{:S(2)}, u32[]{:S(2)}) collective-permute-start(bf16[1024,768]{1,0:T(8,128)(2,1)} %bitcast.106), channel_id=1, source_target_pairs={{0,1},{1,0},{2,3},{3,2},{4,5},{5,4},{6,7},{7,6},{8,9},{9,8},{10,11... | collective-permute-start | bytes 4718600 | tf_op jit(solution)/shard_map/ppermute | solution.py:918
  76.2 10.7 %slice-start.6 = ((s8[4915200]{0:T(1024)(128)(4,1)}), s8[4194304]{0:T(1024)(128)(4,1)S(1)}, s32[]{:S(2)}) async-start(s8[4915200]{0:T(1024)(128)(4,1)} %bitcast.126), calls=%async_computation.9 | async-start | bytes 8388608
  76.5 10.5 %slice-start.7 = ((s8[4915200]{0:T(1024)(128)(4,1)}), s8[720896]{0:T(1024)(128)(4,1)S(1)}, s32[]{:S(2)}) async-start(s8[4915200]{0:T(1024)(128)(4,1)} %bitcast.126), calls=%async_computation.10 | async-start | bytes 1441792
  87.0 4.3 %copy-start.11 = (bf16[512,768]{1,0:T(8,128)(2,1)}, bf16[512,768]{1,0:T(8,128)(2,1)S(1)}, u32[]{:S(2)}) copy-start(bf16[512,768]{1,0:T(8,128)(2,1)S(1)} %get-tuple-element.123.refs_0_) | copy-start | bytes 2359300
  91.3 26.2 %slice-start = ((s8[4718592]{0:T(1024)(128)(4,1)}), s8[4194304]{0:T(1024)(128)(4,1)S(1)}, s32[]{:S(2)}) async-start(s8[4718592]{0:T(1024)(128)(4,1)} %bitcast.93), calls=%async_computation.3 | async-start | bytes 8388608
  93.8 23.7 %slice-start.1 = ((s8[4718592]{0:T(1024)(128)(4,1)}), s8[524288]{0:T(1024)(128)(4,1)S(1)}, s32[]{:S(2)}) async-start(s8[4718592]{0:T(1024)(128)(4,1)} %bitcast.93), calls=%async_computation.4 | async-start | bytes 1048576
  137.1 23.2 %copy-start.1 = (bf16[1,512,768]{2,1,0:T(8,128)(2,1)S(1)}, bf16[1,512,768]{2,1,0:T(8,128)(2,1)}, u32[]{:S(2)}) copy-start(bf16[1,512,768]{2,1,0:T(8,128)(2,1)} %param.29) | copy-start | bytes 2359300
  192.3 27.2 %copy-start.5 = (f32[512,768]{1,0:T(8,128)S(1)}, f32[512,768]{1,0:T(8,128)}, u32[]{:S(2)}) copy-start(f32[512,768]{1,0:T(8,128)} %copy-done.4) | copy-start | bytes 4718596
  219.5 7.7 %slice-start.2 = ((s8[4718592]{0:T(1024)(128)(4,1)}), s8[4194304]{0:T(1024)(128)(4,1)S(1)}, s32[]{:S(2)}) async-start(s8[4718592]{0:T(1024)(128)(4,1)} %bitcast.97), calls=%async_computation.5 | async-start | bytes 8388608
  222.2 5.0 %slice-start.3 = ((s8[4718592]{0:T(1024)(128)(4,1)}), s8[524288]{0:T(1024)(128)(4,1)S(1)}, s32[]{:S(2)}) async-start(s8[4718592]{0:T(1024)(128)(4,1)} %bitcast.97), calls=%async_computation.6 | async-start | bytes 1048576
  223.8 3.4 copy-start.10
  223.8 3.4 copy-start.16
  231.8 20.1 %copy-start.22 = (f32[1024,128]{1,0:T(8,128)S(1)}, f32[1024,128]{1,0:T(8,128)}, u32[]{:S(2)}) copy-start(f32[1024,128]{1,0:T(8,128)} %constant.67) | copy-start | bytes 1572868
  231.8 20.5 %copy-start.26 = (f32[512,128]{1,0:T(8,128)S(1)}, f32[512,128]{1,0:T(8,128)}, u32[]{:S(2)}) copy-start(f32[512,128]{1,0:T(8,128)} %constant.68) | copy-start | bytes 786436
  259.1 113.6 %collective-permute-start.2 = (bf16[512,768]{1,0:T(8,128)(2,1)}, bf16[512,768]{1,0:T(8,128)(2,1)}, u32[]{:S(2)}, u32[]{:S(2)}) collective-permute-start(bf16[512,768]{1,0:T(8,128)(2,1)} %add_convert_fusion.1), channel_id=1, source_target_pairs={{1,0},{3,2},{5,4},{7,6},{9,8},{11,10},{13,12},{15,14},{17,16},{19,... | collective-permute-start | bytes 2359304 | tf_op jit(solution)/shard_map/ppermute | solution.py:928
  260.4 112.3 %collective-permute-start.3 = (bf16[1024,768]{1,0:T(8,128)(2,1)}, bf16[1024,768]{1,0:T(8,128)(2,1)S(1)}, u32[]{:S(2)}, u32[]{:S(2)}) collective-permute-start(bf16[1024,768]{1,0:T(8,128)(2,1)} %add_convert_fusion), channel_id=1, source_target_pairs={{0,1},{1,0},{2,3},{3,2},{4,5},{5,4},{6,7},{7,6},{8,9},{9,8},{10,11... | collective-permute-start | bytes 4718600 | tf_op jit(solution)/shard_map/ppermute | solution.py:928
  264.8 98.9 %copy-start.20 = (bf16[768,1024]{1,0:T(8,128)(2,1)S(1)}, bf16[768,1024]{1,0:T(8,128)(2,1)}, u32[]{:S(2)}) copy-start(bf16[768,1024]{1,0:T(8,128)(2,1)} %get-tuple-element.62.refs_4_) | copy-start | bytes 4718596
  360.0 9.2 %slice-start.4 = ((s8[4718592]{0:T(1024)(128)(4,1)}), s8[4194304]{0:T(1024)(128)(4,1)S(1)}, s32[]{:S(2)}) async-start(s8[4718592]{0:T(1024)(128)(4,1)} %bitcast.101), calls=%async_computation.7 | async-start | bytes 8388608
  363.7 5.6 %slice-start.5 = ((s8[4718592]{0:T(1024)(128)(4,1)}), s8[524288]{0:T(1024)(128)(4,1)S(1)}, s32[]{:S(2)}) async-start(s8[4718592]{0:T(1024)(128)(4,1)} %bitcast.101), calls=%async_computation.8 | async-start | bytes 1048576
  366.0 3.3 copy-start.17
  381.4 3.9 copy-start.23
  381.4 4.6 %copy-start.29 = (f32[24,768]{1,0:T(8,128)S(1)}, f32[24,768]{1,0:T(8,128)}, u32[]{:S(2)}) copy-start(f32[24,768]{1,0:T(8,128)} %get-tuple-element.151) | copy-start | bytes 221188
  (18 other events, 34.7 us)
Sparse Core Ops, SparseCore 0:
  63.7 85.2 all-gather.1
  192.4 160.8 reduce-scatter.1

commit v4 on v3

--- a/solution.py
+++ b/solution.py
@@ -33,6 +33,16 @@
     return lax.dot_general(a, b, dims, preferred_element_type=f32)
 
 
+def inverse_rms(values):
+    return lax.rsqrt(jnp.mean(values * values, axis=-1, keepdims=True) + epsilon)
+
+
+def norm_back(values, inverse, gain, grad):
+    unit = values * inverse
+    grad = grad * gain
+    return inverse * (grad - unit * jnp.mean(grad * unit, axis=-1, keepdims=True))
+
+
 def head_lanes(which):
     low = lax.broadcasted_iota(jnp.int32, (1, 128), 1) < HDIM
     return low if which == 0 else jnp.logical_not(low)
@@ -65,54 +75,62 @@
     return jnp.sum(tile, axis=0, keepdims=True)
 
 
-ROW, MEMORY_ROW, END_ONE, END_TWO, MEMORY_ONE, MEMORY_TWO, FLAG_ONE, FLAG_TWO = range(8)
-
-
 def pairs_between(place, end_one, end_two):
     return (place >= end_one).astype(jnp.int32) + (place >= end_two).astype(jnp.int32)
 
 
-def flagged(info, first, count, width):
-    place = lax.broadcasted_iota(jnp.int32, (count, width), 0) + (info[ROW] + first)
-    pair = pairs_between(place, info[END_ONE], info[END_TWO])
-    return jnp.where(pair == 0, info[FLAG_ONE], jnp.where(pair == 1, info[FLAG_TWO], 0)) > 0
-
-
-def extra_columns(info, rows, keys, causal, query_extra, key_extra):
+def decoder_pairs(lengths, place):
+    return pairs_between(place, lengths[0, 0], lengths[0, 0] + lengths[0, 1])
+
+
+def flagged(numbers, rows, first, count, width):
+    lengths, flags = numbers
+    place = lax.broadcasted_iota(jnp.int32, (count, width), 0)
+    pair = decoder_pairs(lengths, place + (lax.axis_index("seq") * rows + first))
+    return jnp.where(pair == 0, flags[0, 0], jnp.where(pair == 1, flags[0, 1], 0)) > 0
+
+
+def extra_columns(numbers, rows, keys, segments, query_extra, key_extra):
+    lengths = numbers[0]
+    here = lax.axis_index("seq") * rows
     lane = lax.broadcasted_iota(jnp.int32, (rows, 128), 1) & (HDIM - 1)
-    place = lax.broadcasted_iota(jnp.int32, (rows, 128), 0) + info[ROW]
-    pair = pairs_between(place, info[END_ONE], info[END_TWO])
-    flag = flagged(info, 0, rows, 128).astype(jnp.int32)
+    pair = decoder_pairs(lengths, lax.broadcasted_iota(jnp.int32, (rows, 128), 0) + here)
+    flag = flagged(numbers, rows, 0, rows, 128).astype(jnp.int32)
     wanted = jnp.where(lane < 3, pair, (flag << 1) + 3)
     chosen = jnp.where(lane < 3, lane, ((lane - 3) & ~1) + 3)
-    here = jnp.logical_and(wanted == chosen, lane < 7)
-    query_extra[...] = jnp.where(here, 1.0, 0.0).astype(bf16)
+    fits = jnp.logical_and(wanted == chosen, lane < 7)
+    query_extra[...] = jnp.where(fits, 1.0, 0.0).astype(bf16)
     lane = lax.broadcasted_iota(jnp.int32, (keys, 128), 1) & (HDIM - 1)
     place = lax.broadcasted_iota(jnp.int32, (keys, 128), 0)
-    if causal:
-        place = place + (info[ROW] + rows - keys)
-        pair = pairs_between(place, info[END_ONE], info[END_TWO])
-        pair = jnp.where(place < 0, 3, pair)
+    if segments is None:
+        place = place + (here + rows - keys)
+        pair = jnp.where(place < 0, 3, decoder_pairs(lengths, place))
     else:
-        place = place + info[MEMORY_ROW]
+        place = place + lax.axis_index("seq") * (keys // lax.axis_size("seq"))
         place = jnp.where(place >= keys, place - keys, place)
-        pair = pairs_between(place, info[MEMORY_ONE], info[MEMORY_TWO])
+
+        def below(pair):
+            count = jnp.sum((segments[...] < pair).astype(f32), axis=0, keepdims=True)
+            return jnp.sum(count, axis=1, keepdims=True).astype(jnp.int32)
+
+        pair = pairs_between(place, below(1), below(2))
     wrong = jnp.logical_and(pair != lane, lane < 3)
     key_extra[...] = jnp.where(wrong, neg_large, 0.0).astype(bf16)
 
 
 def attend_body(rows, keys, causal, step, parts, *refs):
-    info, q_ref = refs[:2]
-    key_refs, value_refs = refs[2 : 2 + parts], refs[2 + parts : 2 + 2 * parts]
+    numbers, q_ref = refs[:2], refs[2]
+    key_refs, value_refs = refs[3 : 3 + parts], refs[3 + parts : 3 + 2 * parts]
     o_ref, e_ref, inv_ref, query_extra, key_extra = refs[-5:]
 
     @pl.when(pl.program_id(0) == 0)
     def _():
-        extra_columns(info, rows, keys, causal, query_extra, key_extra)
+        segments = None if causal else refs[3 + 2 * parts]
+        extra_columns(numbers, rows, keys, segments, query_extra, key_extra)
 
     extra = key_extra[...]
     if causal:
-        far_ref, near_ref = refs[2 + 2 * parts : 4 + 2 * parts]
+        far_ref, near_ref = refs[3 + 2 * parts : 5 + 2 * parts]
         extra = extra + far_ref[0]
     key_pair = jnp.concatenate([ref[...] for ref in key_refs], axis=0)
     value_pair = jnp.concatenate([ref[...] for ref in value_refs], axis=0)
@@ -130,7 +148,7 @@
             scores = mm(query, key_head[:width], NT)
             if causal:
                 cut = width - 256
-                flag = flagged(info, here.start, step, 1)
+                flag = flagged(numbers, rows, here.start, step, 1)
                 near = scores[:, cut:] + jnp.where(flag, tile_one, tile_zero)
                 far = scores[:, :cut]
                 peak = jnp.maximum(
@@ -160,9 +178,9 @@
     return pl.BlockSpec((rows, 128), lambda p: (0, first + p))
 
 
-def operands_of(info, query, parts):
-    arrays = [info, query] + [part[0] for part in parts] * 2
-    specs = [pl.BlockSpec(memory_space=pltpu.SMEM), pair_columns(query.shape[0])]
+def operands_of(numbers, query, parts):
+    arrays = [*numbers, query] + [part[0] for part in parts] * 2
+    specs = [pl.BlockSpec(memory_space=pltpu.SMEM)] * 2 + [pair_columns(query.shape[0])]
     for place in (1, 2):
         specs += [pair_columns(part[0].shape[0], part[place]) for part in parts]
     return arrays, specs
@@ -172,14 +190,17 @@
     return pl.BlockSpec((1, height, width), lambda p: (p, 0, 0))
 
 
-def attend(info, rows, query, parts, far=None, near=None):
+def attend(numbers, rows, query, parts, segments=None, far=None, near=None):
     keys = sum(part[0].shape[0] for part in parts)
     causal = far is not None
     step = 128 if causal else min(256, rows)
-    operands, specs = operands_of(info, query, parts)
+    operands, specs = operands_of(numbers, query, parts)
     if causal:
         operands += [far, near]
         specs += [per_pair(1, 128), per_pair(4, 256)]
+    else:
+        operands.append(segments)
+        specs.append(pl.BlockSpec(segments.shape, lambda p: (0, 0)))
     return pl.pallas_call(
         functools.partial(attend_body, rows, keys, causal, step, len(parts)),
         grid=(PAIRS,),
@@ -201,13 +222,14 @@
 
 
 def attend_back_body(rows, keys, causal, step, parts, *refs):
-    info, q_ref = refs[:2]
-    key_refs, value_refs = refs[2 : 2 + parts], refs[2 + parts : 2 + 2 * parts]
-    e_ref, o_ref, inv_ref, d_ref = refs[2 + 2 * parts : 6 + 2 * parts]
+    numbers, q_ref = refs[:2], refs[2]
+    refs = refs[3:]
+    key_refs, value_refs = refs[:parts], refs[parts : 2 * parts]
+    e_ref, o_ref, inv_ref, d_ref = refs[2 * parts : 4 + 2 * parts]
     if causal:
-        dq_ref, dk_ref, dv_ref, near_ref, sum_ref, ds_ref = refs[6 + 2 * parts :]
+        dq_ref, dk_ref, dv_ref, near_ref, sum_ref, ds_ref = refs[4 + 2 * parts :]
     else:
-        dq_ref, dk_ref, dv_ref, ds_ref = refs[6 + 2 * parts :]
+        dq_ref, dk_ref, dv_ref, ds_ref = refs[4 + 2 * parts :]
     lane = lax.broadcasted_iota(jnp.int32, (1, 128), 1)
     key_pair = jnp.concatenate([ref[...] for ref in key_refs], axis=0)
     value_pair = jnp.concatenate([ref[...] for ref in value_refs], axis=0)
@@ -239,7 +261,7 @@
             if causal:
                 near = grad_scores[:, width - 256 :]
                 near_all = near_all + near
-                flag = flagged(info, here.start, step, 1)
+                flag = flagged(numbers, rows, here.start, step, 1)
                 near_one = near_one + jnp.where(flag, near, 0.0)
             grad_scores = grad_scores.astype(bf16)
             ds_ref[here, :width] = grad_scores
@@ -266,7 +288,7 @@
         both = jnp.where(low, query_parts[0][index], query_parts[1][index])
         dq_ref[here] = (both * 0.125).astype(dq_ref.dtype)
     if causal:
-        flags = flagged(info, 0, rows, 1)
+        flags = flagged(numbers, rows, 0, rows, 1)
         for which in (0, 1):
             whole = jnp.concatenate(query_parts[which], axis=0)
             one = jnp.sum(jnp.where(flags, whole, 0.0), axis=0, keepdims=True)
@@ -275,10 +297,10 @@
             sum_ref[0, 2 * which + 1 : 2 * which + 2, :] = one
 
 
-def attend_back(info, query, parts, weights, mixed, inverse, grad_mixed, causal):
+def attend_back(numbers, query, parts, weights, mixed, inverse, grad_mixed, causal):
     rows, keys = weights.shape[1:]
     step = 128 if causal else min(256, rows)
-    operands, specs = operands_of(info, query, parts)
+    operands, specs = operands_of(numbers, query, parts)
     operands += [weights, mixed, inverse, grad_mixed]
     specs += [pl.BlockSpec((2, rows, keys), lambda p: (p, 0, 0))] + [pair_columns(rows)] * 3
     turned = jax.ShapeDtypeStruct((D, keys), bf16)
@@ -337,9 +359,32 @@
     pl.semaphore_wait(barrier, 4 + ((z + 1) // 2) % 2)
 
 
-def gather_body(count, *refs):
-    sources, wholes = refs[:count], refs[count : 2 * count]
-    own_sems, up_sems, down_sems, side_sems, turn_sems, mate_sems, recv_sems = refs[2 * count :]
+def unit_order():
+    place = np.arange(512)
+    return (place[:, None] == (place % 128) * 4 + place // 128).astype(np.float32)
+
+
+def gather_body(*refs):
+    masters, refs = refs[:9], refs[9:]
+    wholes, pair_whole = refs[:2], refs[2]
+    sources, pair_source = refs[3:5], refs[5]
+    own_sems, up_sems, down_sems, side_sems, turn_sems, mate_sems, recv_sems, pair_sems = refs[6:]
+    self_proj, self_out, cross_proj, cross_out, ffn_in, ffn_out, norm_gains, table, order = masters
+    count = 2
+    shard = self_out.shape[0]
+    for stacked, single, source in ((self_proj, self_out, sources[0]), (cross_proj, cross_out, sources[1])):
+        for j in range(3):
+            source[:, j * D : (j + 1) * D] = stacked[j].astype(bf16)
+        source[:, 3 * D : 4 * D] = single[...].astype(bf16)
+    lane = lax.broadcasted_iota(jnp.int32, (shard, 128), 1)
+    row = lax.broadcasted_iota(jnp.int32, (shard, shard), 0)
+    same = row == lax.broadcasted_iota(jnp.int32, (shard, shard), 1)
+    small = jnp.zeros((shard, 128), f32)
+    for j in range(4):
+        line = norm_gains[j : j + 1] if j < 3 else table[...]
+        column = jnp.sum(jnp.where(same, jnp.broadcast_to(line, same.shape), 0.0), axis=1, keepdims=True)
+        small = jnp.where(lane == j, column, small)
+    sources[0][:, 4 * D :] = small.astype(bf16)
     z, x, core, y = place_here()
     mate = device_of(z, x, 1 - core, y)
     me = block_of(z, x, core, y)
@@ -408,10 +453,33 @@
     own = [
         pltpu.make_async_copy(sources[i], wholes[i].at[me], own_sems.at[i]) for i in range(count)
     ]
+    own.append(pltpu.make_async_copy(pair_source, pair_whole.at[y], pair_sems.at[0]))
+    pair = pltpu.make_async_remote_copy(
+        src_ref=pair_source,
+        dst_ref=pair_whole.at[y],
+        send_sem=pair_sems.at[1],
+        recv_sem=pair_sems.at[2],
+        device_id=device_of(z, x, core, 1 - y),
+        device_id_type=MESH,
+    )
     for which in range(count):
         onwards(which, 0, True, 0, 0, sources[which])
-    for copy in own:
+    for copy in own[:count]:
         copy.start()
+    units = FF // D
+    for m in range(FF // 512):
+        piece = mm(ffn_in[:, 512 * m : 512 * (m + 1)].astype(bf16), order[...]).astype(bf16)
+        for b in range(units):
+            first = b * D + 128 * m
+            pair_source[:, first : first + 128] = piece[:, 128 * b : 128 * (b + 1)]
+    row = lax.broadcasted_iota(jnp.int32, (shard, units * shard), 0) * units
+    place = lax.broadcasted_iota(jnp.int32, (shard, units * shard), 1)
+    held = ffn_out[...].astype(bf16)
+    for b in range(units):
+        rows = mm(jnp.where(row + b == place, 1.0, 0.0).astype(bf16), held)
+        pair_source[:, FF + b * D : FF + (b + 1) * D] = rows.astype(bf16)
+    own[count].start()
+    pair.start()
     waves = [[] for _ in range(6)]
     for side in (0, 1):
         for turn in (0, 1):
@@ -446,29 +514,39 @@
                         when(exists(far, up), finish)
     for copy in own:
         copy.wait()
-
-
-def gather_blocks(*blocks):
-    count = len(blocks)
-    any_space = pl.BlockSpec(memory_space=pl.ANY)
+    pair.wait_send()
+    came = pair_whole.at[1 - y]
+    pltpu.make_async_copy(came, came, pair_sems.at[2]).wait()
+
+
+def gather_blocks(self_proj, self_out, cross_proj, cross_out, ffn_in, ffn_out, norm_gains, rel_table):
+    shard = self_out.shape[0]
+    shapes = [(shard, 4 * D + 128), (shard, 4 * D)]
+    pair = (shard, 2 * FF)
     dma = pltpu.SemaphoreType.DMA
     return pl.pallas_call(
-        functools.partial(gather_body, count),
-        in_specs=[any_space] * count,
-        out_specs=[any_space] * count,
-        out_shape=[jax.ShapeDtypeStruct((32, *block.shape), block.dtype) for block in blocks],
-        scratch_shapes=[
-            dma((count,)),
-            dma((count, 4)),
-            dma((count, 4)),
-            dma((count, 7)),
-            dma((count, 14)),
-            dma((count, 28)),
-            dma((count, 32)),
-        ],
+        gather_body,
+        in_specs=[pl.BlockSpec(memory_space=pltpu.VMEM)] * 9,
+        out_specs=[pl.BlockSpec(memory_space=pl.ANY)] * 3,
+        out_shape=[jax.ShapeDtypeStruct((32, *shape), bf16) for shape in shapes]
+        + [jax.ShapeDtypeStruct((2, *pair), bf16)],
+        scratch_shapes=[pltpu.VMEM(shape, bf16) for shape in (*shapes, pair)]
+        + [dma((3,))]
+        + [dma((2, n)) for n in (4, 4, 7, 14, 28, 32)]
+        + [dma((3,))],
         compiler_params=pltpu.CompilerParams(collective_id=0, has_side_effects=True),
         name="gather_blocks",
-    )(*blocks)
+    )(
+        self_proj,
+        self_out,
+        cross_proj,
+        cross_out,
+        ffn_in,
+        ffn_out,
+        norm_gains,
+        rel_table[None],
+        jnp.asarray(unit_order(), bf16),
+    )
 
 
 SELF_PRODUCTS = (((1,), 2, False), ((0, 1), 3, True), ((0, 1), 4, True), ((5,), 6, False))
@@ -477,13 +555,16 @@
 
 def scatter_body(counts, *refs):
     total_in = sum(counts)
-    arrays, small, outs = refs[:total_in], refs[total_in], refs[total_in + 1 : total_in + 6]
-    refs = refs[total_in + 6 :]
+    arrays, small = refs[:total_in], refs[total_in]
+    weights_ref, tokens_ref, resid_ref, gain_ref = refs[total_in + 1 : total_in + 5]
+    refs = refs[total_in + 5 :]
+    outs, grad_ref, refs = refs[:5], refs[5], refs[6:]
     held, small_held = refs[:total_in], refs[total_in]
     refs = refs[total_in + 1 :]
     parts, mate_in, first_in, second_in, line_in = (refs[2 * i : 2 * i + 2] for i in range(5))
     load_sems, mate_sems, first_sems, second_sems, line_sems = refs[10:15]
-    mate_recv, first_recv, second_recv, line_recv = refs[15:]
+    mate_recv, first_recv, second_recv, line_recv = refs[15:19]
+    back_in, back_sems, late_sems = refs[19:]
     z, x, core, y = place_here()
     loads = [
         pltpu.make_async_copy(source, target, load_sems.at[i])
@@ -495,15 +576,17 @@
     half = z // 2
     order = (3 - 3 * half, 2 - half, 1 - z + 4 * half, z)
 
-    def near(first, second):
-        return (x + first) % 2, (y + second) % 2
-
-    def block(i, first, second, other_core=0):
-        bx, by = near(first, second)
+    def near(which, first, second):
+        if which == 0:
+            return (x + first) % 2, (y + second) % 2
+        return (x + second) % 2, (y + first) % 2
+
+    def block(which, i, first, second, other_core=0):
+        bx, by = near(which, first, second)
         return block_of(order[i], bx, (core + other_core) % 2, by)
 
-    def slot_of(i, first, second):
-        bx, by = near(first, second)
+    def slot_of(which, i, first, second):
+        bx, by = near(which, first, second)
         return (order[i] * 2 + bx) * 2 + by
 
     def remote(source, target, send_sem, recv_sem, device):
@@ -517,9 +600,9 @@
         )
 
     def to_mate(which, i, first, second):
-        slot = slot_of(i, first, second)
+        slot = slot_of(which, i, first, second)
         return remote(
-            parts[which].at[block(i, first, second, 1)],
+            parts[which].at[block(which, i, first, second, 1)],
             mate_in[which].at[slot],
             mate_sems.at[which, slot],
             mate_recv.at[which, slot],
@@ -527,9 +610,9 @@
         )
 
     def to_first(which, i, second):
-        bx, by = near(1, 0)
+        bx, by = near(which, 1, 0)
         return remote(
-            parts[which].at[block(i, 1, second)],
+            parts[which].at[block(which, i, 1, second)],
             first_in[which].at[2 * i + second],
             first_sems.at[which, 2 * i + second],
             first_recv.at[which, 2 * i + second],
@@ -537,21 +620,24 @@
         )
 
     def to_second(which, i):
-        bx, by = near(0, 1)
+        bx, by = near(which, 0, 1)
         return remote(
-            parts[which].at[block(i, 0, 1)],
+            parts[which].at[block(which, i, 0, 1)],
             second_in[which].at[i],
             second_sems.at[which, i],
             second_recv.at[which, i],
             device_of(z, bx, core, by),
         )
 
+    def line_slot(which, came, at_z, second):
+        return (came * 4 + at_z) * 2 + second if which == 0 else came * 4 + at_z
+
     def along_line(which, i, second=0):
         step = 1 - 2 * half if i < 2 else 1 - 2 * (z % 2)
         came = (1 - step) // 2
-        slot = (came * 4 + order[i]) * 2 + second
+        slot = line_slot(which, came, order[i], second)
         return slot, remote(
-            parts[which].at[block(i, 0, second)],
+            parts[which].at[block(which, i, 0, second)],
             line_in[which].at[slot],
             line_sems.at[which, 2 * i + second],
             line_recv.at[which, slot],
@@ -601,8 +687,8 @@
                 to_mate(which, i, first, second).start()
 
     def chip_sum(which, i, first, second):
-        here = block(i, first, second)
-        slot = slot_of(i, first, second)
+        here = block(which, i, first, second)
+        slot = slot_of(which, i, first, second)
         arrived(mate_in[which].at[slot], mate_recv.at[which, slot])
         return here, wide(parts[which], here) + wide(mate_in[which], slot)
 
@@ -652,7 +738,7 @@
 
     def from_line(which, second, add):
         for came, there in ((0, z > 0), (1, z < 3)):
-            slot = (came * 4 + z) * 2 + second
+            slot = line_slot(which, came, z, second)
 
             @pl.when(there)
             def _():
@@ -682,6 +768,53 @@
             outs[4][...] = outs[4][...] + piece if add else piece
 
 
+    split = arrays[0].shape[0]
+    cross = held[counts[0] :]
+    weights_kv, weights_q = cross[4].at[:, : 2 * D], cross[5].at[:, :D]
+    rows_held, back_out = cross[0], cross[1]
+    late = (
+        pltpu.make_async_copy(weights_ref.at[:, D : 3 * D], weights_kv, late_sems.at[0]),
+        pltpu.make_async_copy(weights_ref.at[:, :D], weights_q, late_sems.at[1]),
+        pltpu.make_async_copy(tokens_ref, rows_held, late_sems.at[2]),
+        pltpu.make_async_copy(resid_ref, grad_ref, late_sems.at[3]),
+    )
+    back = remote(
+        back_out, back_in, back_sems.at[0], back_sems.at[1], device_of(z, x, core, 0)
+    )
+
+    def key_value_rows(columns):
+        value = mm(held[3][:, columns].T, weights_kv[:, :D], NT)
+        return value + mm(held[4][:, columns].T, weights_kv[:, D:], NT)
+
+    def rows_before():
+        late[0].wait()
+        back_out[...] = key_value_rows(slice(0, split)).astype(bf16)
+
+        @pl.when(y == 1)
+        def _():
+            back.start()
+
+    def rows_here():
+        late[1].wait()
+        late[2].wait()
+        late[3].wait()
+        grad = key_value_rows(slice(split, 2 * split)) + mm(held[2][...], weights_q[...], NT)
+        add_rows(grad)
+
+    def add_rows(grad):
+        value = rows_held[...].astype(f32)
+        grad_ref[...] += norm_back(value, inverse_rms(value), gain_ref[...], grad)
+
+    def rows_back():
+        @pl.when(y == 0)
+        def _():
+            arrived(back_in, back_sems.at[1])
+            add_rows(back_in[...].astype(f32))
+
+        @pl.when(y == 1)
+        def _():
+            back.wait_send()
+
     make(0)
     make(1)
     send_first(0)
@@ -690,21 +823,26 @@
     send_second(0)
     line_self(0)
     make(3)
+    for copy in late:
+        copy.start()
     send_first(2)
     send_second(1)
     line_self(1)
     line_cross(0)
     send_first(3)
+    rows_before()
     send_second(2)
     line_self(2)
     line_cross(1)
     send_second(3)
     line_cross(2)
+    rows_here()
     last_self()
     line_cross(3)
     from_line(1, 0, lambda value: put(1, value, True))
     arrived(second_in[0].at[3], second_recv.at[0, 3])
     put(0, wide(second_in[0], 3), True)
+    rows_back()
 
     for which in (0, 1):
         for i in range(4):
@@ -719,7 +857,7 @@
                     along_line(which, i, second)[1].wait_send()
 
 
-def scatter_products(self_arrays, cross_arrays, small):
+def scatter_products(self_arrays, cross_arrays, small, weights, tokens, resid, gain):
     counts = (len(self_arrays), len(cross_arrays))
     arrays = (*self_arrays, *cross_arrays)
     shard = small.shape[1]
@@ -731,18 +869,19 @@
 
     return pl.pallas_call(
         functools.partial(scatter_body, counts),
-        in_specs=[pl.BlockSpec(memory_space=pl.ANY)] * (len(arrays) + 1),
-        out_specs=[pl.BlockSpec(memory_space=pltpu.VMEM)] * 5,
+        in_specs=[pl.BlockSpec(memory_space=pl.ANY)] * (len(arrays) + 4)
+        + [pl.BlockSpec(memory_space=pltpu.VMEM)],
+        out_specs=[pl.BlockSpec(memory_space=pltpu.VMEM)] * 6,
         out_shape=[
             jax.ShapeDtypeStruct(shape, f32)
-            for shape in ((3, shard, D), (shard, D), (3, shard, D), (shard, D), (shard, small.shape[2]))
+            for shape in ((3, shard, D), (shard, D), (3, shard, D), (shard, D), (shard, small.shape[2]), resid.shape)
         ],
         scratch_shapes=[pltpu.VMEM(array.shape, array.dtype) for array in (*arrays, small)]
         + buffers(32)
         + buffers(16)
         + buffers(8)
         + buffers(4)
-        + buffers(16)
+        + [pltpu.VMEM((16 - 8 * i, *shape), bf16) for i, shape in enumerate(shapes)]
         + [
             dma((len(arrays) + 1,)),
             dma((2, 16)),
@@ -753,22 +892,15 @@
             dma((2, 8)),
             dma((2, 4)),
             dma((2, 16)),
+            pltpu.VMEM(tokens.shape, bf16),
+            dma((2,)),
+            dma((4,)),
         ],
         compiler_params=pltpu.CompilerParams(
             collective_id=1, has_side_effects=True, vmem_limit_bytes=60 << 20
         ),
         name="scatter_products",
-    )(*arrays, small)
-
-
-def inverse_rms(values):
-    return lax.rsqrt(jnp.mean(values * values, axis=-1, keepdims=True) + epsilon)
-
-
-def norm_back(values, inverse, gain, grad):
-    unit = values * inverse
-    grad = grad * gain
-    return inverse * (grad - unit * jnp.mean(grad * unit, axis=-1, keepdims=True))
+    )(*arrays, small, weights, tokens, resid, gain)
 
 
 def gelu_and_slope(value):
@@ -891,8 +1023,11 @@
 
 
 def bias_parts(table_low):
-    by_pair = table_low.T.reshape(PAIRS, 4 * BUCKETS)
-    both = mm(by_pair, jnp.asarray(bias_matrices()[0], bf16)) * LOG2E
+    place = np.arange(2 * BUCKETS * HEADS)
+    code, head = place // HEADS, place % HEADS
+    chosen = (head // 2 == np.arange(PAIRS)[:, None]).astype(np.float32)
+    spread = bias_matrices()[0][(head % 2) * 2 * BUCKETS + code]
+    both = mm(jnp.asarray(chosen, bf16), table_low * jnp.asarray(spread, bf16)) * LOG2E
     far = both[:, 1024:]
     high = far.astype(bf16)
     rest = (far - high.astype(f32)).astype(bf16)
@@ -949,32 +1084,32 @@
     out_grad,
 ):
     shard = self_out.shape[0]
-    small = jnp.concatenate((norm_gains, rel_table[None]), axis=0).T
-    block_self = jnp.concatenate(
-        (self_proj[0], self_proj[1], self_proj[2], self_out, jnp.pad(small, ((0, 0), (0, 124)))),
-        axis=1,
-    ).astype(bf16)
-    block_cross = jnp.concatenate(
-        (cross_proj[0], cross_proj[1], cross_proj[2], cross_out), axis=1
-    ).astype(bf16)
+    units = FF // D
     own_kernels = (lax.axis_size("dp"), lax.axis_size("seq")) == (16, 2)
     if own_kernels:
-        all_self, all_cross = gather_blocks(block_self, block_cross)
+        all_self, all_cross, pair_ffn = gather_blocks(
+            self_proj, self_out, cross_proj, cross_out, ffn_in, ffn_out, norm_gains, rel_table
+        )
         all_self = all_self.reshape(-1, all_self.shape[2])
         all_cross = all_cross.reshape(-1, all_cross.shape[2])
+        pair_ffn = pair_ffn.reshape(2 * shard, 2 * FF)
+        all_ffn = lax.all_gather(pair_ffn, "dp", axis=0, tiled=True)
     else:
+        small = jnp.concatenate((norm_gains, rel_table[None]), axis=0).T
+        small = jnp.pad(small, ((0, 0), (0, 124)))
+        block_self = jnp.concatenate((*self_proj, self_out, small), axis=1).astype(bf16)
+        block_cross = jnp.concatenate((*cross_proj, cross_out), axis=1).astype(bf16)
+        ffn_in_here = jnp.swapaxes(ffn_in.reshape(shard, D, units), 1, 2).reshape(shard, FF)
+        block_ffn = jnp.concatenate((ffn_in_here, ffn_out.reshape(shard, FF)), axis=1).astype(bf16)
         all_self = lax.all_gather(block_self, BOTH, axis=0, tiled=True)
         all_cross = lax.all_gather(block_cross, BOTH, axis=0, tiled=True)
-    units = FF // D
-    ffn_in_here = jnp.swapaxes(ffn_in.reshape(shard, D, units), 1, 2).reshape(shard, FF)
-    block_ffn = jnp.concatenate((ffn_in_here, ffn_out.reshape(shard, FF)), axis=1).astype(bf16)
-    block_ffn, encoder_out = lax.optimization_barrier((block_ffn, encoder_out, all_cross))[:2]
-    all_ffn = lax.all_gather(block_ffn, BOTH, axis=0, tiled=True)
+        all_ffn = lax.all_gather(block_ffn, BOTH, axis=0, tiled=True)
+    encoder_out = lax.optimization_barrier((encoder_out, all_cross))[0]
     self_q, self_k, self_v, out_self = (all_self[:, i * D : (i + 1) * D] for i in range(4))
     cross_q, cross_k, cross_v = (all_cross[:, i * D : (i + 1) * D] for i in range(3))
-    small_all = all_self[:, 4 * D : 4 * D + 4].T
-    gains = small_all[:3].astype(f32)
-    far_lanes, near_lines = bias_parts(small_all[3].reshape(2 * BUCKETS, HEADS))
+    small_all = all_self[:, 4 * D :]
+    gains = small_all[:, :3].T.astype(f32)
+    far_lanes, near_lines = bias_parts(small_all[:, 3:4])
 
     tokens = decoder_in[0]
     memory = encoder_out[0]
@@ -984,21 +1119,7 @@
     seq_index = lax.axis_index("seq")
     keys, enc_keys = rows * seq_count, enc_rows * seq_count
 
-    lengths = dec_lengths[0]
-    memory_one = jnp.sum((enc_segments[0] < 1).astype(jnp.int32))
-    memory_two = jnp.sum((enc_segments[0] < 2).astype(jnp.int32))
-    info = jnp.stack(
-        (
-            seq_index * rows,
-            seq_index * enc_rows,
-            lengths[0],
-            lengths[0] + lengths[1],
-            memory_one,
-            memory_two,
-            pair_flags[0, 0],
-            pair_flags[0, 1],
-        )
-    ).astype(jnp.int32)
+    numbers = (dec_lengths, pair_flags)
     before = others_rows(tokens, True)
     others = others_rows(memory, False)
 
@@ -1012,7 +1133,9 @@
     kv_one = mm(normed_one, all_self[:, D : 3 * D]).astype(bf16)
     kv_before = mm(normed_before, all_self[:, D : 3 * D]).astype(bf16)
     parts_one = ((kv_before, 0, PAIRS), (kv_one, 0, PAIRS))
-    mixed_one, weights_one, total_one = attend(info, rows, query_one, parts_one, far_lanes, near_lines)
+    mixed_one, weights_one, total_one = attend(
+        numbers, rows, query_one, parts_one, far=far_lanes, near=near_lines
+    )
     resid_one = tokens + mm(mixed_one, out_self)
     inverse_two = inverse_rms(resid_one)
     normed_two = (resid_one * inverse_two * gains[1]).astype(bf16)
@@ -1020,13 +1143,13 @@
     kv_memory = mm(memory, all_cross[:, D : 3 * D]).astype(bf16)
     kv_others = mm(others, all_cross[:, D : 3 * D]).astype(bf16)
     parts_two = ((kv_memory, 0, PAIRS), (kv_others, 0, PAIRS))
-    mixed_two, weights_two, total_two = attend(info, rows, query_two, parts_two)
+    mixed_two, weights_two, total_two = attend(numbers, rows, query_two, parts_two, segments=enc_segments)
     layer_out, grad_resid, grad_low_two, grad_mixed, grad_ffn = feed_forward(
         resid_one, mixed_two, all_cross, gains[2], grad_out, all_ffn
     )
 
     grad_query, grad_key, grad_value = attend_back(
-        info, query_two, parts_two, weights_two, mixed_two, total_two, grad_mixed, False
+        numbers, query_two, parts_two, weights_two, mixed_two, total_two, grad_mixed, False
     )
     turned = (((0,), (1,)), ((), ()))
     kv_other = mm(grad_key[:, enc_rows:], cross_k, turned)
@@ -1040,12 +1163,9 @@
     grad_mixed = mm(grad_low, out_self, NT).astype(bf16)
     grad_mixed, kv_other = lax.optimization_barrier((grad_mixed, kv_other))
     grad_query, grad_key, grad_value, near_sums, row_sums = attend_back(
-        info, query_one, parts_one, weights_one, mixed_one, total_one, grad_mixed, True
+        numbers, query_one, parts_one, weights_one, mixed_one, total_one, grad_mixed, True
     )
     grad_others = to_owners(kv_other, False)
-    split = keys - rows
-    grad_before = mm(grad_key[:, :split], self_k, turned) + mm(grad_value[:, :split], self_v, turned)
-    grad_before = to_owners(grad_before.astype(bf16), True)
     table_grad = table_gradient(near_sums, row_sums)
     small = jnp.broadcast_to(table_grad[:, None], (D, 128)).astype(bf16)
 
@@ -1056,10 +1176,14 @@
         return jnp.stack([block[:, i * D : (i + 1) * D] for i in range(3)], axis=0)
 
     if own_kernels:
-        own_self, own_self_out, own_cross, own_cross_out, own_small = scatter_products(
+        own_self, own_self_out, own_cross, own_cross_out, own_small, grad_input = scatter_products(
             (normed_before, normed_one, grad_query, grad_key, grad_value, mixed_one, grad_low),
             (normed_two, grad_two[0], memory, others, grad_two[1], grad_two[2], mixed_two, grad_low_two),
             small.reshape(-1, shard, small.shape[1]),
+            all_self,
+            decoder_in[0],
+            grad_resid,
+            gains[:1],
         )
     else:
         normed_all = jnp.concatenate((normed_before, normed_one), axis=0)
@@ -1082,13 +1206,15 @@
         own_small = block[:, 4 * D :]
         block = owned(jnp.concatenate(cross_grads, axis=1).astype(bf16))
         own_cross, own_cross_out = projections(block), block[:, 3 * D :]
-
-    arrived = lax.optimization_barrier((grad_before, grad_others, own_small))
-    grad_before, grad_others, own_small = arrived
+        split = keys - rows
+        grad_before = mm(grad_key[:, :split], self_k, turned) + mm(grad_value[:, :split], self_v, turned)
+        grad_before = to_owners(grad_before.astype(bf16), True)
+        grad_normed = mm(grad_key[:, split:], self_k, turned) + mm(grad_value[:, split:], self_v, turned)
+        grad_normed = grad_normed + mm(grad_query, self_q, NT) + grad_before.astype(f32)
+        grad_input = grad_resid + norm_back(tokens, inverse_one, gains[0], grad_normed)
+
+    grad_others, own_small = lax.optimization_barrier((grad_others, own_small))
     grad_encoder = grad_memory + grad_others.astype(f32)
-    grad_normed = mm(grad_key[:, split:], self_k, turned) + mm(grad_value[:, split:], self_v, turned)
-    grad_normed = grad_normed + mm(grad_query, self_q, NT) + grad_before.astype(f32)
-    grad_input = grad_resid + norm_back(tokens, inverse_one, gains[0], grad_normed)
     own_ffn = owned(grad_ffn)
     own_ffn_in = jnp.swapaxes(own_ffn[:, :FF].reshape(shard, units, D), 1, 2).reshape(shard, FF)
     own_ffn_out = own_ffn[:, FF:].reshape(ffn_out.shape)

time: 401 us -> 362 us (0.903)
  waiting for transfers between devices: 15.5 us -> 5.23 us
  matrix products: 50 us -> 41.7 us
  other arithmetic: 18.8 us -> 11.3 us
  local copies, waits for them, and re-layouts: 22.7 us -> 16.1 us
    ppermute x2, waiting for transfers between devices: 15.5 us -> 5.17 us  [others_rows(): return lax.ppermute(rows, 'seq', [(0, 1)] if own_last else [(0, 1), (1, 0)])]
    pallas_call x1, Pallas kernels: 95.3 us -> 86.3 us  [scatter_products(): pl.pallas_call(functools.partial(scatter_body, counts), in_specs=[pl.Bloc...]
    dot_general x19 -> x14, matrix products: 48.7 us -> 40.4 us  [mm(): return lax.dot_general(a, b, dims, preferred_element_type=f32)]
    pallas_call x1, Pallas kernels: 47.5 us -> 55.2 us  [gather_blocks(): pl.pallas_call(gather_body, in_specs=[pl.BlockSpec(memory_space=pltpu.VME...]
    another operation x5 -> x0, other arithmetic: 4.49 us -> none
    unnamed x100 -> x76, local copies, waits for them, and re-layouts: 9.07 us -> 8.73 us
  transfers between devices with their start and end apart: 6 -> 5, of which waited for: 2 -> 2; matrix products, arithmetic and copies ran while one was open for 18% -> 16% of each run, Pallas kernels for 47% -> 50%
where the time goes in v4:
time: 362 us; the launch traced here: 356 us
  Pallas kernels  262 us (72%)
  matrix products  41.7 us (12%)
  local copies, waits for them, and re-layouts  16.1 us (4%)
  between operations  14.8 us (4%)
  other arithmetic  11.3 us (3%)
  starting transfers between devices  5.3 us (1%)
  waiting for transfers between devices  5.23 us (1%)
    pallas_call x1, Pallas kernels, scatter_products(): pl.pallas_call(functools.partial(scatter_body, counts), in_specs=[pl.Bloc...  86.3 us
    pallas_call x1, Pallas kernels, gather_blocks(): pl.pallas_call(gather_body, in_specs=[pl.BlockSpec(memory_space=pltpu.VME...  55.2 us
    pallas_call x2, Pallas kernels, attend_back(): pl.pallas_call(functools.partial(attend_back_body, rows, keys, causal, st...  46.8 us
    pallas_call x2, Pallas kernels, attend(): pl.pallas_call(functools.partial(attend_body, rows, keys, causal, step, l...  44.8 us
    dot_general x14, matrix products, mm(): return lax.dot_general(a, b, dims, preferred_element_type=f32)  40.4 us
    pallas_call x1, Pallas kernels, feed_forward(): pl.pallas_call(functools.partial(feed_forward_body, rows), grid=(units, 2...  28.7 us
    unnamed x76, local copies, waits for them, and re-layouts  8.73 us
  transfers between devices with their start and end apart: 5, of which 2 were waited for; matrix products, arithmetic and copies ran while one was open for 16% of the time, Pallas kernels for 50%

profile of v4, /device:TPU:0, one launch (start us, length us, event | category | flops | bytes accessed | tf_op | source)
XLA Modules:
  0.0 356.3 jit_solution(16937924747502431258)
XLA Ops:
  7.2 55.2 %gather_blocks.1 = (bf16[32,24,3200]{2,1,0:T(8,128)(2,1)}, bf16[32,24,3072]{2,1,0:T(8,128)(2,1)}, bf16[2,24,6144]{2,1,0:T(8,128)(2,1)}) custom-call(f32[3,24,768]{2,1,0:T(8,128)} %refs_0_.5, f32[24,768]{1,0:T(8,128)} %refs_1_.5, f32[3,24,768]{2,1,0:T(8,128)} %refs_2_.1, f32[24,768]{1,0:T(8,128)} %refs_3_.1, f32[24,3072]{1,0:T(8,128)} %refs_4_.1, ...), custom_call_target="tpu_custom_call" | custom-call | tf_op jit(solution)/shard_map/gather_blocks/pallas_call | solution.py:527
  62.6 2.6 collective-permute-start
  65.3 1.2 slice_reduce_fusion
  66.5 2.0 fusion
  71.7 6.2 %convolution_convert_fusion.1.refs_3_.refs_5_ = bf16[1024,1536]{1,0:T(8,128)(2,1)} fusion(bf16[768,3072]{1,0:T(8,128)(2,1)} %bitcast.47, bf16[1,1024,768]{2,1,0:T(8,128)(2,1)S(1)} %copy-done.15), kind=kOutput, calls=%fused_computation.1 | convolution fusion | flops 2417491968 | bytes 7077888 | tf_op jit(solution)/shard_map/dot_general | solution.py:33
  78.0 4.9 %collective-permute-done = bf16[512,768]{1,0:T(8,128)(2,1)S(1)} collective-permute-done((bf16[512,768]{1,0:T(8,128)(2,1)S(1)}, bf16[512,768]{1,0:T(8,128)(2,1)S(1)}, u32[]{:S(2)}, u32[]{:S(2)}) %collective-permute-start) | collective-permute-done | bytes 786464 | tf_op jit(solution)/shard_map/ppermute | solution.py:1053
  83.6 2.6 convolution_convert_fusion.2.refs_4_.refs_6_
  86.2 1.7 multiply_convert_fusion.2.refs_2_
  87.9 2.6 convolution_convert_fusion.3.refs_3_.refs_5_
  90.4 21.1 %attend_causal.1 = (bf16[512,768]{1,0:T(8,128)(2,1)}, bf16[12,512,1024]{2,1,0:T(8,128)(2,1)}, f32[512,768]{1,0:T(8,128)}) custom-call(s32[1,2]{1,0:T(1,128)} %refs_0_.9, s32[1,2]{1,0:T(1,128)} %refs_1_.9, bf16[512,768]{1,0:T(8,128)(2,1)} %multiply_convert_fusion.2.refs_2_, bf16[512,1536]{1,0:T(8,128)(2,1)} %convolution_convert_fusion.3.refs_3_.refs_5_, ...), custom_call_target="tpu_custom_call" | custom-call | tf_op jit(solution)/shard_map/attend_causal/pallas_call | solution.py:204
  111.5 2.4 multiply_reduce_fusion.1
  114.2 1.7 multiply_convert_fusion.refs_2_
  116.1 5.5 %convolution_convert_fusion.refs_4_.refs_6_ = bf16[1024,1536]{1,0:T(8,128)(2,1)} fusion(bf16[1024,768]{1,0:T(8,128)(2,1)} %collective-permute-done.1.refs_10_, bf16[768,3072]{1,0:T(8,128)(2,1)S(1)} %bitcast.55), kind=kOutput, calls=%fused_computation | convolution fusion | flops 2417491968 | bytes 7077888 | tf_op jit(solution)/shard_map/dot_general | solution.py:33
  121.6 23.7 %attend_cross.1 = (bf16[512,768]{1,0:T(8,128)(2,1)}, bf16[12,512,2048]{2,1,0:T(8,128)(2,1)}, f32[512,768]{1,0:T(8,128)}) custom-call(s32[1,2]{1,0:T(1,128)} %refs_0_.9, s32[1,2]{1,0:T(1,128)} %refs_1_.9, bf16[512,768]{1,0:T(8,128)(2,1)} %multiply_convert_fusion.refs_2_, bf16[1024,1536]{1,0:T(8,128)(2,1)} %convolution_convert_fusion.1.refs_3_.refs_5_, ...), custom_call_target="tpu_custom_call" | custom-call | tf_op jit(solution)/shard_map/attend_cross/pallas_call | solution.py:204
  145.4 1.1 copy-done
  146.5 28.7 %feed_forward.1 = (bf16[512,768]{1,0:T(8,128)(2,1)}, f32[512,768]{1,0:T(8,128)S(1)}, bf16[512,768]{1,0:T(8,128)(2,1)S(1)}, bf16[512,768]{1,0:T(8,128)(2,1)S(1)}, bf16[768,6144]{1,0:T(8,128)(2,1)}) custom-call(f32[512,768]{1,0:T(8,128)} %copy-done.4, bf16[512,768]{1,0:T(8,128)(2,1)S(1)} %copy-done, bf16[768,3072]{1,0:T(8,128)(2,1)} %bitcast.48, ...), custom_call_target="tpu_custom_call" | custom-call | tf_op jit(solution)/shard_map/feed_forward/pallas_call | solution.py:965
  177.0 27.4 %attend_cross_back.1 = (bf16[512,768]{1,0:T(8,128)(2,1)}, bf16[768,2048]{1,0:T(8,128)(2,1)}, bf16[768,2048]{1,0:T(8,128)(2,1)}) custom-call(s32[1,2]{1,0:T(1,128)} %refs_0_.9, s32[1,2]{1,0:T(1,128)} %refs_1_.9, bf16[512,768]{1,0:T(8,128)(2,1)} %multiply_convert_fusion.refs_2_, bf16[1024,1536]{1,0:T(8,128)(2,1)} %convolution_convert_fusion.1.refs_3_.refs_5_, ...), custom_call_target="tpu_custom_call" | custom-call | tf_op jit(solution)/shard_map/attend_cross_back/pallas_call | solution.py:316
  204.4 2.7 multiply_reduce_fusion
  207.1 1.6 fusion.34
  208.7 3.4 convolution_convert_fusion.4.refs_10_
  212.0 1.5 fusion.17
  214.1 2.6 add_convert_fusion
  216.7 2.5 collective-permute-start.2
  219.2 19.4 %attend_causal_back.1 = (bf16[512,768]{1,0:T(8,128)(2,1)}, bf16[768,1024]{1,0:T(8,128)(2,1)}, bf16[768,1024]{1,0:T(8,128)(2,1)}, f32[6,4,256]{2,1,0:T(4,128)}, f32[6,4,128]{2,1,0:T(4,128)}) custom-call(s32[1,2]{1,0:T(1,128)} %refs_0_.9, s32[1,2]{1,0:T(1,128)} %refs_1_.9, bf16[512,768]{1,0:T(8,128)(2,1)} %multiply_convert_fusion.2.refs_2_, ...), custom_call_target="tpu_custom_call" | custom-call | tf_op jit(solution)/shard_map/attend_causal_back/pallas_call | solution.py:316
  241.9 86.3 %scatter_products.1 = (f32[3,24,768]{2,1,0:T(8,128)}, f32[24,768]{1,0:T(8,128)}, f32[3,24,768]{2,1,0:T(8,128)}, f32[24,768]{1,0:T(8,128)}, f32[24,128]{1,0:T(8,128)}, /*index=5*/f32[512,768]{1,0:T(8,128)}) custom-call(bf16[512,768]{1,0:T(8,128)(2,1)} %copy-done.8, bf16[512,768]{1,0:T(8,128)(2,1)} %copy-done.9, bf16[512,768]{1,0:T(8,128)(2,1)} %get-tuple-element.61.refs_2_, ...), custom_call_target="tpu_custom_call" | custom-call | tf_op jit(solution)/shard_map/scatter_products/pallas_call | solution.py:870
  328.2 1.0 multiply_reduce_fusion.4
  329.3 1.1 multiply_reduce_fusion.3
  330.3 2.9 fusion.14
  333.3 2.8 fusion.12
  336.7 3.7 %add_bitcast_fusion = f32[1,1024,768]{2,1,0:T(8,128)} fusion(bf16[1024,768]{1,0:T(8,128)(2,1)} %collective-permute-done.2, f32[1024,768]{1,0:T(8,128)S(1)} %fusion.14, f32[1024,768]{1,0:T(8,128)S(1)} %fusion.12), kind=kLoop, calls=%fused_computation.2 | loop fusion | flops 2359296 | bytes 11010048 | tf_op jit(solution)/shard_map/broadcast_in_dim | solution.py:1238
  343.5 1.2 multiply_reduce_fusion.2
  345.4 1.1 copy.62
  (113 shorter events, 17.2 us)
Async XLA Ops:
  7.2 59.3 %copy-start.27 = (bf16[6,768]{1,0:T(8,128)(2,1)S(1)}, bf16[6,768]{1,0:T(8,128)(2,1)}, u32[]{:S(2)}) copy-start(bf16[6,768]{1,0:T(8,128)(2,1)} %constant.40.clone) | copy-start | bytes 27652
  7.2 55.4 %copy-start.6 = (bf16[1,512,768]{2,1,0:T(8,128)(2,1)S(1)}, bf16[1,512,768]{2,1,0:T(8,128)(2,1)}, u32[]{:S(2)}) copy-start(bf16[1,512,768]{2,1,0:T(8,128)(2,1)} %param.18) | copy-start | bytes 2359300
  7.2 138.1 %all-gather.2.cloned.1.call-start = ((), (), s32[]{:S(2)}) async-start(), calls=%async_computation.1 | async-start | bytes 10027008 | tf_op jit(solution)/shard_map/all_gather | solution.py:1096
  62.5 277.8 %reduce-scatter.2.cloned.1.call-start = ((), (), s32[]{:S(2)}) async-start(), calls=%async_computation.2 | async-start | bytes 9732096 | tf_op jit(solution)/shard_map/reduce_scatter | solution.py:1173
  62.6 20.3 %collective-permute-start = (bf16[512,768]{1,0:T(8,128)(2,1)S(1)}, bf16[512,768]{1,0:T(8,128)(2,1)S(1)}, u32[]{:S(2)}, u32[]{:S(2)}) collective-permute-start(bf16[512,768]{1,0:T(8,128)(2,1)S(1)} %bitcast.61), channel_id=1, source_target_pairs={{0,1},{2,3},{4,5},{6,7},{8,9},{10,11},{12,13},{14,15},{16,17},{18,... | collective-permute-start | bytes 2359304 | tf_op jit(solution)/shard_map/ppermute | solution.py:1053
  65.2 50.9 %collective-permute-start.1 = (bf16[1024,768]{1,0:T(8,128)(2,1)}, bf16[1024,768]{1,0:T(8,128)(2,1)}, u32[]{:S(2)}, u32[]{:S(2)}) collective-permute-start(bf16[1024,768]{1,0:T(8,128)(2,1)} %bitcast.73), channel_id=1, source_target_pairs={{0,1},{1,0},{2,3},{3,2},{4,5},{5,4},{6,7},{7,6},{8,9},{9,8},{10,11... | collective-permute-start | bytes 4718600 | tf_op jit(solution)/shard_map/ppermute | solution.py:1053
  66.5 5.3 %copy-start.15 = (bf16[1,1024,768]{2,1,0:T(8,128)(2,1)S(1)}, bf16[1,1024,768]{2,1,0:T(8,128)(2,1)}, u32[]{:S(2)}) copy-start(bf16[1,1024,768]{2,1,0:T(8,128)(2,1)} %param.19) | copy-start | bytes 4718596
  70.9 12.7 %slice-start.4 = ((s8[4915200]{0:T(1024)(128)(4,1)}), s8[4194304]{0:T(1024)(128)(4,1)S(1)}, s32[]{:S(2)}) async-start(s8[4915200]{0:T(1024)(128)(4,1)} %bitcast.68), calls=%async_computation.7 | async-start | bytes 8388608
  71.7 11.9 %slice-start.5 = ((s8[4915200]{0:T(1024)(128)(4,1)}), s8[720896]{0:T(1024)(128)(4,1)S(1)}, s32[]{:S(2)}) async-start(s8[4915200]{0:T(1024)(128)(4,1)} %bitcast.68), calls=%async_computation.8 | async-start | bytes 1441792
  83.6 2.6 copy-start.9
  83.6 4.3 %copy-start.8 = (bf16[512,768]{1,0:T(8,128)(2,1)}, bf16[512,768]{1,0:T(8,128)(2,1)S(1)}, u32[]{:S(2)}) copy-start(bf16[512,768]{1,0:T(8,128)(2,1)S(1)} %get-tuple-element.120.refs_0_) | copy-start | bytes 2359300
  87.9 26.2 %slice-start = ((s8[4718592]{0:T(1024)(128)(4,1)}), s8[4194304]{0:T(1024)(128)(4,1)S(1)}, s32[]{:S(2)}) async-start(s8[4718592]{0:T(1024)(128)(4,1)} %bitcast.52), calls=%async_computation.3 | async-start | bytes 8388608
  90.4 23.7 %slice-start.1 = ((s8[4718592]{0:T(1024)(128)(4,1)}), s8[524288]{0:T(1024)(128)(4,1)S(1)}, s32[]{:S(2)}) async-start(s8[4718592]{0:T(1024)(128)(4,1)} %bitcast.52), calls=%async_computation.4 | async-start | bytes 1048576
  113.9 1.9 copy-start.4
  121.6 23.7 %copy-start.1 = (bf16[1,512,768]{2,1,0:T(8,128)(2,1)S(1)}, bf16[1,512,768]{2,1,0:T(8,128)(2,1)}, u32[]{:S(2)}) copy-start(bf16[1,512,768]{2,1,0:T(8,128)(2,1)} %param.31) | copy-start | bytes 2359300
  177.0 27.4 %copy-start.5 = (f32[512,768]{1,0:T(8,128)S(1)}, f32[512,768]{1,0:T(8,128)}, u32[]{:S(2)}) copy-start(f32[512,768]{1,0:T(8,128)} %copy-done.4) | copy-start | bytes 4718596
  204.4 7.6 %slice-start.2 = ((s8[4718592]{0:T(1024)(128)(4,1)}), s8[4194304]{0:T(1024)(128)(4,1)S(1)}, s32[]{:S(2)}) async-start(s8[4718592]{0:T(1024)(128)(4,1)} %bitcast.56), calls=%async_computation.5 | async-start | bytes 8388608
  207.1 4.9 %slice-start.3 = ((s8[4718592]{0:T(1024)(128)(4,1)}), s8[524288]{0:T(1024)(128)(4,1)S(1)}, s32[]{:S(2)}) async-start(s8[4718592]{0:T(1024)(128)(4,1)} %bitcast.56), calls=%async_computation.6 | async-start | bytes 1048576
  208.7 3.4 copy-start.7
  208.7 3.4 copy-start.13
  212.0 2.0 copy-start.11
  216.7 119.3 %collective-permute-start.2 = (bf16[1024,768]{1,0:T(8,128)(2,1)}, bf16[1024,768]{1,0:T(8,128)(2,1)}, u32[]{:S(2)}, u32[]{:S(2)}) collective-permute-start(bf16[1024,768]{1,0:T(8,128)(2,1)} %add_convert_fusion), channel_id=1, source_target_pairs={{0,1},{1,0},{2,3},{3,2},{4,5},{5,4},{6,7},{7,6},{8,9},{9,8},{10,11... | collective-permute-start | bytes 4718600 | tf_op jit(solution)/shard_map/ppermute | solution.py:1063
  219.2 20.2 %copy-start.20 = (f32[1024,128]{1,0:T(8,128)S(1)}, f32[1024,128]{1,0:T(8,128)}, u32[]{:S(2)}) copy-start(f32[1024,128]{1,0:T(8,128)} %constant.56) | copy-start | bytes 1572868
  219.2 20.6 %copy-start.22 = (f32[512,128]{1,0:T(8,128)S(1)}, f32[512,128]{1,0:T(8,128)}, u32[]{:S(2)}) copy-start(f32[512,128]{1,0:T(8,128)} %constant.57) | copy-start | bytes 786436
  241.9 87.4 %copy-start.18 = (f32[3,24,768]{2,1,0:T(8,128)S(1)}, f32[3,24,768]{2,1,0:T(8,128)}, u32[]{:S(2)}) copy-start(f32[3,24,768]{2,1,0:T(8,128)} %refs_0_.5) | copy-start | bytes 663556
  241.9 88.4 %copy-start.14 = (bf16[768,2048]{1,0:T(8,128)(2,1)S(1)}, bf16[768,2048]{1,0:T(8,128)(2,1)}, u32[]{:S(2)}) copy-start(bf16[768,2048]{1,0:T(8,128)(2,1)} %get-tuple-element.58.refs_11_) | copy-start | bytes 9437188
  330.3 2.9 copy-start.12
  333.3 2.8 copy-start.25
  343.1 2.3 copy-start.16
  343.5 3.0 copy-start.17
  345.4 2.5 copy-start.21
  345.4 3.2 copy-start.23
  (7 other events, 9.4 us)
Sparse Core Ops, SparseCore 0:
  62.6 81.6 all-gather.1
  177.1 161.3 reduce-scatter.1

commit v5 on v4

--- a/solution.py
+++ b/solution.py
@@ -368,7 +368,8 @@
     masters, refs = refs[:9], refs[9:]
     wholes, pair_whole = refs[:2], refs[2]
     sources, pair_source = refs[3:5], refs[5]
-    own_sems, up_sems, down_sems, side_sems, turn_sems, mate_sems, recv_sems, pair_sems = refs[6:]
+    own_sems, mate_sems, recv_sems, pair_sems = refs[6:10]
+    route_sems = dict(zip(("up", "down", "x", "y"), refs[10:]))
     self_proj, self_out, cross_proj, cross_out, ffn_in, ffn_out, norm_gains, table, order = masters
     count = 2
     shard = self_out.shape[0]
@@ -390,8 +391,8 @@
     me = block_of(z, x, core, y)
     greet_neighbours(z, x, core, y)
 
-    def near(which, side, turn):
-        return ((x + side) % 2, (y + turn) % 2) if which == 0 else ((x + turn) % 2, (y + side) % 2)
+    routes = (("y", "z", "x"), ("z", "x", "y"))
+    slots = {}
 
     def send(which, source, block, send_sem, device):
         return pltpu.make_async_remote_copy(
@@ -403,30 +404,32 @@
             device_id_type=MESH,
         )
 
-    def copies(which, far, up, side, turn, source=None):
+    def copies(which, far, up, dx, dy, source=None):
         at_z = z + far if up else z - far
-        bx, by = near(which, side, turn)
-        block = block_of(at_z, bx, core, by)
+        block = block_of(at_z, (x + dx) % 2, core, (y + dy) % 2)
         source = wholes[which].at[block] if source is None else source
-        slot = (2 * far + (1 if up else 0)) if far else 0
-        slot = max(slot - 1, 0)
-        out = [(None, send(which, source, block, mate_sems.at[which, (side * 2 + turn) * 7 + slot], mate))]
-        if turn == 0:
-            tx, ty = near(which, 0, 1)
-            out.append(
-                (None, send(which, source, block, turn_sems.at[which, side * 7 + slot], device_of(z, tx, core, ty)))
-            )
-            if side == 0:
-                sx, sy = near(which, 1, 0)
-                out.append((None, send(which, source, block, side_sems.at[which, slot], device_of(z, sx, core, sy))))
-                if far == 0 or not up:
-                    out.append(
-                        (z < 3, send(which, source, block, up_sems.at[which, far], device_of(z + 1, x, core, y)))
-                    )
-                if far == 0 or up:
-                    out.append(
-                        (z > 0, send(which, source, block, down_sems.at[which, far], device_of(z - 1, x, core, y)))
-                    )
+        route = routes[which]
+        moved = [axis for axis, steps in (("z", far), ("x", dx), ("y", dy)) if steps]
+        last = max((route.index(axis) for axis in moved), default=-1)
+        targets = []
+        for axis in route[max(last, 0) :]:
+            fresh = route.index(axis) > last
+            if axis == "z" and (fresh or not up):
+                targets.append((z < 3, "up", device_of(z + 1, x, core, y)))
+            if axis == "z" and (fresh or up):
+                targets.append((z > 0, "down", device_of(z - 1, x, core, y)))
+            if axis == "x" and fresh:
+                targets.append((None, "x", device_of(z, 1 - x, core, y)))
+            if axis == "y" and fresh:
+                targets.append((None, "y", device_of(z, x, core, 1 - y)))
+        out = []
+        for condition, kind, device in targets:
+            taken = slots.setdefault((which, kind), {})
+            slot = taken.setdefault((far, up, dx, dy), len(taken))
+            out.append((condition, send(which, source, block, route_sems[kind].at[which, slot], device)))
+        taken = slots.setdefault((which, "mate"), {})
+        slot = taken.setdefault((far, up, dx, dy), len(taken))
+        out.append((None, send(which, source, block, mate_sems.at[which, slot], mate)))
         return block, out
 
     def when(condition, action):
@@ -440,12 +443,12 @@
             return None
         return z + far < 4 if up else z - far >= 0
 
-    def onwards(which, far, up, side, turn, source=None):
+    def onwards(which, far, up, dx, dy, source=None):
         def run():
-            block, out = copies(which, far, up, side, turn, source)
+            block, out = copies(which, far, up, dx, dy, source)
             if source is None:
                 pltpu.make_async_copy(wholes[which].at[block], wholes[which].at[block], recv_sems.at[which, block]).wait()
-            for condition, copy in reversed(out):
+            for condition, copy in out:
                 when(condition, copy.start)
 
         when(exists(far, up), run)
@@ -463,7 +466,7 @@
         device_id_type=MESH,
     )
     for which in range(count):
-        onwards(which, 0, True, 0, 0, sources[which])
+        onwards(which, 0, False, 0, 0, sources[which])
     for copy in own[:count]:
         copy.start()
     units = FF // D
@@ -481,33 +484,32 @@
     own[count].start()
     pair.start()
     waves = [[] for _ in range(6)]
-    for side in (0, 1):
-        for turn in (0, 1):
+    for dx in (0, 1):
+        for dy in (0, 1):
             for far in range(4):
                 for up in (False, True):
-                    if far == 0 and (up or (side == 0 and turn == 0)):
+                    if far == 0 and (up or (dx == 0 and dy == 0)):
                         continue
-                    waves[far + side + turn].append((far, up, side, turn))
+                    waves[far + dx + dy].append((far, up, dx, dy))
     for wave in waves:
-        for far, up, side, turn in wave:
+        for far, up, dx, dy in wave:
             for which in range(count):
-                onwards(which, far, up, side, turn)
-    for side in (0, 1):
-        for turn in (0, 1):
+                onwards(which, far, up, dx, dy)
+    for dx in (0, 1):
+        for dy in (0, 1):
             for far in range(4):
                 for up in (False, True):
                     if far == 0 and up:
                         continue
                     for which in range(count):
 
-                        def finish(which=which, far=far, up=up, side=side, turn=turn):
+                        def finish(which=which, far=far, up=up, dx=dx, dy=dy):
                             at_z = z + far if up else z - far
-                            bx, by = near(which, side, turn)
-                            block = block_of(at_z, bx, 1 - core, by)
+                            block = block_of(at_z, (x + dx) % 2, 1 - core, (y + dy) % 2)
                             whole = wholes[which].at[block]
                             pltpu.make_async_copy(whole, whole, recv_sems.at[which, block]).wait()
-                            source = sources[which] if (far, side, turn) == (0, 0, 0) else None
-                            _, out = copies(which, far, up, side, turn, source)
+                            source = sources[which] if (far, dx, dy) == (0, 0, 0) else None
+                            _, out = copies(which, far, up, dx, dy, source)
                             for condition, copy in out:
                                 when(condition, copy.wait_send)
 
@@ -531,9 +533,8 @@
         out_shape=[jax.ShapeDtypeStruct((32, *shape), bf16) for shape in shapes]
         + [jax.ShapeDtypeStruct((2, *pair), bf16)],
         scratch_shapes=[pltpu.VMEM(shape, bf16) for shape in (*shapes, pair)]
-        + [dma((3,))]
-        + [dma((2, n)) for n in (4, 4, 7, 14, 28, 32)]
-        + [dma((3,))],
+        + [dma((3,)), dma((2, 28)), dma((2, 32)), dma((3,))]
+        + [dma((2, 16))] * 4,
         compiler_params=pltpu.CompilerParams(collective_id=0, has_side_effects=True),
         name="gather_blocks",
     )(

time: 362 us -> 356 us (0.983)
  Pallas kernels: 262 us -> 256 us
    pallas_call x1, Pallas kernels: 55.2 us -> 49.5 us  [gather_blocks(): pl.pallas_call(gather_body, in_specs=[pl.BlockSpec(memory_space=pltpu.VME...]
  transfers between devices with their start and end apart: 5 -> 5, of which waited for: 2 -> 2; matrix products, arithmetic and copies ran while one was open for 16% -> 16% of each run, Pallas kernels for 50% -> 51%
where the time goes in v5:
time: 356 us; the launch traced here: 352 us
  Pallas kernels  256 us (72%)
  matrix products  41.5 us (12%)
  local copies, waits for them, and re-layouts  16.1 us (5%)
  between operations  14.8 us (4%)
  other arithmetic  11.3 us (3%)
  starting transfers between devices  6.28 us (2%)
  waiting for transfers between devices  5.44 us (2%)
    pallas_call x1, Pallas kernels, scatter_products(): pl.pallas_call(functools.partial(scatter_body, counts), in_specs=[pl.Bloc...  86.4 us
    pallas_call x1, Pallas kernels, gather_blocks(): pl.pallas_call(gather_body, in_specs=[pl.BlockSpec(memory_space=pltpu.VME...  49.5 us
    pallas_call x2, Pallas kernels, attend_back(): pl.pallas_call(functools.partial(attend_back_body, rows, keys, causal, st...  46.7 us
    pallas_call x2, Pallas kernels, attend(): pl.pallas_call(functools.partial(attend_body, rows, keys, causal, step, l...  44.8 us
    dot_general x14, matrix products, mm(): return lax.dot_general(a, b, dims, preferred_element_type=f32)  40.3 us
    pallas_call x1, Pallas kernels, feed_forward(): pl.pallas_call(functools.partial(feed_forward_body, rows), grid=(units, 2...  28.7 us
    unnamed x76, local copies, waits for them, and re-layouts  8.73 us
  transfers between devices with their start and end apart: 5, of which 2 were waited for; matrix products, arithmetic and copies ran while one was open for 16% of the time, Pallas kernels for 51%

profile of v5, /device:TPU:0, one launch (start us, length us, event | category | flops | bytes accessed | tf_op | source)
XLA Modules:
  0.0 351.6 jit_solution(2706167547785656759)
XLA Ops:
  7.2 49.5 %gather_blocks.1 = (bf16[32,24,3200]{2,1,0:T(8,128)(2,1)}, bf16[32,24,3072]{2,1,0:T(8,128)(2,1)}, bf16[2,24,6144]{2,1,0:T(8,128)(2,1)}) custom-call(f32[3,24,768]{2,1,0:T(8,128)} %refs_0_.5, f32[24,768]{1,0:T(8,128)} %refs_1_.5, f32[3,24,768]{2,1,0:T(8,128)} %refs_2_.1, f32[24,768]{1,0:T(8,128)} %refs_3_.1, f32[24,3072]{1,0:T(8,128)} %refs_4_.1, ...), custom_call_target="tpu_custom_call" | custom-call | tf_op jit(solution)/shard_map/gather_blocks/pallas_call | solution.py:529
  56.9 3.7 %collective-permute-start = (bf16[512,768]{1,0:T(8,128)(2,1)S(1)}, bf16[512,768]{1,0:T(8,128)(2,1)S(1)}, u32[]{:S(2)}, u32[]{:S(2)}) collective-permute-start(bf16[512,768]{1,0:T(8,128)(2,1)S(1)} %bitcast.61), channel_id=1, source_target_pairs={{0,1},{2,3},{4,5},{6,7},{8,9},{10,11},{12,13},{14,15},{16,17},{18,... | collective-permute-start | bytes 2359304 | tf_op jit(solution)/shard_map/ppermute | solution.py:1054
  60.6 1.2 slice_reduce_fusion
  61.8 2.0 fusion
  67.0 6.0 %convolution_convert_fusion.1.refs_3_.refs_5_ = bf16[1024,1536]{1,0:T(8,128)(2,1)} fusion(bf16[768,3072]{1,0:T(8,128)(2,1)} %bitcast.47, bf16[1,1024,768]{2,1,0:T(8,128)(2,1)S(1)} %copy-done.15), kind=kOutput, calls=%fused_computation.1 | convolution fusion | flops 2417491968 | bytes 7077888 | tf_op jit(solution)/shard_map/dot_general | solution.py:33
  73.1 5.1 %collective-permute-done = bf16[512,768]{1,0:T(8,128)(2,1)S(1)} collective-permute-done((bf16[512,768]{1,0:T(8,128)(2,1)S(1)}, bf16[512,768]{1,0:T(8,128)(2,1)S(1)}, u32[]{:S(2)}, u32[]{:S(2)}) %collective-permute-start) | collective-permute-done | bytes 786464 | tf_op jit(solution)/shard_map/ppermute | solution.py:1054
  78.9 2.6 convolution_convert_fusion.2.refs_4_.refs_6_
  81.5 1.7 multiply_convert_fusion.2.refs_2_
  83.2 2.6 convolution_convert_fusion.3.refs_3_.refs_5_
  85.7 21.1 %attend_causal.1 = (bf16[512,768]{1,0:T(8,128)(2,1)}, bf16[12,512,1024]{2,1,0:T(8,128)(2,1)}, f32[512,768]{1,0:T(8,128)}) custom-call(s32[1,2]{1,0:T(1,128)} %refs_0_.9, s32[1,2]{1,0:T(1,128)} %refs_1_.9, bf16[512,768]{1,0:T(8,128)(2,1)} %multiply_convert_fusion.2.refs_2_, bf16[512,1536]{1,0:T(8,128)(2,1)} %convolution_convert_fusion.3.refs_3_.refs_5_, ...), custom_call_target="tpu_custom_call" | custom-call | tf_op jit(solution)/shard_map/attend_causal/pallas_call | solution.py:204
  106.8 2.4 multiply_reduce_fusion.1
  109.5 1.7 multiply_convert_fusion.refs_2_
  111.4 5.5 %convolution_convert_fusion.refs_4_.refs_6_ = bf16[1024,1536]{1,0:T(8,128)(2,1)} fusion(bf16[1024,768]{1,0:T(8,128)(2,1)} %collective-permute-done.1.refs_10_, bf16[768,3072]{1,0:T(8,128)(2,1)S(1)} %bitcast.55), kind=kOutput, calls=%fused_computation | convolution fusion | flops 2417491968 | bytes 7077888 | tf_op jit(solution)/shard_map/dot_general | solution.py:33
  116.9 23.7 %attend_cross.1 = (bf16[512,768]{1,0:T(8,128)(2,1)}, bf16[12,512,2048]{2,1,0:T(8,128)(2,1)}, f32[512,768]{1,0:T(8,128)}) custom-call(s32[1,2]{1,0:T(1,128)} %refs_0_.9, s32[1,2]{1,0:T(1,128)} %refs_1_.9, bf16[512,768]{1,0:T(8,128)(2,1)} %multiply_convert_fusion.refs_2_, bf16[1024,1536]{1,0:T(8,128)(2,1)} %convolution_convert_fusion.1.refs_3_.refs_5_, ...), custom_call_target="tpu_custom_call" | custom-call | tf_op jit(solution)/shard_map/attend_cross/pallas_call | solution.py:204
  140.7 1.1 copy-done
  141.8 28.7 %feed_forward.1 = (bf16[512,768]{1,0:T(8,128)(2,1)}, f32[512,768]{1,0:T(8,128)S(1)}, bf16[512,768]{1,0:T(8,128)(2,1)S(1)}, bf16[512,768]{1,0:T(8,128)(2,1)S(1)}, bf16[768,6144]{1,0:T(8,128)(2,1)}) custom-call(f32[512,768]{1,0:T(8,128)} %copy-done.4, bf16[512,768]{1,0:T(8,128)(2,1)S(1)} %copy-done, bf16[768,3072]{1,0:T(8,128)(2,1)} %bitcast.48, ...), custom_call_target="tpu_custom_call" | custom-call | tf_op jit(solution)/shard_map/feed_forward/pallas_call | solution.py:966
  172.3 27.4 %attend_cross_back.1 = (bf16[512,768]{1,0:T(8,128)(2,1)}, bf16[768,2048]{1,0:T(8,128)(2,1)}, bf16[768,2048]{1,0:T(8,128)(2,1)}) custom-call(s32[1,2]{1,0:T(1,128)} %refs_0_.9, s32[1,2]{1,0:T(1,128)} %refs_1_.9, bf16[512,768]{1,0:T(8,128)(2,1)} %multiply_convert_fusion.refs_2_, bf16[1024,1536]{1,0:T(8,128)(2,1)} %convolution_convert_fusion.1.refs_3_.refs_5_, ...), custom_call_target="tpu_custom_call" | custom-call | tf_op jit(solution)/shard_map/attend_cross_back/pallas_call | solution.py:316
  199.7 2.7 multiply_reduce_fusion
  202.4 1.6 fusion.34
  203.9 3.4 convolution_convert_fusion.4.refs_10_
  207.4 1.5 fusion.17
  209.4 2.6 add_convert_fusion
  212.0 2.5 collective-permute-start.2
  214.5 19.4 %attend_causal_back.1 = (bf16[512,768]{1,0:T(8,128)(2,1)}, bf16[768,1024]{1,0:T(8,128)(2,1)}, bf16[768,1024]{1,0:T(8,128)(2,1)}, f32[6,4,256]{2,1,0:T(4,128)}, f32[6,4,128]{2,1,0:T(4,128)}) custom-call(s32[1,2]{1,0:T(1,128)} %refs_0_.9, s32[1,2]{1,0:T(1,128)} %refs_1_.9, bf16[512,768]{1,0:T(8,128)(2,1)} %multiply_convert_fusion.2.refs_2_, ...), custom_call_target="tpu_custom_call" | custom-call | tf_op jit(solution)/shard_map/attend_causal_back/pallas_call | solution.py:316
  237.1 86.4 %scatter_products.1 = (f32[3,24,768]{2,1,0:T(8,128)}, f32[24,768]{1,0:T(8,128)}, f32[3,24,768]{2,1,0:T(8,128)}, f32[24,768]{1,0:T(8,128)}, f32[24,128]{1,0:T(8,128)}, /*index=5*/f32[512,768]{1,0:T(8,128)}) custom-call(bf16[512,768]{1,0:T(8,128)(2,1)} %copy-done.8, bf16[512,768]{1,0:T(8,128)(2,1)} %copy-done.9, bf16[512,768]{1,0:T(8,128)(2,1)} %get-tuple-element.61.refs_2_, ...), custom_call_target="tpu_custom_call" | custom-call | tf_op jit(solution)/shard_map/scatter_products/pallas_call | solution.py:871
  323.5 1.0 multiply_reduce_fusion.4
  324.6 1.1 multiply_reduce_fusion.3
  325.6 2.9 fusion.14
  328.6 2.8 fusion.12
  332.0 3.7 %add_bitcast_fusion = f32[1,1024,768]{2,1,0:T(8,128)} fusion(bf16[1024,768]{1,0:T(8,128)(2,1)} %collective-permute-done.2, f32[1024,768]{1,0:T(8,128)S(1)} %fusion.14, f32[1024,768]{1,0:T(8,128)S(1)} %fusion.12), kind=kLoop, calls=%fused_computation.2 | loop fusion | flops 2359296 | bytes 11010048 | tf_op jit(solution)/shard_map/broadcast_in_dim | solution.py:1239
  338.8 1.2 multiply_reduce_fusion.2
  340.7 1.1 copy.62
  (113 shorter events, 17.2 us)
Async XLA Ops:
  7.2 54.6 %copy-start.27 = (bf16[6,768]{1,0:T(8,128)(2,1)S(1)}, bf16[6,768]{1,0:T(8,128)(2,1)}, u32[]{:S(2)}) copy-start(bf16[6,768]{1,0:T(8,128)(2,1)} %constant.40.clone) | copy-start | bytes 27652
  7.2 49.7 %copy-start.6 = (bf16[1,512,768]{2,1,0:T(8,128)(2,1)S(1)}, bf16[1,512,768]{2,1,0:T(8,128)(2,1)}, u32[]{:S(2)}) copy-start(bf16[1,512,768]{2,1,0:T(8,128)(2,1)} %param.18) | copy-start | bytes 2359300
  7.2 133.4 %all-gather.2.cloned.1.call-start = ((), (), s32[]{:S(2)}) async-start(), calls=%async_computation.1 | async-start | bytes 10027008 | tf_op jit(solution)/shard_map/all_gather | solution.py:1097
  56.8 278.9 %reduce-scatter.2.cloned.1.call-start = ((), (), s32[]{:S(2)}) async-start(), calls=%async_computation.2 | async-start | bytes 9732096 | tf_op jit(solution)/shard_map/reduce_scatter | solution.py:1174
  56.9 21.3 %collective-permute-start = (bf16[512,768]{1,0:T(8,128)(2,1)S(1)}, bf16[512,768]{1,0:T(8,128)(2,1)S(1)}, u32[]{:S(2)}, u32[]{:S(2)}) collective-permute-start(bf16[512,768]{1,0:T(8,128)(2,1)S(1)} %bitcast.61), channel_id=1, source_target_pairs={{0,1},{2,3},{4,5},{6,7},{8,9},{10,11},{12,13},{14,15},{16,17},{18,... | collective-permute-start | bytes 2359304 | tf_op jit(solution)/shard_map/ppermute | solution.py:1054
  60.5 50.9 %collective-permute-start.1 = (bf16[1024,768]{1,0:T(8,128)(2,1)}, bf16[1024,768]{1,0:T(8,128)(2,1)}, u32[]{:S(2)}, u32[]{:S(2)}) collective-permute-start(bf16[1024,768]{1,0:T(8,128)(2,1)} %bitcast.73), channel_id=1, source_target_pairs={{0,1},{1,0},{2,3},{3,2},{4,5},{5,4},{6,7},{7,6},{8,9},{9,8},{10,11... | collective-permute-start | bytes 4718600 | tf_op jit(solution)/shard_map/ppermute | solution.py:1054
  61.8 5.2 %copy-start.15 = (bf16[1,1024,768]{2,1,0:T(8,128)(2,1)S(1)}, bf16[1,1024,768]{2,1,0:T(8,128)(2,1)}, u32[]{:S(2)}) copy-start(bf16[1,1024,768]{2,1,0:T(8,128)(2,1)} %param.19) | copy-start | bytes 4718596
  66.2 12.7 %slice-start.4 = ((s8[4915200]{0:T(1024)(128)(4,1)}), s8[4194304]{0:T(1024)(128)(4,1)S(1)}, s32[]{:S(2)}) async-start(s8[4915200]{0:T(1024)(128)(4,1)} %bitcast.68), calls=%async_computation.7 | async-start | bytes 8388608
  67.0 11.9 %slice-start.5 = ((s8[4915200]{0:T(1024)(128)(4,1)}), s8[720896]{0:T(1024)(128)(4,1)S(1)}, s32[]{:S(2)}) async-start(s8[4915200]{0:T(1024)(128)(4,1)} %bitcast.68), calls=%async_computation.8 | async-start | bytes 1441792
  78.8 2.6 copy-start.9
  78.9 4.3 %copy-start.8 = (bf16[512,768]{1,0:T(8,128)(2,1)}, bf16[512,768]{1,0:T(8,128)(2,1)S(1)}, u32[]{:S(2)}) copy-start(bf16[512,768]{1,0:T(8,128)(2,1)S(1)} %get-tuple-element.120.refs_0_) | copy-start | bytes 2359300
  83.2 26.2 %slice-start = ((s8[4718592]{0:T(1024)(128)(4,1)}), s8[4194304]{0:T(1024)(128)(4,1)S(1)}, s32[]{:S(2)}) async-start(s8[4718592]{0:T(1024)(128)(4,1)} %bitcast.52), calls=%async_computation.3 | async-start | bytes 8388608
  85.7 23.7 %slice-start.1 = ((s8[4718592]{0:T(1024)(128)(4,1)}), s8[524288]{0:T(1024)(128)(4,1)S(1)}, s32[]{:S(2)}) async-start(s8[4718592]{0:T(1024)(128)(4,1)} %bitcast.52), calls=%async_computation.4 | async-start | bytes 1048576
  109.2 1.9 copy-start.4
  116.9 23.7 %copy-start.1 = (bf16[1,512,768]{2,1,0:T(8,128)(2,1)S(1)}, bf16[1,512,768]{2,1,0:T(8,128)(2,1)}, u32[]{:S(2)}) copy-start(bf16[1,512,768]{2,1,0:T(8,128)(2,1)} %param.31) | copy-start | bytes 2359300
  172.3 27.4 %copy-start.5 = (f32[512,768]{1,0:T(8,128)S(1)}, f32[512,768]{1,0:T(8,128)}, u32[]{:S(2)}) copy-start(f32[512,768]{1,0:T(8,128)} %copy-done.4) | copy-start | bytes 4718596
  199.7 7.6 %slice-start.2 = ((s8[4718592]{0:T(1024)(128)(4,1)}), s8[4194304]{0:T(1024)(128)(4,1)S(1)}, s32[]{:S(2)}) async-start(s8[4718592]{0:T(1024)(128)(4,1)} %bitcast.56), calls=%async_computation.5 | async-start | bytes 8388608
  202.4 5.0 %slice-start.3 = ((s8[4718592]{0:T(1024)(128)(4,1)}), s8[524288]{0:T(1024)(128)(4,1)S(1)}, s32[]{:S(2)}) async-start(s8[4718592]{0:T(1024)(128)(4,1)} %bitcast.56), calls=%async_computation.6 | async-start | bytes 1048576
  203.9 3.4 copy-start.7
  203.9 3.4 copy-start.13
  207.4 2.0 copy-start.11
  212.0 119.3 %collective-permute-start.2 = (bf16[1024,768]{1,0:T(8,128)(2,1)}, bf16[1024,768]{1,0:T(8,128)(2,1)}, u32[]{:S(2)}, u32[]{:S(2)}) collective-permute-start(bf16[1024,768]{1,0:T(8,128)(2,1)} %add_convert_fusion), channel_id=1, source_target_pairs={{0,1},{1,0},{2,3},{3,2},{4,5},{5,4},{6,7},{7,6},{8,9},{9,8},{10,11... | collective-permute-start | bytes 4718600 | tf_op jit(solution)/shard_map/ppermute | solution.py:1064
  214.5 20.1 %copy-start.20 = (f32[1024,128]{1,0:T(8,128)S(1)}, f32[1024,128]{1,0:T(8,128)}, u32[]{:S(2)}) copy-start(f32[1024,128]{1,0:T(8,128)} %constant.56) | copy-start | bytes 1572868
  214.5 20.5 %copy-start.22 = (f32[512,128]{1,0:T(8,128)S(1)}, f32[512,128]{1,0:T(8,128)}, u32[]{:S(2)}) copy-start(f32[512,128]{1,0:T(8,128)} %constant.57) | copy-start | bytes 786436
  237.1 87.5 %copy-start.18 = (f32[3,24,768]{2,1,0:T(8,128)S(1)}, f32[3,24,768]{2,1,0:T(8,128)}, u32[]{:S(2)}) copy-start(f32[3,24,768]{2,1,0:T(8,128)} %refs_0_.5) | copy-start | bytes 663556
  237.1 88.6 %copy-start.14 = (bf16[768,2048]{1,0:T(8,128)(2,1)S(1)}, bf16[768,2048]{1,0:T(8,128)(2,1)}, u32[]{:S(2)}) copy-start(bf16[768,2048]{1,0:T(8,128)(2,1)} %get-tuple-element.58.refs_11_) | copy-start | bytes 9437188
  325.6 2.9 copy-start.12
  328.5 2.8 copy-start.25
  338.4 2.3 copy-start.16
  338.8 3.0 copy-start.17
  340.6 2.5 copy-start.21
  340.6 3.2 copy-start.23
  (7 other events, 9.4 us)
Sparse Core Ops, SparseCore 0:
  56.9 81.6 all-gather.1
  172.4 160.4 reduce-scatter.1

commit v6 on v5

--- a/solution.py
+++ b/solution.py
@@ -557,15 +557,15 @@
 def scatter_body(counts, *refs):
     total_in = sum(counts)
     arrays, small = refs[:total_in], refs[total_in]
-    weights_ref, tokens_ref, resid_ref, gain_ref = refs[total_in + 1 : total_in + 5]
-    refs = refs[total_in + 5 :]
-    outs, grad_ref, refs = refs[:5], refs[5], refs[6:]
+    weights_ref, cross_ref, tokens_ref, resid_ref, gain_ref = refs[total_in + 1 : total_in + 6]
+    refs = refs[total_in + 6 :]
+    outs, grad_ref, memory_ref, refs = refs[:5], refs[5], refs[6], refs[7:]
     held, small_held = refs[:total_in], refs[total_in]
     refs = refs[total_in + 1 :]
     parts, mate_in, first_in, second_in, line_in = (refs[2 * i : 2 * i + 2] for i in range(5))
     load_sems, mate_sems, first_sems, second_sems, line_sems = refs[10:15]
     mate_recv, first_recv, second_recv, line_recv = refs[15:19]
-    back_in, back_sems, late_sems = refs[19:]
+    back_in, back_sems, late_sems, staged, staged_sems = refs[19:]
     z, x, core, y = place_here()
     loads = [
         pltpu.make_async_copy(source, target, load_sems.at[i])
@@ -771,24 +771,54 @@
 
     split = arrays[0].shape[0]
     cross = held[counts[0] :]
-    weights_kv, weights_q = cross[4].at[:, : 2 * D], cross[5].at[:, :D]
+    own_memory = cross[2].shape[0]
+    self_k, self_v = cross[2].at[:D], cross[3].at[:D]
+    cross_k = cross[4].at[:, own_memory : own_memory + D]
+    cross_v = cross[5].at[:, own_memory : own_memory + D]
+    top = cross[6].shape[0]
+    self_q = (cross[6], cross[7].at[: D - top])
     rows_held, back_out = cross[0], cross[1]
-    late = (
-        pltpu.make_async_copy(weights_ref.at[:, D : 3 * D], weights_kv, late_sems.at[0]),
-        pltpu.make_async_copy(weights_ref.at[:, :D], weights_q, late_sems.at[1]),
-        pltpu.make_async_copy(tokens_ref, rows_held, late_sems.at[2]),
-        pltpu.make_async_copy(resid_ref, grad_ref, late_sems.at[3]),
+    sources = (
+        weights_ref.at[:, D : 2 * D],
+        weights_ref.at[:, 2 * D : 3 * D],
+        weights_ref.at[:top, :D],
+        weights_ref.at[top:, :D],
+        tokens_ref,
+        resid_ref,
+        cross_ref.at[:, D : 2 * D],
+        cross_ref.at[:, 2 * D : 3 * D],
     )
+    targets = (self_k, self_v, *self_q, rows_held, grad_ref, cross_k, cross_v)
+    late = [
+        pltpu.make_async_copy(source, target, late_sems.at[i])
+        for i, (source, target) in enumerate(zip(sources, targets))
+    ]
     back = remote(
         back_out, back_in, back_sems.at[0], back_sems.at[1], device_of(z, x, core, 0)
     )
 
     def key_value_rows(columns):
-        value = mm(held[3][:, columns].T, weights_kv[:, :D], NT)
-        return value + mm(held[4][:, columns].T, weights_kv[:, D:], NT)
+        value = mm(held[3][:, columns].T, self_k[...], NT)
+        return value + mm(held[4][:, columns].T, self_v[...], NT)
+
+    def memory_copy(i):
+        rows = pl.ds(256 * i, 256)
+        return pltpu.make_async_copy(staged.at[i % 2], memory_ref.at[rows], staged_sems.at[i % 2])
+
+    def memory_rows(i):
+        if i == 0:
+            late[6].wait()
+            late[7].wait()
+        if i > 1:
+            memory_copy(i - 2).wait()
+        columns = slice(256 * i, 256 * (i + 1))
+        value = mm(cross[4][:, columns].T, cross_k[...], NT)
+        staged[i % 2] = value + mm(cross[5][:, columns].T, cross_v[...], NT)
+        memory_copy(i).start()
 
     def rows_before():
         late[0].wait()
+        late[1].wait()
         back_out[...] = key_value_rows(slice(0, split)).astype(bf16)
 
         @pl.when(y == 1)
@@ -796,11 +826,11 @@
             back.start()
 
     def rows_here():
-        late[1].wait()
-        late[2].wait()
-        late[3].wait()
-        grad = key_value_rows(slice(split, 2 * split)) + mm(held[2][...], weights_q[...], NT)
-        add_rows(grad)
+        for copy in late[2:6]:
+            copy.wait()
+        query = held[2][...]
+        grad = jnp.concatenate([mm(query, part[...], NT) for part in self_q], axis=1)
+        add_rows(grad + key_value_rows(slice(split, 2 * split)))
 
     def add_rows(grad):
         value = rows_held[...].astype(f32)
@@ -835,8 +865,12 @@
     send_second(2)
     line_self(2)
     line_cross(1)
+    memory_rows(0)
+    memory_rows(1)
     send_second(3)
     line_cross(2)
+    memory_rows(2)
+    memory_rows(3)
     rows_here()
     last_self()
     line_cross(3)
@@ -844,6 +878,8 @@
     arrived(second_in[0].at[3], second_recv.at[0, 3])
     put(0, wide(second_in[0], 3), True)
     rows_back()
+    memory_copy(2).wait()
+    memory_copy(3).wait()
 
     for which in (0, 1):
         for i in range(4):
@@ -858,7 +894,7 @@
                     along_line(which, i, second)[1].wait_send()
 
 
-def scatter_products(self_arrays, cross_arrays, small, weights, tokens, resid, gain):
+def scatter_products(self_arrays, cross_arrays, small, weights, cross_weights, tokens, resid, gain):
     counts = (len(self_arrays), len(cross_arrays))
     arrays = (*self_arrays, *cross_arrays)
     shard = small.shape[1]
@@ -870,12 +906,20 @@
 
     return pl.pallas_call(
         functools.partial(scatter_body, counts),
-        in_specs=[pl.BlockSpec(memory_space=pl.ANY)] * (len(arrays) + 4)
+        in_specs=[pl.BlockSpec(memory_space=pl.ANY)] * (len(arrays) + 5)
         + [pl.BlockSpec(memory_space=pltpu.VMEM)],
-        out_specs=[pl.BlockSpec(memory_space=pltpu.VMEM)] * 6,
+        out_specs=[pl.BlockSpec(memory_space=pltpu.VMEM)] * 6 + [pl.BlockSpec(memory_space=pl.ANY)],
         out_shape=[
             jax.ShapeDtypeStruct(shape, f32)
-            for shape in ((3, shard, D), (shard, D), (3, shard, D), (shard, D), (shard, small.shape[2]), resid.shape)
+            for shape in (
+                (3, shard, D),
+                (shard, D),
+                (3, shard, D),
+                (shard, D),
+                (shard, small.shape[2]),
+                resid.shape,
+                cross_arrays[2].shape,
+            )
         ],
         scratch_shapes=[pltpu.VMEM(array.shape, array.dtype) for array in (*arrays, small)]
         + buffers(32)
@@ -895,13 +939,15 @@
             dma((2, 16)),
             pltpu.VMEM(tokens.shape, bf16),
             dma((2,)),
-            dma((4,)),
+            dma((8,)),
+            pltpu.VMEM((2, 256, D), f32),
+            dma((2,)),
         ],
         compiler_params=pltpu.CompilerParams(
             collective_id=1, has_side_effects=True, vmem_limit_bytes=60 << 20
         ),
         name="scatter_products",
-    )(*arrays, small, weights, tokens, resid, gain)
+    )(*arrays, small, weights, cross_weights, tokens, resid, gain)
 
 
 def gelu_and_slope(value):
@@ -1155,8 +1201,6 @@
     turned = (((0,), (1,)), ((), ()))
     kv_other = mm(grad_key[:, enc_rows:], cross_k, turned)
     kv_other = (kv_other + mm(grad_value[:, enc_rows:], cross_v, turned)).astype(bf16)
-    grad_memory = mm(grad_key[:, :enc_rows], cross_k, turned)
-    grad_memory = grad_memory + mm(grad_value[:, :enc_rows], cross_v, turned)
     grad_two = (grad_query, grad_key, grad_value)
     grad_normed = mm(grad_query, cross_q, NT)
     grad_resid = grad_resid + norm_back(resid_one, inverse_two, gains[1], grad_normed)
@@ -1177,11 +1221,12 @@
         return jnp.stack([block[:, i * D : (i + 1) * D] for i in range(3)], axis=0)
 
     if own_kernels:
-        own_self, own_self_out, own_cross, own_cross_out, own_small, grad_input = scatter_products(
+        own_self, own_self_out, own_cross, own_cross_out, own_small, grad_input, grad_memory = scatter_products(
             (normed_before, normed_one, grad_query, grad_key, grad_value, mixed_one, grad_low),
             (normed_two, grad_two[0], memory, others, grad_two[1], grad_two[2], mixed_two, grad_low_two),
             small.reshape(-1, shard, small.shape[1]),
             all_self,
+            all_cross,
             decoder_in[0],
             grad_resid,
             gains[:1],
@@ -1213,10 +1258,20 @@
         grad_normed = mm(grad_key[:, split:], self_k, turned) + mm(grad_value[:, split:], self_v, turned)
         grad_normed = grad_normed + mm(grad_query, self_q, NT) + grad_before.astype(f32)
         grad_input = grad_resid + norm_back(tokens, inverse_one, gains[0], grad_normed)
+        grad_memory = mm(grad_two[1][:, :enc_rows], cross_k, turned)
+        grad_memory = grad_memory + mm(grad_two[2][:, :enc_rows], cross_v, turned)
 
     grad_others, own_small = lax.optimization_barrier((grad_others, own_small))
     grad_encoder = grad_memory + grad_others.astype(f32)
-    own_ffn = owned(grad_ffn)
+    if own_kernels:
+        both_ffn = lax.psum_scatter(grad_ffn, "dp", scatter_dimension=0, tiled=True)
+        both_ffn, own_small = lax.optimization_barrier((both_ffn, own_small))
+        theirs = lax.dynamic_slice_in_dim(both_ffn, (1 - seq_index) * shard, shard, axis=0)
+        own_ffn = lax.dynamic_slice_in_dim(both_ffn, seq_index * shard, shard, axis=0)
+        came = lax.ppermute(theirs, "seq", [(0, 1), (1, 0)])
+        own_ffn = own_ffn.astype(f32) + came.astype(f32)
+    else:
+        own_ffn = owned(grad_ffn)
     own_ffn_in = jnp.swapaxes(own_ffn[:, :FF].reshape(shard, units, D), 1, 2).reshape(shard, FF)
     own_ffn_out = own_ffn[:, FF:].reshape(ffn_out.shape)
 

time: 356 us -> 351 us (0.986)
  the two profiles are of different devices: /device:TPU:0 before, /device:TPU:8 now
where the time goes in v6:
time: 351 us; the launch traced here: 348 us
  Pallas kernels  254 us (72%)
  matrix products  34.7 us (10%)
  local copies, waits for them, and re-layouts  17.7 us (5%)
  between operations  14.8 us (4%)
  other arithmetic  11.6 us (3%)
  waiting for transfers between devices  8.46 us (2%)
  starting transfers between devices  6.73 us (2%)
    pallas_call x1, Pallas kernels, scatter_products(): pl.pallas_call(functools.partial(scatter_body, counts), in_specs=[pl.Bloc...  85.7 us
    pallas_call x1, Pallas kernels, gather_blocks(): pl.pallas_call(gather_body, in_specs=[pl.BlockSpec(memory_space=pltpu.VME...  48.1 us
    pallas_call x2, Pallas kernels, attend_back(): pl.pallas_call(functools.partial(attend_back_body, rows, keys, causal, st...  46.6 us
    pallas_call x2, Pallas kernels, attend(): pl.pallas_call(functools.partial(attend_body, rows, keys, causal, step, l...  44.7 us
    dot_general x12, matrix products, mm(): return lax.dot_general(a, b, dims, preferred_element_type=f32)  33.4 us
    pallas_call x1, Pallas kernels, feed_forward(): pl.pallas_call(functools.partial(feed_forward_body, rows), grid=(units, 2...  28.7 us
    unnamed x74, local copies, waits for them, and re-layouts  8.58 us
  transfers between devices with their start and end apart: 6, of which 3 were waited for; matrix products, arithmetic and copies ran while one was open for 14% of the time, Pallas kernels for 51%

profile of v6, /device:TPU:8, one launch (start us, length us, event | category | flops | bytes accessed | tf_op | source)
XLA Modules:
  0.0 347.7 jit_solution(2679945001237072172)
XLA Ops:
  7.2 48.1 %gather_blocks.1 = (bf16[32,24,3200]{2,1,0:T(8,128)(2,1)}, bf16[32,24,3072]{2,1,0:T(8,128)(2,1)}, bf16[2,24,6144]{2,1,0:T(8,128)(2,1)}) custom-call(f32[3,24,768]{2,1,0:T(8,128)} %refs_0_.5, f32[24,768]{1,0:T(8,128)} %refs_1_.5, f32[3,24,768]{2,1,0:T(8,128)} %refs_2_.1, f32[24,768]{1,0:T(8,128)} %refs_3_.1, f32[24,3072]{1,0:T(8,128)} %refs_4_.1, ...), custom_call_target="tpu_custom_call" | custom-call | tf_op jit(solution)/shard_map/gather_blocks/pallas_call | solution.py:529
  55.4 3.7 %collective-permute-start = (bf16[512,768]{1,0:T(8,128)(2,1)S(1)}, bf16[512,768]{1,0:T(8,128)(2,1)S(1)}, u32[]{:S(2)}, u32[]{:S(2)}) collective-permute-start(bf16[512,768]{1,0:T(8,128)(2,1)S(1)} %bitcast.60), channel_id=1, source_target_pairs={{0,1},{2,3},{4,5},{6,7},{8,9},{10,11},{12,13},{14,15},{16,17},{18,... | collective-permute-start | bytes 2359304 | tf_op jit(solution)/shard_map/ppermute | solution.py:1100
  60.3 1.2 slice_reduce_fusion
  61.4 2.0 fusion
  65.6 6.1 %convolution_convert_fusion.1.refs_3_.refs_5_ = bf16[1024,1536]{1,0:T(8,128)(2,1)} fusion(bf16[768,3072]{1,0:T(8,128)(2,1)} %bitcast.47, bf16[1,1024,768]{2,1,0:T(8,128)(2,1)S(1)} %copy-done.13), kind=kOutput, calls=%fused_computation.1 | convolution fusion | flops 2417491968 | bytes 7077888 | tf_op jit(solution)/shard_map/dot_general | solution.py:33
  71.7 5.0 %collective-permute-done = bf16[512,768]{1,0:T(8,128)(2,1)S(1)} collective-permute-done((bf16[512,768]{1,0:T(8,128)(2,1)S(1)}, bf16[512,768]{1,0:T(8,128)(2,1)S(1)}, u32[]{:S(2)}, u32[]{:S(2)}) %collective-permute-start) | collective-permute-done | bytes 786464 | tf_op jit(solution)/shard_map/ppermute | solution.py:1100
  77.4 2.6 convolution_convert_fusion.2.refs_4_.refs_6_
  80.0 1.7 multiply_convert_fusion.2.refs_2_
  81.7 2.6 convolution_convert_fusion.3.refs_3_.refs_5_
  84.3 21.1 %attend_causal.1 = (bf16[512,768]{1,0:T(8,128)(2,1)}, bf16[12,512,1024]{2,1,0:T(8,128)(2,1)}, f32[512,768]{1,0:T(8,128)}) custom-call(s32[1,2]{1,0:T(1,128)} %refs_0_.9, s32[1,2]{1,0:T(1,128)} %refs_1_.9, bf16[512,768]{1,0:T(8,128)(2,1)} %multiply_convert_fusion.2.refs_2_, bf16[512,1536]{1,0:T(8,128)(2,1)} %convolution_convert_fusion.3.refs_3_.refs_5_, ...), custom_call_target="tpu_custom_call" | custom-call | tf_op jit(solution)/shard_map/attend_causal/pallas_call | solution.py:204
  105.4 2.4 multiply_reduce_fusion.1
  108.0 1.7 multiply_convert_fusion.refs_2_
  110.0 5.5 %convolution_convert_fusion.refs_4_.refs_6_ = bf16[1024,1536]{1,0:T(8,128)(2,1)} fusion(bf16[1024,768]{1,0:T(8,128)(2,1)} %collective-permute-done.1.refs_10_, bf16[768,3072]{1,0:T(8,128)(2,1)S(1)} %bitcast.54), kind=kOutput, calls=%fused_computation | convolution fusion | flops 2417491968 | bytes 7077888 | tf_op jit(solution)/shard_map/dot_general | solution.py:33
  115.4 23.6 %attend_cross.1 = (bf16[512,768]{1,0:T(8,128)(2,1)}, bf16[12,512,2048]{2,1,0:T(8,128)(2,1)}, f32[512,768]{1,0:T(8,128)}) custom-call(s32[1,2]{1,0:T(1,128)} %refs_0_.9, s32[1,2]{1,0:T(1,128)} %refs_1_.9, bf16[512,768]{1,0:T(8,128)(2,1)} %multiply_convert_fusion.refs_2_, bf16[1024,1536]{1,0:T(8,128)(2,1)} %convolution_convert_fusion.1.refs_3_.refs_5_, ...), custom_call_target="tpu_custom_call" | custom-call | tf_op jit(solution)/shard_map/attend_cross/pallas_call | solution.py:204
  139.1 1.1 copy-done
  140.3 28.7 %feed_forward.1 = (bf16[512,768]{1,0:T(8,128)(2,1)}, f32[512,768]{1,0:T(8,128)S(1)}, bf16[512,768]{1,0:T(8,128)(2,1)S(1)}, bf16[512,768]{1,0:T(8,128)(2,1)S(1)}, bf16[768,6144]{1,0:T(8,128)(2,1)}) custom-call(f32[512,768]{1,0:T(8,128)} %copy-done.4, bf16[512,768]{1,0:T(8,128)(2,1)S(1)} %copy-done, bf16[768,3072]{1,0:T(8,128)(2,1)} %bitcast.48, ...), custom_call_target="tpu_custom_call" | custom-call | tf_op jit(solution)/shard_map/feed_forward/pallas_call | solution.py:1012
  170.8 27.4 %attend_cross_back.1 = (bf16[512,768]{1,0:T(8,128)(2,1)}, bf16[768,2048]{1,0:T(8,128)(2,1)}, bf16[768,2048]{1,0:T(8,128)(2,1)}) custom-call(s32[1,2]{1,0:T(1,128)} %refs_0_.9, s32[1,2]{1,0:T(1,128)} %refs_1_.9, bf16[512,768]{1,0:T(8,128)(2,1)} %multiply_convert_fusion.refs_2_, bf16[1024,1536]{1,0:T(8,128)(2,1)} %convolution_convert_fusion.1.refs_3_.refs_5_, ...), custom_call_target="tpu_custom_call" | custom-call | tf_op jit(solution)/shard_map/attend_cross_back/pallas_call | solution.py:316
  198.2 2.6 multiply_reduce_fusion
  200.8 1.6 fusion.28
  202.3 3.3 convolution_convert_fusion.4.refs_10_
  205.7 1.5 fusion.13
  207.6 1.5 add_convert_fusion
  209.1 2.8 collective-permute-start.2
  211.9 19.3 %attend_causal_back.1 = (bf16[512,768]{1,0:T(8,128)(2,1)}, bf16[768,1024]{1,0:T(8,128)(2,1)}, bf16[768,1024]{1,0:T(8,128)(2,1)}, f32[6,4,256]{2,1,0:T(4,128)}, f32[6,4,128]{2,1,0:T(4,128)}) custom-call(s32[1,2]{1,0:T(1,128)} %refs_0_.9, s32[1,2]{1,0:T(1,128)} %refs_1_.9, bf16[512,768]{1,0:T(8,128)(2,1)} %multiply_convert_fusion.2.refs_2_, ...), custom_call_target="tpu_custom_call" | custom-call | tf_op jit(solution)/shard_map/attend_causal_back/pallas_call | solution.py:316
  234.5 85.7 %scatter_products.1 = (f32[3,24,768]{2,1,0:T(8,128)}, f32[24,768]{1,0:T(8,128)}, f32[3,24,768]{2,1,0:T(8,128)}, f32[24,768]{1,0:T(8,128)}, f32[24,128]{1,0:T(8,1...) custom-call(bf16[512,768]{1,0:T(8,128)(2,1)} %copy-done.10, bf16[512,768]{1,0:T(8,128)(2,1)} %copy-done.11, ...), custom_call_target="tpu_custom_call" | custom-call | tf_op jit(solution)/shard_map/scatter_products/pallas_call | solution.py:907
  320.1 1.0 multiply_reduce_fusion.4
  321.2 1.1 multiply_reduce_fusion.3
  323.4 3.9 %add_bitcast_fusion = f32[1,1024,768]{2,1,0:T(8,128)} fusion(f32[1024,768]{1,0:T(8,128)} %get-tuple-element.71, bf16[1024,768]{1,0:T(8,128)(2,1)S(1)} %collective-permute-done.2), kind=kLoop, calls=%fused_computation.2 | loop fusion | flops 1572864 | bytes 7864320 | tf_op jit(solution)/shard_map/broadcast_in_dim | solution.py:1294
  327.9 3.1 collective-permute-done.3
  333.1 1.2 multiply_reduce_fusion.2
  334.4 1.8 reshape.119
  336.8 1.1 copy.62
  (113 shorter events, 17.1 us)
Async XLA Ops:
  7.2 48.2 %copy-start.6 = (bf16[1,512,768]{2,1,0:T(8,128)(2,1)S(1)}, bf16[1,512,768]{2,1,0:T(8,128)(2,1)}, u32[]{:S(2)}) copy-start(bf16[1,512,768]{2,1,0:T(8,128)(2,1)} %param.18) | copy-start | bytes 2359300
  7.2 131.9 %all-gather.2.cloned.1.call-start = ((), (), s32[]{:S(2)}) async-start(), calls=%async_computation.1 | async-start | bytes 10027008 | tf_op jit(solution)/shard_map/all_gather | solution.py:1143
  7.2 54.2 %copy-start.26 = (bf16[6,768]{1,0:T(8,128)(2,1)S(1)}, bf16[6,768]{1,0:T(8,128)(2,1)}, u32[]{:S(2)}) copy-start(bf16[6,768]{1,0:T(8,128)(2,1)} %constant.50.clone) | copy-start | bytes 27652
  55.3 266.9 %reduce-scatter.2.cloned.1.call-start = ((), (), s32[]{:S(2)}) async-start(), calls=%async_computation.2 | async-start | bytes 10027008 | tf_op jit(solution)/shard_map/reduce_scatter | solution.py:1267
  55.4 21.3 %collective-permute-start = (bf16[512,768]{1,0:T(8,128)(2,1)S(1)}, bf16[512,768]{1,0:T(8,128)(2,1)S(1)}, u32[]{:S(2)}, u32[]{:S(2)}) collective-permute-start(bf16[512,768]{1,0:T(8,128)(2,1)S(1)} %bitcast.60), channel_id=1, source_target_pairs={{0,1},{2,3},{4,5},{6,7},{8,9},{10,11},{12,13},{14,15},{16,17},{18,... | collective-permute-start | bytes 2359304 | tf_op jit(solution)/shard_map/ppermute | solution.py:1100
  59.1 50.9 %collective-permute-start.1 = (bf16[1024,768]{1,0:T(8,128)(2,1)}, bf16[1024,768]{1,0:T(8,128)(2,1)}, u32[]{:S(2)}, u32[]{:S(2)}) collective-permute-start(bf16[1024,768]{1,0:T(8,128)(2,1)} %bitcast.72), channel_id=1, source_target_pairs={{0,1},{1,0},{2,3},{3,2},{4,5},{5,4},{6,7},{7,6},{8,9},{9,8},{10,11... | collective-permute-start | bytes 4718600 | tf_op jit(solution)/shard_map/ppermute | solution.py:1100
  61.4 4.1 %copy-start.13 = (bf16[1,1024,768]{2,1,0:T(8,128)(2,1)S(1)}, bf16[1,1024,768]{2,1,0:T(8,128)(2,1)}, u32[]{:S(2)}) copy-start(bf16[1,1024,768]{2,1,0:T(8,128)(2,1)} %param.19) | copy-start | bytes 4718596
  64.7 12.7 %slice-start.4 = ((s8[4915200]{0:T(1024)(128)(4,1)}), s8[4194304]{0:T(1024)(128)(4,1)S(1)}, s32[]{:S(2)}) async-start(s8[4915200]{0:T(1024)(128)(4,1)} %bitcast.67), calls=%async_computation.7 | async-start | bytes 8388608
  65.6 11.9 %slice-start.5 = ((s8[4915200]{0:T(1024)(128)(4,1)}), s8[720896]{0:T(1024)(128)(4,1)S(1)}, s32[]{:S(2)}) async-start(s8[4915200]{0:T(1024)(128)(4,1)} %bitcast.67), calls=%async_computation.8 | async-start | bytes 1441792
  77.4 2.6 copy-start.11
  77.4 4.3 %copy-start.10 = (bf16[512,768]{1,0:T(8,128)(2,1)}, bf16[512,768]{1,0:T(8,128)(2,1)S(1)}, u32[]{:S(2)}) copy-start(bf16[512,768]{1,0:T(8,128)(2,1)S(1)} %get-tuple-element.126.refs_0_) | copy-start | bytes 2359300
  81.7 26.2 %slice-start = ((s8[4718592]{0:T(1024)(128)(4,1)}), s8[4194304]{0:T(1024)(128)(4,1)S(1)}, s32[]{:S(2)}) async-start(s8[4718592]{0:T(1024)(128)(4,1)} %bitcast.51), calls=%async_computation.3 | async-start | bytes 8388608
  84.3 23.7 %slice-start.1 = ((s8[4718592]{0:T(1024)(128)(4,1)}), s8[524288]{0:T(1024)(128)(4,1)S(1)}, s32[]{:S(2)}) async-start(s8[4718592]{0:T(1024)(128)(4,1)} %bitcast.51), calls=%async_computation.4 | async-start | bytes 1048576
  107.7 1.9 copy-start.4
  115.4 23.7 %copy-start.1 = (bf16[1,512,768]{2,1,0:T(8,128)(2,1)S(1)}, bf16[1,512,768]{2,1,0:T(8,128)(2,1)}, u32[]{:S(2)}) copy-start(bf16[1,512,768]{2,1,0:T(8,128)(2,1)} %param.31) | copy-start | bytes 2359300
  170.8 27.4 %copy-start.5 = (f32[512,768]{1,0:T(8,128)S(1)}, f32[512,768]{1,0:T(8,128)}, u32[]{:S(2)}) copy-start(f32[512,768]{1,0:T(8,128)} %copy-done.4) | copy-start | bytes 4718596
  198.2 7.5 %slice-start.2 = ((s8[4718592]{0:T(1024)(128)(4,1)}), s8[4194304]{0:T(1024)(128)(4,1)S(1)}, s32[]{:S(2)}) async-start(s8[4718592]{0:T(1024)(128)(4,1)} %bitcast.55), calls=%async_computation.5 | async-start | bytes 8388608
  200.8 4.9 %slice-start.3 = ((s8[4718592]{0:T(1024)(128)(4,1)}), s8[524288]{0:T(1024)(128)(4,1)S(1)}, s32[]{:S(2)}) async-start(s8[4718592]{0:T(1024)(128)(4,1)} %bitcast.55), calls=%async_computation.6 | async-start | bytes 1048576
  202.3 3.3 copy-start.9
  202.3 3.4 copy-start.7
  209.1 113.2 %collective-permute-start.2 = (bf16[1024,768]{1,0:T(8,128)(2,1)S(1)}, bf16[1024,768]{1,0:T(8,128)(2,1)S(1)}, u32[]{:S(2)}, u32[]{:S(2)}) collective-permute-start(bf16[1024,768]{1,0:T(8,128)(2,1)S(1)} %add_convert_fusion), channel_id=1, source_target_pairs={{0,1},{1,0},{2,3},{3,2},{4,5},{5,4},{6,7},{7,6},{8,9},{9,8},{10,11... | collective-permute-start | bytes 4718600 | tf_op jit(solution)/shard_map/ppermute | solution.py:1110
  211.9 20.0 %copy-start.19 = (f32[1024,128]{1,0:T(8,128)S(1)}, f32[1024,128]{1,0:T(8,128)}, u32[]{:S(2)}) copy-start(f32[1024,128]{1,0:T(8,128)} %constant.66) | copy-start | bytes 1572868
  211.9 20.4 %copy-start.21 = (f32[512,128]{1,0:T(8,128)S(1)}, f32[512,128]{1,0:T(8,128)}, u32[]{:S(2)}) copy-start(f32[512,128]{1,0:T(8,128)} %constant.67) | copy-start | bytes 786436
  234.5 86.7 %copy-start.16 = (f32[3,24,768]{2,1,0:T(8,128)S(1)}, f32[3,24,768]{2,1,0:T(8,128)}, u32[]{:S(2)}) copy-start(f32[3,24,768]{2,1,0:T(8,128)} %refs_0_.5) | copy-start | bytes 663556
  323.3 7.7 %collective-permute-start.3 = (bf16[24,6144]{1,0:T(8,128)(2,1)S(1)}, bf16[24,6144]{1,0:T(8,128)(2,1)S(1)}, u32[]{:S(2)}, u32[]{:S(2)}) collective-permute-start(bf16[24,6144]{1,0:T(8,128)(2,1)S(1)} %constant_dynamic-slice_fusion), channel_id=1, source_target_pairs={{0,1},{1,0},{2,3},{3,2},{4,5},{5,4},{6,7},{7,6},{8,9},{9,8},{10,11... | collective-permute-start | bytes 884744 | tf_op jit(solution)/shard_map/ppermute | solution.py:1271
  323.3 3.9 %copy-start.24 = (f32[24,128]{1,0:T(8,128)S(1)}, f32[24,128]{1,0:T(8,128)}, u32[]{:S(2)}) copy-start(f32[24,128]{1,0:T(8,128)} %get-tuple-element.82) | copy-start | bytes 36868
  323.4 7.6 %copy-start.18 = (bf16[48,6144]{1,0:T(8,128)(2,1)S(1)}, bf16[48,6144]{1,0:T(8,128)(2,1)}, u32[]{:S(2)}) copy-start(bf16[48,6144]{1,0:T(8,128)(2,1)} %reduce-scatter.2.cloned.1.call-done) | copy-start | bytes 1769476
  332.7 3.5 copy-start.25
  332.7 4.0 %copy-start.14 = (f32[512,768]{1,0:T(8,128)S(1)}, f32[512,768]{1,0:T(8,128)}, u32[]{:S(2)}) copy-start(f32[512,768]{1,0:T(8,128)} %get-tuple-element.70) | copy-start | bytes 4718596
  333.1 4.8 %copy-start.15 = (f32[24,3072]{1,0:T(8,128)}, f32[24,3072]{1,0:T(8,128)S(1)}, u32[]{:S(2)}) copy-start(f32[24,3072]{1,0:T(8,128)S(1)} %copy.50) | copy-start | bytes 884740
  336.7 2.5 copy-start.20
  336.7 3.2 copy-start.22
  (7 other events, 9.6 us)
Sparse Core Ops, SparseCore 0:
  55.5 80.7 all-gather.1
  170.9 131.6 reduce-scatter.1

commit v7 on v6

--- a/solution.py
+++ b/solution.py
@@ -571,7 +571,7 @@
         pltpu.make_async_copy(source, target, load_sems.at[i])
         for i, (source, target) in enumerate(zip((*arrays, small), (*held, small_held)))
     ]
-    for load in loads:
+    for load in (*loads[counts[0] :], *loads[: counts[0]]):
         load.start()
     greet_neighbours(z, x, core, y)
     half = z // 2
@@ -866,14 +866,14 @@
     line_self(2)
     line_cross(1)
     memory_rows(0)
-    memory_rows(1)
     send_second(3)
     line_cross(2)
+    rows_here()
+    memory_rows(1)
+    last_self()
+    line_cross(3)
     memory_rows(2)
     memory_rows(3)
-    rows_here()
-    last_self()
-    line_cross(3)
     from_line(1, 0, lambda value: put(1, value, True))
     arrived(second_in[0].at[3], second_recv.at[0, 3])
     put(0, wide(second_in[0], 3), True)

time: 351 us -> 348 us (level)
  the two profiles are of different devices: /device:TPU:8 before, /device:TPU:0 now
where the time goes in v7:
time: 348 us; the launch traced here: 342 us
  Pallas kernels  249 us (72%)
  matrix products  34.7 us (10%)
  local copies, waits for them, and re-layouts  17.7 us (5%)
  between operations  14.7 us (4%)
  other arithmetic  11.6 us (3%)
  starting transfers between devices  7.5 us (2%)
  waiting for transfers between devices  6.75 us (2%)
    pallas_call x1, Pallas kernels, scatter_products(): pl.pallas_call(functools.partial(scatter_body, counts), in_specs=[pl.Bloc...  79.9 us
    pallas_call x1, Pallas kernels, gather_blocks(): pl.pallas_call(gather_body, in_specs=[pl.BlockSpec(memory_space=pltpu.VME...  49.5 us
    pallas_call x2, Pallas kernels, attend_back(): pl.pallas_call(functools.partial(attend_back_body, rows, keys, causal, st...  46.7 us
    pallas_call x2, Pallas kernels, attend(): pl.pallas_call(functools.partial(attend_body, rows, keys, causal, step, l...  44.7 us
    dot_general x12, matrix products, mm(): return lax.dot_general(a, b, dims, preferred_element_type=f32)  33.4 us
    pallas_call x1, Pallas kernels, feed_forward(): pl.pallas_call(functools.partial(feed_forward_body, rows), grid=(units, 2...  28.7 us
    unnamed x74, local copies, waits for them, and re-layouts  8.58 us
  transfers between devices with their start and end apart: 6, of which 3 were waited for; matrix products, arithmetic and copies ran while one was open for 15% of the time, Pallas kernels for 50%

profile of v7, /device:TPU:0, one launch (start us, length us, event | category | flops | bytes accessed | tf_op | source)
XLA Modules:
  0.0 342.4 jit_solution(3350706126916167515)
XLA Ops:
  7.2 49.5 %gather_blocks.1 = (bf16[32,24,3200]{2,1,0:T(8,128)(2,1)}, bf16[32,24,3072]{2,1,0:T(8,128)(2,1)}, bf16[2,24,6144]{2,1,0:T(8,128)(2,1)}) custom-call(f32[3,24,768]{2,1,0:T(8,128)} %refs_0_.5, f32[24,768]{1,0:T(8,128)} %refs_1_.5, f32[3,24,768]{2,1,0:T(8,128)} %refs_2_.1, f32[24,768]{1,0:T(8,128)} %refs_3_.1, f32[24,3072]{1,0:T(8,128)} %refs_4_.1, ...), custom_call_target="tpu_custom_call" | custom-call | tf_op jit(solution)/shard_map/gather_blocks/pallas_call | solution.py:529
  56.9 3.7 %collective-permute-start = (bf16[512,768]{1,0:T(8,128)(2,1)S(1)}, bf16[512,768]{1,0:T(8,128)(2,1)S(1)}, u32[]{:S(2)}, u32[]{:S(2)}) collective-permute-start(bf16[512,768]{1,0:T(8,128)(2,1)S(1)} %bitcast.60), channel_id=1, source_target_pairs={{0,1},{2,3},{4,5},{6,7},{8,9},{10,11},{12,13},{14,15},{16,17},{18,... | collective-permute-start | bytes 2359304 | tf_op jit(solution)/shard_map/ppermute | solution.py:1100
  61.7 1.2 slice_reduce_fusion
  62.9 2.1 fusion
  67.1 6.0 %convolution_convert_fusion.1.refs_3_.refs_5_ = bf16[1024,1536]{1,0:T(8,128)(2,1)} fusion(bf16[768,3072]{1,0:T(8,128)(2,1)} %bitcast.47, bf16[1,1024,768]{2,1,0:T(8,128)(2,1)S(1)} %copy-done.13), kind=kOutput, calls=%fused_computation.1 | convolution fusion | flops 2417491968 | bytes 7077888 | tf_op jit(solution)/shard_map/dot_general | solution.py:33
  73.1 5.0 %collective-permute-done = bf16[512,768]{1,0:T(8,128)(2,1)S(1)} collective-permute-done((bf16[512,768]{1,0:T(8,128)(2,1)S(1)}, bf16[512,768]{1,0:T(8,128)(2,1)S(1)}, u32[]{:S(2)}, u32[]{:S(2)}) %collective-permute-start) | collective-permute-done | bytes 786464 | tf_op jit(solution)/shard_map/ppermute | solution.py:1100
  78.9 2.6 convolution_convert_fusion.2.refs_4_.refs_6_
  81.5 1.7 multiply_convert_fusion.2.refs_2_
  83.2 2.6 convolution_convert_fusion.3.refs_3_.refs_5_
  85.7 21.1 %attend_causal.1 = (bf16[512,768]{1,0:T(8,128)(2,1)}, bf16[12,512,1024]{2,1,0:T(8,128)(2,1)}, f32[512,768]{1,0:T(8,128)}) custom-call(s32[1,2]{1,0:T(1,128)} %refs_0_.9, s32[1,2]{1,0:T(1,128)} %refs_1_.9, bf16[512,768]{1,0:T(8,128)(2,1)} %multiply_convert_fusion.2.refs_2_, bf16[512,1536]{1,0:T(8,128)(2,1)} %convolution_convert_fusion.3.refs_3_.refs_5_, ...), custom_call_target="tpu_custom_call" | custom-call | tf_op jit(solution)/shard_map/attend_causal/pallas_call | solution.py:204
  106.8 2.4 multiply_reduce_fusion.1
  109.5 1.7 multiply_convert_fusion.refs_2_
  111.4 5.5 %convolution_convert_fusion.refs_4_.refs_6_ = bf16[1024,1536]{1,0:T(8,128)(2,1)} fusion(bf16[1024,768]{1,0:T(8,128)(2,1)} %collective-permute-done.1.refs_10_, bf16[768,3072]{1,0:T(8,128)(2,1)S(1)} %bitcast.54), kind=kOutput, calls=%fused_computation | convolution fusion | flops 2417491968 | bytes 7077888 | tf_op jit(solution)/shard_map/dot_general | solution.py:33
  116.9 23.6 %attend_cross.1 = (bf16[512,768]{1,0:T(8,128)(2,1)}, bf16[12,512,2048]{2,1,0:T(8,128)(2,1)}, f32[512,768]{1,0:T(8,128)}) custom-call(s32[1,2]{1,0:T(1,128)} %refs_0_.9, s32[1,2]{1,0:T(1,128)} %refs_1_.9, bf16[512,768]{1,0:T(8,128)(2,1)} %multiply_convert_fusion.refs_2_, bf16[1024,1536]{1,0:T(8,128)(2,1)} %convolution_convert_fusion.1.refs_3_.refs_5_, ...), custom_call_target="tpu_custom_call" | custom-call | tf_op jit(solution)/shard_map/attend_cross/pallas_call | solution.py:204
  140.6 1.1 copy-done
  141.7 28.7 %feed_forward.1 = (bf16[512,768]{1,0:T(8,128)(2,1)}, f32[512,768]{1,0:T(8,128)S(1)}, bf16[512,768]{1,0:T(8,128)(2,1)S(1)}, bf16[512,768]{1,0:T(8,128)(2,1)S(1)}, bf16[768,6144]{1,0:T(8,128)(2,1)}) custom-call(f32[512,768]{1,0:T(8,128)} %copy-done.4, bf16[512,768]{1,0:T(8,128)(2,1)S(1)} %copy-done, bf16[768,3072]{1,0:T(8,128)(2,1)} %bitcast.48, ...), custom_call_target="tpu_custom_call" | custom-call | tf_op jit(solution)/shard_map/feed_forward/pallas_call | solution.py:1012
  172.3 27.4 %attend_cross_back.1 = (bf16[512,768]{1,0:T(8,128)(2,1)}, bf16[768,2048]{1,0:T(8,128)(2,1)}, bf16[768,2048]{1,0:T(8,128)(2,1)}) custom-call(s32[1,2]{1,0:T(1,128)} %refs_0_.9, s32[1,2]{1,0:T(1,128)} %refs_1_.9, bf16[512,768]{1,0:T(8,128)(2,1)} %multiply_convert_fusion.refs_2_, bf16[1024,1536]{1,0:T(8,128)(2,1)} %convolution_convert_fusion.1.refs_3_.refs_5_, ...), custom_call_target="tpu_custom_call" | custom-call | tf_op jit(solution)/shard_map/attend_cross_back/pallas_call | solution.py:316
  199.6 2.6 multiply_reduce_fusion
  202.2 1.6 fusion.28
  203.8 3.3 convolution_convert_fusion.4.refs_10_
  207.2 1.5 fusion.13
  209.0 1.5 add_convert_fusion
  210.5 2.8 collective-permute-start.2
  213.3 19.3 %attend_causal_back.1 = (bf16[512,768]{1,0:T(8,128)(2,1)}, bf16[768,1024]{1,0:T(8,128)(2,1)}, bf16[768,1024]{1,0:T(8,128)(2,1)}, f32[6,4,256]{2,1,0:T(4,128)}, f32[6,4,128]{2,1,0:T(4,128)}) custom-call(s32[1,2]{1,0:T(1,128)} %refs_0_.9, s32[1,2]{1,0:T(1,128)} %refs_1_.9, bf16[512,768]{1,0:T(8,128)(2,1)} %multiply_convert_fusion.2.refs_2_, ...), custom_call_target="tpu_custom_call" | custom-call | tf_op jit(solution)/shard_map/attend_causal_back/pallas_call | solution.py:316
  235.9 79.9 %scatter_products.1 = (f32[3,24,768]{2,1,0:T(8,128)}, f32[24,768]{1,0:T(8,128)}, f32[3,24,768]{2,1,0:T(8,128)}, f32[24,768]{1,0:T(8,128)}, f32[24,128]{1,0:T(8,1...) custom-call(bf16[512,768]{1,0:T(8,128)(2,1)} %copy-done.10, bf16[512,768]{1,0:T(8,128)(2,1)} %copy-done.11, ...), custom_call_target="tpu_custom_call" | custom-call | tf_op jit(solution)/shard_map/scatter_products/pallas_call | solution.py:907
  315.8 1.0 multiply_reduce_fusion.4
  316.9 1.1 multiply_reduce_fusion.3
  319.8 3.9 %add_bitcast_fusion = f32[1,1024,768]{2,1,0:T(8,128)} fusion(f32[1024,768]{1,0:T(8,128)} %get-tuple-element.71, bf16[1024,768]{1,0:T(8,128)(2,1)S(1)} %collective-permute-done.2), kind=kLoop, calls=%fused_computation.2 | loop fusion | flops 1572864 | bytes 7864320 | tf_op jit(solution)/shard_map/broadcast_in_dim | solution.py:1294
  324.4 1.4 collective-permute-done.3
  327.9 1.2 multiply_reduce_fusion.2
  329.1 1.8 reshape.119
  331.5 1.1 copy.62
  (113 shorter events, 17.9 us)
Async XLA Ops:
  7.2 49.7 %copy-start.6 = (bf16[1,512,768]{2,1,0:T(8,128)(2,1)S(1)}, bf16[1,512,768]{2,1,0:T(8,128)(2,1)}, u32[]{:S(2)}) copy-start(bf16[1,512,768]{2,1,0:T(8,128)(2,1)} %param.18) | copy-start | bytes 2359300
  7.2 133.4 %all-gather.2.cloned.1.call-start = ((), (), s32[]{:S(2)}) async-start(), calls=%async_computation.1 | async-start | bytes 10027008 | tf_op jit(solution)/shard_map/all_gather | solution.py:1143
  7.2 55.6 %copy-start.26 = (bf16[6,768]{1,0:T(8,128)(2,1)S(1)}, bf16[6,768]{1,0:T(8,128)(2,1)}, u32[]{:S(2)}) copy-start(bf16[6,768]{1,0:T(8,128)(2,1)} %constant.50.clone) | copy-start | bytes 27652
  56.8 261.2 %reduce-scatter.2.cloned.1.call-start = ((), (), s32[]{:S(2)}) async-start(), calls=%async_computation.2 | async-start | bytes 10027008 | tf_op jit(solution)/shard_map/reduce_scatter | solution.py:1267
  56.9 21.3 %collective-permute-start = (bf16[512,768]{1,0:T(8,128)(2,1)S(1)}, bf16[512,768]{1,0:T(8,128)(2,1)S(1)}, u32[]{:S(2)}, u32[]{:S(2)}) collective-permute-start(bf16[512,768]{1,0:T(8,128)(2,1)S(1)} %bitcast.60), channel_id=1, source_target_pairs={{0,1},{2,3},{4,5},{6,7},{8,9},{10,11},{12,13},{14,15},{16,17},{18,... | collective-permute-start | bytes 2359304 | tf_op jit(solution)/shard_map/ppermute | solution.py:1100
  60.5 50.9 %collective-permute-start.1 = (bf16[1024,768]{1,0:T(8,128)(2,1)}, bf16[1024,768]{1,0:T(8,128)(2,1)}, u32[]{:S(2)}, u32[]{:S(2)}) collective-permute-start(bf16[1024,768]{1,0:T(8,128)(2,1)} %bitcast.72), channel_id=1, source_target_pairs={{0,1},{1,0},{2,3},{3,2},{4,5},{5,4},{6,7},{7,6},{8,9},{9,8},{10,11... | collective-permute-start | bytes 4718600 | tf_op jit(solution)/shard_map/ppermute | solution.py:1100
  62.9 4.2 %copy-start.13 = (bf16[1,1024,768]{2,1,0:T(8,128)(2,1)S(1)}, bf16[1,1024,768]{2,1,0:T(8,128)(2,1)}, u32[]{:S(2)}) copy-start(bf16[1,1024,768]{2,1,0:T(8,128)(2,1)} %param.19) | copy-start | bytes 4718596
  66.2 12.6 %slice-start.4 = ((s8[4915200]{0:T(1024)(128)(4,1)}), s8[4194304]{0:T(1024)(128)(4,1)S(1)}, s32[]{:S(2)}) async-start(s8[4915200]{0:T(1024)(128)(4,1)} %bitcast.67), calls=%async_computation.7 | async-start | bytes 8388608
  67.1 11.8 %slice-start.5 = ((s8[4915200]{0:T(1024)(128)(4,1)}), s8[720896]{0:T(1024)(128)(4,1)S(1)}, s32[]{:S(2)}) async-start(s8[4915200]{0:T(1024)(128)(4,1)} %bitcast.67), calls=%async_computation.8 | async-start | bytes 1441792
  78.8 2.6 copy-start.11
  78.9 4.3 %copy-start.10 = (bf16[512,768]{1,0:T(8,128)(2,1)}, bf16[512,768]{1,0:T(8,128)(2,1)S(1)}, u32[]{:S(2)}) copy-start(bf16[512,768]{1,0:T(8,128)(2,1)S(1)} %get-tuple-element.126.refs_0_) | copy-start | bytes 2359300
  83.2 26.2 %slice-start = ((s8[4718592]{0:T(1024)(128)(4,1)}), s8[4194304]{0:T(1024)(128)(4,1)S(1)}, s32[]{:S(2)}) async-start(s8[4718592]{0:T(1024)(128)(4,1)} %bitcast.51), calls=%async_computation.3 | async-start | bytes 8388608
  85.7 23.7 %slice-start.1 = ((s8[4718592]{0:T(1024)(128)(4,1)}), s8[524288]{0:T(1024)(128)(4,1)S(1)}, s32[]{:S(2)}) async-start(s8[4718592]{0:T(1024)(128)(4,1)} %bitcast.51), calls=%async_computation.4 | async-start | bytes 1048576
  109.2 1.9 copy-start.4
  116.9 23.7 %copy-start.1 = (bf16[1,512,768]{2,1,0:T(8,128)(2,1)S(1)}, bf16[1,512,768]{2,1,0:T(8,128)(2,1)}, u32[]{:S(2)}) copy-start(bf16[1,512,768]{2,1,0:T(8,128)(2,1)} %param.31) | copy-start | bytes 2359300
  172.2 27.4 %copy-start.5 = (f32[512,768]{1,0:T(8,128)S(1)}, f32[512,768]{1,0:T(8,128)}, u32[]{:S(2)}) copy-start(f32[512,768]{1,0:T(8,128)} %copy-done.4) | copy-start | bytes 4718596
  199.6 7.5 %slice-start.2 = ((s8[4718592]{0:T(1024)(128)(4,1)}), s8[4194304]{0:T(1024)(128)(4,1)S(1)}, s32[]{:S(2)}) async-start(s8[4718592]{0:T(1024)(128)(4,1)} %bitcast.55), calls=%async_computation.5 | async-start | bytes 8388608
  202.2 4.9 %slice-start.3 = ((s8[4718592]{0:T(1024)(128)(4,1)}), s8[524288]{0:T(1024)(128)(4,1)S(1)}, s32[]{:S(2)}) async-start(s8[4718592]{0:T(1024)(128)(4,1)} %bitcast.55), calls=%async_computation.6 | async-start | bytes 1048576
  203.8 3.3 copy-start.9
  203.8 3.4 copy-start.7
  210.5 107.4 %collective-permute-start.2 = (bf16[1024,768]{1,0:T(8,128)(2,1)S(1)}, bf16[1024,768]{1,0:T(8,128)(2,1)S(1)}, u32[]{:S(2)}, u32[]{:S(2)}) collective-permute-start(bf16[1024,768]{1,0:T(8,128)(2,1)S(1)} %add_convert_fusion), channel_id=1, source_target_pairs={{0,1},{1,0},{2,3},{3,2},{4,5},{5,4},{6,7},{7,6},{8,9},{9,8},{10,11... | collective-permute-start | bytes 4718600 | tf_op jit(solution)/shard_map/ppermute | solution.py:1110
  213.3 20.1 %copy-start.19 = (f32[1024,128]{1,0:T(8,128)S(1)}, f32[1024,128]{1,0:T(8,128)}, u32[]{:S(2)}) copy-start(f32[1024,128]{1,0:T(8,128)} %constant.66) | copy-start | bytes 1572868
  213.3 20.4 %copy-start.21 = (f32[512,128]{1,0:T(8,128)S(1)}, f32[512,128]{1,0:T(8,128)}, u32[]{:S(2)}) copy-start(f32[512,128]{1,0:T(8,128)} %constant.67) | copy-start | bytes 786436
  235.9 81.0 %copy-start.16 = (f32[3,24,768]{2,1,0:T(8,128)S(1)}, f32[3,24,768]{2,1,0:T(8,128)}, u32[]{:S(2)}) copy-start(f32[3,24,768]{2,1,0:T(8,128)} %refs_0_.5) | copy-start | bytes 663556
  319.0 6.8 %collective-permute-start.3 = (bf16[24,6144]{1,0:T(8,128)(2,1)S(1)}, bf16[24,6144]{1,0:T(8,128)(2,1)S(1)}, u32[]{:S(2)}, u32[]{:S(2)}) collective-permute-start(bf16[24,6144]{1,0:T(8,128)(2,1)S(1)} %constant_dynamic-slice_fusion), channel_id=1, source_target_pairs={{0,1},{1,0},{2,3},{3,2},{4,5},{5,4},{6,7},{7,6},{8,9},{9,8},{10,11... | collective-permute-start | bytes 884744 | tf_op jit(solution)/shard_map/ppermute | solution.py:1271
  319.8 3.9 %copy-start.24 = (f32[24,128]{1,0:T(8,128)S(1)}, f32[24,128]{1,0:T(8,128)}, u32[]{:S(2)}) copy-start(f32[24,128]{1,0:T(8,128)} %get-tuple-element.82) | copy-start | bytes 36868
  319.8 5.9 %copy-start.18 = (bf16[48,6144]{1,0:T(8,128)(2,1)S(1)}, bf16[48,6144]{1,0:T(8,128)(2,1)}, u32[]{:S(2)}) copy-start(bf16[48,6144]{1,0:T(8,128)(2,1)} %reduce-scatter.2.cloned.1.call-done) | copy-start | bytes 1769476
  327.4 3.5 %copy-start.25 = (f32[3,24]{1,0:T(4,128)S(1)}, f32[3,24]{1,0:T(4,128)}, u32[]{:S(2)}) copy-start(f32[3,24]{1,0:T(4,128)} %refs_6_.1) | copy-start | bytes 868
  327.4 4.0 %copy-start.14 = (f32[512,768]{1,0:T(8,128)S(1)}, f32[512,768]{1,0:T(8,128)}, u32[]{:S(2)}) copy-start(f32[512,768]{1,0:T(8,128)} %get-tuple-element.70) | copy-start | bytes 4718596
  327.9 4.8 %copy-start.15 = (f32[24,3072]{1,0:T(8,128)}, f32[24,3072]{1,0:T(8,128)S(1)}, u32[]{:S(2)}) copy-start(f32[24,3072]{1,0:T(8,128)S(1)} %copy.50) | copy-start | bytes 884740
  331.5 2.5 copy-start.20
  331.5 3.2 copy-start.22
  (7 other events, 9.6 us)
Sparse Core Ops, SparseCore 0:
  56.9 81.6 all-gather.1
  172.4 132.9 reduce-scatter.1

commit v8 on v7

--- a/solution.py
+++ b/solution.py
@@ -558,7 +558,8 @@
     total_in = sum(counts)
     arrays, small = refs[:total_in], refs[total_in]
     weights_ref, cross_ref, tokens_ref, resid_ref, gain_ref = refs[total_in + 1 : total_in + 6]
-    refs = refs[total_in + 6 :]
+    own_weights = refs[total_in + 6 : total_in + 8]
+    refs = refs[total_in + 8 :]
     outs, grad_ref, memory_ref, refs = refs[:5], refs[5], refs[6], refs[7:]
     held, small_held = refs[:total_in], refs[total_in]
     refs = refs[total_in + 1 :]
@@ -877,6 +878,14 @@
     from_line(1, 0, lambda value: put(1, value, True))
     arrived(second_in[0].at[3], second_recv.at[0, 3])
     put(0, wide(second_in[0], 3), True)
+    def by_rows(which, j):
+        weight = own_weights[which][j].astype(bf16).astype(f32)
+        return jnp.sum(weight * outs[2 * which][j], axis=1, keepdims=True)
+
+    lane = lax.broadcasted_iota(jnp.int32, outs[4].shape, 1)
+    first_gain = by_rows(0, 0) + by_rows(0, 1) + by_rows(0, 2)
+    values = jnp.where(lane == 1, first_gain, outs[4][...])
+    outs[4][...] = jnp.where(lane == 2, by_rows(1, 0), values)
     rows_back()
     memory_copy(2).wait()
     memory_copy(3).wait()
@@ -894,7 +903,9 @@
                     along_line(which, i, second)[1].wait_send()
 
 
-def scatter_products(self_arrays, cross_arrays, small, weights, cross_weights, tokens, resid, gain):
+def scatter_products(
+    self_arrays, cross_arrays, small, weights, cross_weights, tokens, resid, gain, self_proj, cross_proj
+):
     counts = (len(self_arrays), len(cross_arrays))
     arrays = (*self_arrays, *cross_arrays)
     shard = small.shape[1]
@@ -907,7 +918,7 @@
     return pl.pallas_call(
         functools.partial(scatter_body, counts),
         in_specs=[pl.BlockSpec(memory_space=pl.ANY)] * (len(arrays) + 5)
-        + [pl.BlockSpec(memory_space=pltpu.VMEM)],
+        + [pl.BlockSpec(memory_space=pltpu.VMEM)] * 3,
         out_specs=[pl.BlockSpec(memory_space=pltpu.VMEM)] * 6 + [pl.BlockSpec(memory_space=pl.ANY)],
         out_shape=[
             jax.ShapeDtypeStruct(shape, f32)
@@ -947,7 +958,7 @@
             collective_id=1, has_side_effects=True, vmem_limit_bytes=60 << 20
         ),
         name="scatter_products",
-    )(*arrays, small, weights, cross_weights, tokens, resid, gain)
+    )(*arrays, small, weights, cross_weights, tokens, resid, gain, self_proj, cross_proj)
 
 
 def gelu_and_slope(value):
@@ -1230,6 +1241,8 @@
             decoder_in[0],
             grad_resid,
             gains[:1],
+            self_proj,
+            cross_proj,
         )
     else:
         normed_all = jnp.concatenate((normed_before, normed_one), axis=0)
@@ -1278,14 +1291,12 @@
     def products(weight, grad):
         return jnp.sum(weight.astype(bf16).astype(f32) * grad, axis=-1)
 
-    gain_grads = jnp.stack(
-        (
-            jnp.sum(products(self_proj, own_self), axis=0),
-            products(cross_proj[0], own_cross[0]),
-            products(ffn_in, own_ffn_in),
-        ),
-        axis=0,
-    )
+    if own_kernels:
+        gain_one, gain_two = own_small[:, 1], own_small[:, 2]
+    else:
+        gain_one = jnp.sum(products(self_proj, own_self), axis=0)
+        gain_two = products(cross_proj[0], own_cross[0])
+    gain_grads = jnp.stack((gain_one, gain_two, products(ffn_in, own_ffn_in)), axis=0)
     gain_grads = gain_grads / norm_gains.astype(bf16).astype(f32)
 
     return (

time: 348 us -> 346 us (level)
    unnamed x74 -> x72, local copies, waits for them, and re-layouts: 8.58 us -> 8.57 us
  transfers between devices with their start and end apart: 6 -> 6, of which waited for: 3 -> 3; matrix products, arithmetic and copies ran while one was open for 15% -> 14% of each run, Pallas kernels for 50% -> 50%
where the time goes in v8:
time: 346 us; the launch traced here: 340 us
  Pallas kernels  249 us (72%)
  matrix products  34.7 us (10%)
  local copies, waits for them, and re-layouts  17.7 us (5%)
  between operations  14.7 us (4%)
  other arithmetic  9.46 us (3%)
  starting transfers between devices  7.82 us (2%)
  waiting for transfers between devices  6.41 us (2%)
    pallas_call x1, Pallas kernels, scatter_products(): pl.pallas_call(functools.partial(scatter_body, counts), in_specs=[pl.Bloc...  79.9 us
    pallas_call x1, Pallas kernels, gather_blocks(): pl.pallas_call(gather_body, in_specs=[pl.BlockSpec(memory_space=pltpu.VME...  49.5 us
    pallas_call x2, Pallas kernels, attend_back(): pl.pallas_call(functools.partial(attend_back_body, rows, keys, causal, st...  46.7 us
    pallas_call x2, Pallas kernels, attend(): pl.pallas_call(functools.partial(attend_body, rows, keys, causal, step, l...  44.7 us
    dot_general x12, matrix products, mm(): return lax.dot_general(a, b, dims, preferred_element_type=f32)  33.4 us
    pallas_call x1, Pallas kernels, feed_forward(): pl.pallas_call(functools.partial(feed_forward_body, rows), grid=(units, 2...  28.7 us
    unnamed x72, local copies, waits for them, and re-layouts  8.57 us
  transfers between devices with their start and end apart: 6, of which 3 were waited for; matrix products, arithmetic and copies ran while one was open for 14% of the time, Pallas kernels for 50%

profile of v8, /device:TPU:0, one launch (start us, length us, event | category | flops | bytes accessed | tf_op | source)
XLA Modules:
  0.0 340.2 jit_solution(4351272261330905796)
XLA Ops:
  7.2 49.5 %gather_blocks.1 = (bf16[32,24,3200]{2,1,0:T(8,128)(2,1)}, bf16[32,24,3072]{2,1,0:T(8,128)(2,1)}, bf16[2,24,6144]{2,1,0:T(8,128)(2,1)}) custom-call(f32[3,24,768]{2,1,0:T(8,128)} %refs_21_.1, f32[24,768]{1,0:T(8,128)} %refs_1_.5, f32[3,24,768]{2,1,0:T(8,128)} %refs_22_.1, f32[24,768]{1,0:T(8,128)} %refs_3_.1, f32[24,3072]{1,0:T(8,128)} %refs_4_.1, ...), custom_call_target="tpu_custom_call" | custom-call | tf_op jit(solution)/shard_map/gather_blocks/pallas_call | solution.py:529
  56.9 3.7 %collective-permute-start = (bf16[512,768]{1,0:T(8,128)(2,1)S(1)}, bf16[512,768]{1,0:T(8,128)(2,1)S(1)}, u32[]{:S(2)}, u32[]{:S(2)}) collective-permute-start(bf16[512,768]{1,0:T(8,128)(2,1)S(1)} %bitcast.60), channel_id=1, source_target_pairs={{0,1},{2,3},{4,5},{6,7},{8,9},{10,11},{12,13},{14,15},{16,17},{18,... | collective-permute-start | bytes 2359304 | tf_op jit(solution)/shard_map/ppermute | solution.py:1111
  61.7 1.2 slice_reduce_fusion
  62.9 2.1 fusion
  67.1 6.0 %convolution_convert_fusion.1.refs_3_.refs_5_ = bf16[1024,1536]{1,0:T(8,128)(2,1)} fusion(bf16[768,3072]{1,0:T(8,128)(2,1)} %bitcast.47, bf16[1,1024,768]{2,1,0:T(8,128)(2,1)S(1)} %copy-done.14), kind=kOutput, calls=%fused_computation.1 | convolution fusion | flops 2417491968 | bytes 7077888 | tf_op jit(solution)/shard_map/dot_general | solution.py:33
  73.1 5.0 %collective-permute-done = bf16[512,768]{1,0:T(8,128)(2,1)S(1)} collective-permute-done((bf16[512,768]{1,0:T(8,128)(2,1)S(1)}, bf16[512,768]{1,0:T(8,128)(2,1)S(1)}, u32[]{:S(2)}, u32[]{:S(2)}) %collective-permute-start) | collective-permute-done | bytes 786464 | tf_op jit(solution)/shard_map/ppermute | solution.py:1111
  78.9 2.6 convolution_convert_fusion.2.refs_4_.refs_6_
  81.5 1.7 multiply_convert_fusion.2.refs_2_
  83.2 2.6 convolution_convert_fusion.3.refs_3_.refs_5_
  85.7 21.1 %attend_causal.1 = (bf16[512,768]{1,0:T(8,128)(2,1)}, bf16[12,512,1024]{2,1,0:T(8,128)(2,1)}, f32[512,768]{1,0:T(8,128)}) custom-call(s32[1,2]{1,0:T(1,128)} %refs_0_.9, s32[1,2]{1,0:T(1,128)} %refs_1_.9, bf16[512,768]{1,0:T(8,128)(2,1)} %multiply_convert_fusion.2.refs_2_, bf16[512,1536]{1,0:T(8,128)(2,1)} %convolution_convert_fusion.3.refs_3_.refs_5_, ...), custom_call_target="tpu_custom_call" | custom-call | tf_op jit(solution)/shard_map/attend_causal/pallas_call | solution.py:204
  106.8 2.4 multiply_reduce_fusion.1
  109.5 1.7 multiply_convert_fusion.refs_2_
  111.4 5.5 %convolution_convert_fusion.refs_4_.refs_6_ = bf16[1024,1536]{1,0:T(8,128)(2,1)} fusion(bf16[1024,768]{1,0:T(8,128)(2,1)} %collective-permute-done.1.refs_10_, bf16[768,3072]{1,0:T(8,128)(2,1)S(1)} %bitcast.54), kind=kOutput, calls=%fused_computation | convolution fusion | flops 2417491968 | bytes 7077888 | tf_op jit(solution)/shard_map/dot_general | solution.py:33
  116.9 23.6 %attend_cross.1 = (bf16[512,768]{1,0:T(8,128)(2,1)}, bf16[12,512,2048]{2,1,0:T(8,128)(2,1)}, f32[512,768]{1,0:T(8,128)}) custom-call(s32[1,2]{1,0:T(1,128)} %refs_0_.9, s32[1,2]{1,0:T(1,128)} %refs_1_.9, bf16[512,768]{1,0:T(8,128)(2,1)} %multiply_convert_fusion.refs_2_, bf16[1024,1536]{1,0:T(8,128)(2,1)} %convolution_convert_fusion.1.refs_3_.refs_5_, ...), custom_call_target="tpu_custom_call" | custom-call | tf_op jit(solution)/shard_map/attend_cross/pallas_call | solution.py:204
  140.6 1.1 copy-done
  141.7 28.7 %feed_forward.1 = (bf16[512,768]{1,0:T(8,128)(2,1)}, f32[512,768]{1,0:T(8,128)S(1)}, bf16[512,768]{1,0:T(8,128)(2,1)S(1)}, bf16[512,768]{1,0:T(8,128)(2,1)S(1)}, bf16[768,6144]{1,0:T(8,128)(2,1)}) custom-call(f32[512,768]{1,0:T(8,128)} %copy-done.4, bf16[512,768]{1,0:T(8,128)(2,1)S(1)} %copy-done, bf16[768,3072]{1,0:T(8,128)(2,1)} %bitcast.48, ...), custom_call_target="tpu_custom_call" | custom-call | tf_op jit(solution)/shard_map/feed_forward/pallas_call | solution.py:1023
  172.3 27.4 %attend_cross_back.1 = (bf16[512,768]{1,0:T(8,128)(2,1)}, bf16[768,2048]{1,0:T(8,128)(2,1)}, bf16[768,2048]{1,0:T(8,128)(2,1)}) custom-call(s32[1,2]{1,0:T(1,128)} %refs_0_.9, s32[1,2]{1,0:T(1,128)} %refs_1_.9, bf16[512,768]{1,0:T(8,128)(2,1)} %multiply_convert_fusion.refs_2_, bf16[1024,1536]{1,0:T(8,128)(2,1)} %convolution_convert_fusion.1.refs_3_.refs_5_, ...), custom_call_target="tpu_custom_call" | custom-call | tf_op jit(solution)/shard_map/attend_cross_back/pallas_call | solution.py:316
  199.6 2.6 multiply_reduce_fusion
  202.2 1.6 fusion.28
  203.8 3.3 convolution_convert_fusion.4.refs_10_
  207.2 1.5 fusion.13
  209.0 1.5 add_convert_fusion
  210.5 2.8 collective-permute-start.2
  213.3 19.3 %attend_causal_back.1 = (bf16[512,768]{1,0:T(8,128)(2,1)}, bf16[768,1024]{1,0:T(8,128)(2,1)}, bf16[768,1024]{1,0:T(8,128)(2,1)}, f32[6,4,256]{2,1,0:T(4,128)}, f32[6,4,128]{2,1,0:T(4,128)}) custom-call(s32[1,2]{1,0:T(1,128)} %refs_0_.9, s32[1,2]{1,0:T(1,128)} %refs_1_.9, bf16[512,768]{1,0:T(8,128)(2,1)} %multiply_convert_fusion.2.refs_2_, ...), custom_call_target="tpu_custom_call" | custom-call | tf_op jit(solution)/shard_map/attend_causal_back/pallas_call | solution.py:316
  235.9 79.9 %scatter_products.1 = (f32[3,24,768]{2,1,0:T(8,128)}, f32[24,768]{1,0:T(8,128)}, f32[3,24,768]{2,1,0:T(8,128)}, f32[24,768]{1,0:T(8,128)}, f32[24,128]{1,0:T(8,1...) custom-call(bf16[512,768]{1,0:T(8,128)(2,1)} %copy-done.10, bf16[512,768]{1,0:T(8,128)(2,1)} %copy-done.11, ...), custom_call_target="tpu_custom_call" | custom-call | tf_op jit(solution)/shard_map/scatter_products/pallas_call | solution.py:918
  315.8 1.0 constant_dynamic-slice_fusion
  316.8 1.2 collective-permute-start.3
  318.0 3.9 %add_bitcast_fusion = f32[1,1024,768]{2,1,0:T(8,128)} fusion(f32[1024,768]{1,0:T(8,128)} %get-tuple-element.71, bf16[1024,768]{1,0:T(8,128)(2,1)S(1)} %collective-permute-done.2), kind=kLoop, calls=%fused_computation.2 | loop fusion | flops 1572864 | bytes 7864320 | tf_op jit(solution)/shard_map/broadcast_in_dim | solution.py:1305
  322.6 1.0 collective-permute-done.3
  325.7 1.2 multiply_reduce_fusion.2
  327.0 1.8 reshape.116
  329.3 1.1 copy.62
  (109 shorter events, 16.1 us)
Async XLA Ops:
  7.2 49.7 %copy-start.6 = (bf16[1,512,768]{2,1,0:T(8,128)(2,1)S(1)}, bf16[1,512,768]{2,1,0:T(8,128)(2,1)}, u32[]{:S(2)}) copy-start(bf16[1,512,768]{2,1,0:T(8,128)(2,1)} %param.18) | copy-start | bytes 2359300
  7.2 133.4 %all-gather.2.cloned.1.call-start = ((), (), s32[]{:S(2)}) async-start(), calls=%async_computation.1 | async-start | bytes 10027008 | tf_op jit(solution)/shard_map/all_gather | solution.py:1154
  7.2 55.6 %copy-start.25 = (bf16[6,768]{1,0:T(8,128)(2,1)S(1)}, bf16[6,768]{1,0:T(8,128)(2,1)}, u32[]{:S(2)}) copy-start(bf16[6,768]{1,0:T(8,128)(2,1)} %constant.50.clone) | copy-start | bytes 27652
  56.8 259.0 %reduce-scatter.2.cloned.1.call-start = ((), (), s32[]{:S(2)}) async-start(), calls=%async_computation.2 | async-start | bytes 10027008 | tf_op jit(solution)/shard_map/reduce_scatter | solution.py:1280
  56.9 21.3 %collective-permute-start = (bf16[512,768]{1,0:T(8,128)(2,1)S(1)}, bf16[512,768]{1,0:T(8,128)(2,1)S(1)}, u32[]{:S(2)}, u32[]{:S(2)}) collective-permute-start(bf16[512,768]{1,0:T(8,128)(2,1)S(1)} %bitcast.60), channel_id=1, source_target_pairs={{0,1},{2,3},{4,5},{6,7},{8,9},{10,11},{12,13},{14,15},{16,17},{18,... | collective-permute-start | bytes 2359304 | tf_op jit(solution)/shard_map/ppermute | solution.py:1111
  60.5 50.9 %collective-permute-start.1 = (bf16[1024,768]{1,0:T(8,128)(2,1)}, bf16[1024,768]{1,0:T(8,128)(2,1)}, u32[]{:S(2)}, u32[]{:S(2)}) collective-permute-start(bf16[1024,768]{1,0:T(8,128)(2,1)} %bitcast.73), channel_id=1, source_target_pairs={{0,1},{1,0},{2,3},{3,2},{4,5},{5,4},{6,7},{7,6},{8,9},{9,8},{10,11... | collective-permute-start | bytes 4718600 | tf_op jit(solution)/shard_map/ppermute | solution.py:1111
  62.9 4.2 %copy-start.14 = (bf16[1,1024,768]{2,1,0:T(8,128)(2,1)S(1)}, bf16[1,1024,768]{2,1,0:T(8,128)(2,1)}, u32[]{:S(2)}) copy-start(bf16[1,1024,768]{2,1,0:T(8,128)(2,1)} %param.19) | copy-start | bytes 4718596
  66.2 12.6 %slice-start.4 = ((s8[4915200]{0:T(1024)(128)(4,1)}), s8[4194304]{0:T(1024)(128)(4,1)S(1)}, s32[]{:S(2)}) async-start(s8[4915200]{0:T(1024)(128)(4,1)} %bitcast.67), calls=%async_computation.7 | async-start | bytes 8388608
  67.1 11.8 %slice-start.5 = ((s8[4915200]{0:T(1024)(128)(4,1)}), s8[720896]{0:T(1024)(128)(4,1)S(1)}, s32[]{:S(2)}) async-start(s8[4915200]{0:T(1024)(128)(4,1)} %bitcast.67), calls=%async_computation.8 | async-start | bytes 1441792
  78.8 2.6 copy-start.11
  78.9 4.3 %copy-start.10 = (bf16[512,768]{1,0:T(8,128)(2,1)}, bf16[512,768]{1,0:T(8,128)(2,1)S(1)}, u32[]{:S(2)}) copy-start(bf16[512,768]{1,0:T(8,128)(2,1)S(1)} %get-tuple-element.129.refs_0_) | copy-start | bytes 2359300
  83.2 26.2 %slice-start = ((s8[4718592]{0:T(1024)(128)(4,1)}), s8[4194304]{0:T(1024)(128)(4,1)S(1)}, s32[]{:S(2)}) async-start(s8[4718592]{0:T(1024)(128)(4,1)} %bitcast.51), calls=%async_computation.3 | async-start | bytes 8388608
  85.7 23.7 %slice-start.1 = ((s8[4718592]{0:T(1024)(128)(4,1)}), s8[524288]{0:T(1024)(128)(4,1)S(1)}, s32[]{:S(2)}) async-start(s8[4718592]{0:T(1024)(128)(4,1)} %bitcast.51), calls=%async_computation.4 | async-start | bytes 1048576
  109.2 1.9 copy-start.4
  116.9 23.7 %copy-start.1 = (bf16[1,512,768]{2,1,0:T(8,128)(2,1)S(1)}, bf16[1,512,768]{2,1,0:T(8,128)(2,1)}, u32[]{:S(2)}) copy-start(bf16[1,512,768]{2,1,0:T(8,128)(2,1)} %param.31) | copy-start | bytes 2359300
  172.2 27.4 %copy-start.5 = (f32[512,768]{1,0:T(8,128)S(1)}, f32[512,768]{1,0:T(8,128)}, u32[]{:S(2)}) copy-start(f32[512,768]{1,0:T(8,128)} %copy-done.4) | copy-start | bytes 4718596
  199.6 7.5 %slice-start.2 = ((s8[4718592]{0:T(1024)(128)(4,1)}), s8[4194304]{0:T(1024)(128)(4,1)S(1)}, s32[]{:S(2)}) async-start(s8[4718592]{0:T(1024)(128)(4,1)} %bitcast.55), calls=%async_computation.5 | async-start | bytes 8388608
  202.2 4.9 %slice-start.3 = ((s8[4718592]{0:T(1024)(128)(4,1)}), s8[524288]{0:T(1024)(128)(4,1)S(1)}, s32[]{:S(2)}) async-start(s8[4718592]{0:T(1024)(128)(4,1)} %bitcast.55), calls=%async_computation.6 | async-start | bytes 1048576
  203.8 3.3 copy-start.9
  203.8 3.4 copy-start.7
  207.2 1.9 copy-start.8
  210.5 105.2 %collective-permute-start.2 = (bf16[1024,768]{1,0:T(8,128)(2,1)S(1)}, bf16[1024,768]{1,0:T(8,128)(2,1)S(1)}, u32[]{:S(2)}, u32[]{:S(2)}) collective-permute-start(bf16[1024,768]{1,0:T(8,128)(2,1)S(1)} %add_convert_fusion), channel_id=1, source_target_pairs={{0,1},{1,0},{2,3},{3,2},{4,5},{5,4},{6,7},{7,6},{8,9},{9,8},{10,11... | collective-permute-start | bytes 4718600 | tf_op jit(solution)/shard_map/ppermute | solution.py:1121
  213.3 20.1 %copy-start.17 = (f32[1024,128]{1,0:T(8,128)S(1)}, f32[1024,128]{1,0:T(8,128)}, u32[]{:S(2)}) copy-start(f32[1024,128]{1,0:T(8,128)} %constant.66) | copy-start | bytes 1572868
  213.3 20.4 %copy-start.18 = (f32[512,128]{1,0:T(8,128)S(1)}, f32[512,128]{1,0:T(8,128)}, u32[]{:S(2)}) copy-start(f32[512,128]{1,0:T(8,128)} %constant.67) | copy-start | bytes 786436
  316.8 6.8 %collective-permute-start.3 = (bf16[24,6144]{1,0:T(8,128)(2,1)S(1)}, bf16[24,6144]{1,0:T(8,128)(2,1)S(1)}, u32[]{:S(2)}, u32[]{:S(2)}) collective-permute-start(bf16[24,6144]{1,0:T(8,128)(2,1)S(1)} %constant_dynamic-slice_fusion), channel_id=1, source_target_pairs={{0,1},{1,0},{2,3},{3,2},{4,5},{5,4},{6,7},{7,6},{8,9},{9,8},{10,11... | collective-permute-start | bytes 884744 | tf_op jit(solution)/shard_map/ppermute | solution.py:1284
  318.0 3.9 %copy-start.21 = (f32[24,128]{1,0:T(8,128)S(1)}, f32[24,128]{1,0:T(8,128)}, u32[]{:S(2)}) copy-start(f32[24,128]{1,0:T(8,128)} %get-tuple-element.82) | copy-start | bytes 36868
  318.0 5.6 %copy-start.16 = (bf16[48,6144]{1,0:T(8,128)(2,1)S(1)}, bf16[48,6144]{1,0:T(8,128)(2,1)}, u32[]{:S(2)}) copy-start(bf16[48,6144]{1,0:T(8,128)(2,1)} %reduce-scatter.2.cloned.1.call-done) | copy-start | bytes 1769476
  325.3 3.5 %copy-start.24 = (f32[3,24]{1,0:T(4,128)S(1)}, f32[3,24]{1,0:T(4,128)}, u32[]{:S(2)}) copy-start(f32[3,24]{1,0:T(4,128)} %refs_6_.1) | copy-start | bytes 868
  325.3 4.0 %copy-start.13 = (f32[512,768]{1,0:T(8,128)S(1)}, f32[512,768]{1,0:T(8,128)}, u32[]{:S(2)}) copy-start(f32[512,768]{1,0:T(8,128)} %get-tuple-element.70) | copy-start | bytes 4718596
  325.7 4.8 %copy-start.15 = (f32[24,3072]{1,0:T(8,128)}, f32[24,3072]{1,0:T(8,128)S(1)}, u32[]{:S(2)}) copy-start(f32[24,3072]{1,0:T(8,128)S(1)} %copy.50) | copy-start | bytes 884740
  329.3 2.5 copy-start.19
  329.3 3.2 copy-start.22
  (6 other events, 7.7 us)
Sparse Core Ops, SparseCore 0:
  56.9 81.6 all-gather.1
  172.4 132.5 reduce-scatter.1
